TPU v7x, 32 devices: a whole 2x2x4 slice. The times are simulated.
32 devices in a mesh: groups: 2 (over x), expert: 16 (over z, y, core).
Axes of the slice: x: 2, y: 2, z: 4, core: 2. Of those that a mesh axis runs over, the one named last changes fastest.
Arguments:
- tokens: bfloat16 [96, 256, 1280], P(('groups', 'expert')), parts along dimension 0, may hold values from -40 to 40
- router: bfloat16 [1280, 4], P(None, 'groups'), parts along dimension 1, may hold values from -1 to 1
- w_in: bfloat16 [32, 1280, 640], P(('groups', 'expert')), parts along dimension 0, may hold values from -0.15625 to 0.15625
- w_out: bfloat16 [32, 640, 1280], P(('groups', 'expert')), parts along dimension 0, may hold values from -0.078125 to 0.078125
- d_out: bfloat16 [96, 256, 1280], P(('groups', 'expert')), parts along dimension 0, may hold values from -6 to 6
Outputs:
- grad_tokens: bfloat16 [96, 256, 1280], P(('groups', 'expert')), parts along dimension 0
- grad_w_in: bfloat16 [32, 1280, 640], P(('groups', 'expert')), parts along dimension 0
- grad_w_out: bfloat16 [32, 640, 1280], P(('groups', 'expert')), parts along dimension 0
- grad_router: float32 [1280, 4], P(None, 'groups'), parts along dimension 1
There are 2 independent parts, one for each index of `groups`. A program takes and returns all parts, laid end to end along the dimension named above; each array names one. Nothing has to cross between parts.
All inputs are finite; a program needn't handle non-finite values.
Results may differ from a plain program's by a relative error of at most 0.0083.
Values may be sent and summed in bfloat16 or wider, within the bound.
No kernel may reach another device: no remote copies, remote signals or barrier semaphores. Data moves between devices by JAX's collectives and lax.ppermute only.
A program may use at most 64 MiB of HBM per device.

v0:
```python
import jax
import jax.numpy as jnp
from jax import lax
from jax.sharding import PartitionSpec as P


def gelu_grad(pre, grad):
    return jax.vjp(lambda value: jax.nn.gelu(value, approximate=True), pre)[1](grad)[0]


def per_device(tokens, router, w_in, w_out, d_out):
    f32 = jnp.float32
    bf16 = jnp.bfloat16
    devices = lax.axis_size("expert")
    slots = router.shape[1]
    split_count = devices // slots
    images = tokens.shape[0]
    width = tokens.shape[2]
    logits = jnp.einsum("bmd,ds->bsm", tokens, router, preferred_element_type=f32)
    dispatch = jax.nn.softmax(logits, axis=2)
    combine = jax.nn.softmax(logits, axis=1)
    disp_b = dispatch.astype(bf16)
    comb_b = combine.astype(bf16)
    slot_in = jnp.einsum("bsm,bmd->bsd", disp_b, tokens, preferred_element_type=f32).astype(bf16)
    grad_slot_out = jnp.einsum("bsm,bmd->bsd", comb_b, d_out, preferred_element_type=f32).astype(
        bf16
    )
    all_in, all_grad = (
        lax.all_gather(slot_in, "expert", axis=0, tiled=True),
        lax.all_gather(grad_slot_out, "expert", axis=0, tiled=True),
    )
    own_expert = lax.axis_index("expert") // split_count
    rows_in = lax.dynamic_index_in_dim(all_in, own_expert, 1, keepdims=False)
    rows_grad = lax.dynamic_index_in_dim(all_grad, own_expert, 1, keepdims=False)
    w_one = w_in[0]
    w_two = w_out[0]
    hidden_pre = jnp.dot(rows_in, w_one, preferred_element_type=f32)
    hidden = jax.nn.gelu(hidden_pre, approximate=True).astype(bf16)
    out_part = jnp.dot(hidden, w_two, preferred_element_type=f32)

    def to_owners(part_rows):
        return part_rows.reshape(devices, images, width)

    def from_owners(received):
        summed = jnp.sum(received.reshape(slots, split_count, images, width), axis=1)
        return jnp.swapaxes(summed, 0, 1).astype(bf16)

    grad_hidden = jnp.einsum("bd,fd->bf", rows_grad, w_two, preferred_element_type=f32)
    grad_pre = gelu_grad(hidden_pre, grad_hidden).astype(bf16)
    grad_two = jnp.einsum("bf,bd->fd", hidden, rows_grad, preferred_element_type=f32).astype(bf16)
    grad_one = jnp.einsum("bd,bf->df", rows_in, grad_pre, preferred_element_type=f32).astype(bf16)
    slot_part = jnp.einsum("bf,df->bd", grad_pre, w_one, preferred_element_type=f32)
    grad_w_in, grad_w_out, slot_part = (grad_one[None], grad_two[None], slot_part)
    recv_out, recv_slot = (
        lax.all_to_all(to_owners(out_part), "expert", split_axis=0, concat_axis=0, tiled=True),
        lax.all_to_all(to_owners(slot_part), "expert", split_axis=0, concat_axis=0, tiled=True),
    )
    slot_out = from_owners(recv_out)
    grad_slot_in = from_owners(recv_slot)
    grad_combine = jnp.einsum("bmd,bsd->bsm", d_out, slot_out, preferred_element_type=f32)
    grad_dispatch = jnp.einsum("bsd,bmd->bsm", grad_slot_in, tokens, preferred_element_type=f32)
    grad_logits = dispatch * (
        grad_dispatch - jnp.sum(dispatch * grad_dispatch, axis=2, keepdims=True)
    )
    grad_logits = grad_logits + combine * (
        grad_combine - jnp.sum(combine * grad_combine, axis=1, keepdims=True)
    )
    gl_b = grad_logits.astype(bf16)
    grad_tokens = jnp.einsum("bsm,bsd->bmd", disp_b, grad_slot_in, preferred_element_type=f32)
    grad_tokens = grad_tokens + jnp.einsum("bsm,ds->bmd", gl_b, router, preferred_element_type=f32)
    router_terms = jnp.einsum("bmd,bsm->ds", tokens, gl_b, preferred_element_type=f32)
    grad_router = lax.psum(router_terms, "expert")
    return (grad_tokens.astype(bf16), grad_w_in, grad_w_out, grad_router)


def solution(mesh):
    in_specs = (
        P(("groups", "expert"), None, None),
        P(None, "groups"),
        P(("groups", "expert"), None, None),
        P(("groups", "expert"), None, None),
        P(("groups", "expert"), None, None),
    )
    out_specs = (
        P(("groups", "expert"), None, None),
        P(("groups", "expert"), None, None),
        P(("groups", "expert"), None, None),
        P(None, "groups"),
    )
    return jax.shard_map(
        per_device, mesh=mesh, in_specs=in_specs, out_specs=out_specs, check_vma=False
    )
```

profile of v0, /device:TPU:0, one launch (start us, length us, event | category | flops | bytes accessed | tf_op | source)
XLA Modules:
  0.0 149.3 jit_solution(17893321355164806572)
XLA Ops:
  0.7 1.5 %copy-done = bf16[3,256,1280]{2,1,0:T(8,128)(2,1)S(1)} copy-done((bf16[3,256,1280]{2,1,0:T(8,128)(2,1)S(1)}, bf16[3,256,1280]{2,1,0:T(8,128)(2,1)}, u32[]{:S(2)}) %copy-start) | copy-done | bytes 1966104
  2.2 1.3 convolution_bitcast_fusion.1
  3.8 0.4 convolution_convert_fusion.2
  4.2 23.8 %all_gather.7 = bf16[48,2,1280]{2,1,0:T(2,128)(2,1)S(1)} all-gather(bf16[3,2,1280]{2,1,0:T(2,128)(2,1)S(1)} %convolution_convert_fusion.2), channel_id=1, replica_groups=mesh['groups'=2,'expert'=16] {'expert'}, dimensions={0}, use_global_device_ids=true | all-gather | bytes 261120 | tf_op jit(solution)/shard_map/all_gather | solution.py:29
  27.9 1.9 %convolution_convert_fusion.3 = bf16[3,2,1280]{2,1,0:T(2,128)(2,1)S(1)} fusion(bf16[3,256,1280]{2,1,0:T(8,128)(2,1)} %param.9, f32[3,2,256]{2,1,0:T(2,128)S(1)} %get-tuple-element.7, f32[3,256]{1,0:T(4,128)S(1)} %get-tuple-element.6), kind=kOutput, calls=%fused_computation.11 | convolution fusion | flops 3942912 | bytes 1990656 | tf_op jit(solution)/shard_map/bsm,bmd->bsd/dot_general | solution.py:25
  29.9 18.1 %all_gather.6 = bf16[48,2,1280]{2,1,0:T(2,128)(2,1)S(1)} all-gather(bf16[3,2,1280]{2,1,0:T(2,128)(2,1)S(1)} %convolution_convert_fusion.3), channel_id=1, replica_groups=mesh['groups'=2,'expert'=16] {'expert'}, dimensions={0}, use_global_device_ids=true | all-gather | bytes 261120 | tf_op jit(solution)/shard_map/all_gather | solution.py:30
  48.5 1.8 %multiply_convert_fusion = (bf16[48,640]{1,0:T(8,128)(2,1)S(1)}, f32[48,640]{1,0:T(8,128)S(1)}) fusion(bf16[1,1280,640]{2,1,0:T(8,128)(2,1)} %param.7, bf16[48,1,1280]{2,1,0:T(2,128)(2,1)S(1)} %constant_dynamic-slice_fusion), kind=kOutput, calls=%fused_computation.45 | convolution fusion | flops 78919680 | bytes 1945600 | tf_op jit(solution)/shard_map/dot_general | solution.py:37
  50.3 0.6 fusion.31
  51.0 2.0 %fusion.9 = f32[16,3,1280]{2,0,1:T(8,128)S(1)} fusion(bf16[1,1280,640]{2,1,0:T(8,128)(2,1)} %param.7, bf16[16,3,640]{2,1,0:T(4,128)(2,1)S(1)} %dot_general.53), kind=kOutput, calls=%fused_computation.15 | convolution fusion | flops 78643200 | bytes 1945600 | tf_op jit(solution)/shard_map/bf,df->bd/dot_general | solution.py:52
  53.0 0.9 copy.22
  53.9 3.5 %all-to-all-start = ((f32[16,3,1280]{2,1,0:T(4,128)}), f32[16,3,1280]{2,1,0:T(4,128)S(1)}, u32[]{:S(2)}, u32[]{:S(2)}) async-start(f32[16,3,1280]{2,1,0:T(4,128)} %copy.22), calls=%async_computation | async-start | bytes 655360 | tf_op jit(solution)/shard_map/all_to_all | solution.py:56
  57.5 1.8 %fusion.7 = f32[16,3,1280]{2,0,1:T(8,128)S(1)} fusion(bf16[1,640,1280]{2,1,0:T(8,128)(2,1)} %param.8, bf16[16,3,640]{2,1,0:T(4,128)(2,1)S(1)} %dot_general.57), kind=kOutput, calls=%fused_computation.13 | convolution fusion | flops 78643200 | bytes 1945600 | tf_op jit(solution)/shard_map/dot_general | solution.py:39
  59.3 0.9 copy.26
  60.2 1.8 %fusion.5 = bf16[1,1280,640]{2,1,0:T(8,128)(2,1)} fusion(bf16[48,640]{1,0:T(8,128)(2,1)S(1)} %fusion.31, bf16[48,1,1280]{2,1,0:T(2,128)(2,1)S(1)} %constant_dynamic-slice_fusion), kind=kOutput, calls=%fused_computation.8 | convolution fusion | flops 79462400 | bytes 1822720 | tf_op jit(solution)/shard_map/bd,bf->df/dot_general | solution.py:51
  62.0 1.8 %fusion.6 = bf16[1,640,1280]{2,1,0:T(8,128)(2,1)} fusion(bf16[48,640]{1,0:T(8,128)(2,1)S(1)} %get-tuple-element.8, bf16[48,1,1280]{2,1,0:T(2,128)(2,1)S(1)} %constant_dynamic-slice_fusion.1), kind=kOutput, calls=%fused_computation.9 | convolution fusion | flops 79462400 | bytes 1822720 | tf_op jit(solution)/shard_map/bf,bd->fd/dot_general | solution.py:50
  63.7 4.8 %all-to-all-done = f32[16,3,1280]{2,1,0:T(4,128)S(1)} async-done(((f32[16,3,1280]{2,1,0:T(4,128)}), f32[16,3,1280]{2,1,0:T(4,128)S(1)}, u32[]{:S(2)}, u32[]{:S(2)}) %all-to-all-start) | async-done | bytes 245792 | tf_op jit(solution)/shard_map/all_to_all | solution.py:56
  68.5 3.5 %all-to-all-start.1 = ((f32[16,3,1280]{2,1,0:T(4,128)}), f32[16,3,1280]{2,1,0:T(4,128)S(1)}, u32[]{:S(2)}, u32[]{:S(2)}) async-start(f32[16,3,1280]{2,1,0:T(4,128)} %copy.26), calls=%async_computation.1 | async-start | bytes 655360 | tf_op jit(solution)/shard_map/all_to_all | solution.py:55
  72.1 0.6 fusion.42
  72.7 2.8 %fusion.44 = f32[3,256,1280]{2,1,0:T(8,128)} fusion(bf16[3,2,1280]{2,0,1:T(4,128)(2,1)S(1)} %bitcast.64, f32[3,2]{1,0:T(4,128)S(1)} %get-tuple-element.4, f32[3,2,256]{2,1,0:T(2,128)S(1)} %convolution_bitcast_fusion.1), kind=kOutput, calls=%fused_computation.57 | convolution fusion | flops 3937029 | bytes 3953688 | tf_op jit(solution)/shard_map/bsm,bsd->bmd/dot_general | solution.py:69
  75.5 7.6 %all-to-all-done.1 = f32[16,3,1280]{2,1,0:T(4,128)S(1)} async-done(((f32[16,3,1280]{2,1,0:T(4,128)}), f32[16,3,1280]{2,1,0:T(4,128)S(1)}, u32[]{:S(2)}, u32[]{:S(2)}) %all-to-all-start.1) | async-done | bytes 245792 | tf_op jit(solution)/shard_map/all_to_all | solution.py:55
  83.2 2.2 %fusion.36 = f32[3,2,256]{2,1,0:T(2,128)S(1)} fusion(bf16[3,256,1280]{2,1,0:T(8,128)(2,1)} %param.9, bf16[3,2,1280]{2,0,1:T(4,128)(2,1)S(1)} %bitcast.65), kind=kOutput, calls=%fused_computation.50 | convolution fusion | flops 3932160 | bytes 1987584 | tf_op jit(solution)/shard_map/bmd,bsd->bsm/dot_general | solution.py:60
  85.4 0.5 convolution_bitcast_fusion
  85.9 4.3 %fusion.4 = bf16[3,256,1280]{2,1,0:T(8,128)(2,1)} fusion(f32[3,256,1280]{2,1,0:T(8,128)} %fusion.44, f32[3,2,256]{2,1,0:T(2,128)S(1)} %fusion.23, f32[3,2,256]{2,1,0:T(2,128)S(1)} %fusion.42, bf16[1280,2]{0,1:T(2,128)(2,1)S(1)} %copy-done.2, f32[3,2,256]{2,1,0:T(2,128)S(1)} %get-tuple-element.5, f32[3,2]{1,0:T(4,128)S(1)} %get-tuple-element.4), kind=kOutput, calls=%fused_computation.5 | convolution fusion | flops 5909253 | bytes 5921816 | tf_op jit(solution)/shard_map/bsm,ds->bmd/dot_general | solution.py:70
  90.2 59.1 %psum.7 = f32[1280,2]{0,1:T(2,128)} all-reduce(f32[1280,2]{0,1:T(2,128)S(1)} %convolution_bitcast_fusion), channel_id=1, replica_groups=mesh['groups'=2,'expert'=16] {'expert'}, use_global_device_ids=true, to_apply=%region_8.9 | all-reduce | flops 2560 | bytes 20480 | tf_op jit(solution)/shard_map/psum | solution.py:72
  (14 shorter events, 1.0 us)
Async XLA Ops:
  0.6 1.6 %copy-start = (bf16[3,256,1280]{2,1,0:T(8,128)(2,1)S(1)}, bf16[3,256,1280]{2,1,0:T(8,128)(2,1)}, u32[]{:S(2)}) copy-start(bf16[3,256,1280]{2,1,0:T(8,128)(2,1)} %param.5) | copy-start | bytes 5898244
  48.0 2.4 %copy-start.1 = (bf16[1,640,1280]{2,1,0:T(8,128)(2,1)S(1)}, bf16[1,640,1280]{2,1,0:T(8,128)(2,1)}, u32[]{:S(2)}) copy-start(bf16[1,640,1280]{2,1,0:T(8,128)(2,1)} %param.8) | copy-start | bytes 4915204
  53.9 14.6 %all-to-all-start = ((f32[16,3,1280]{2,1,0:T(4,128)}), f32[16,3,1280]{2,1,0:T(4,128)S(1)}, u32[]{:S(2)}, u32[]{:S(2)}) async-start(f32[16,3,1280]{2,1,0:T(4,128)} %copy.22), calls=%async_computation | async-start | bytes 655360 | tf_op jit(solution)/shard_map/all_to_all | solution.py:56
  68.5 14.6 %all-to-all-start.1 = ((f32[16,3,1280]{2,1,0:T(4,128)}), f32[16,3,1280]{2,1,0:T(4,128)S(1)}, u32[]{:S(2)}, u32[]{:S(2)}) async-start(f32[16,3,1280]{2,1,0:T(4,128)} %copy.26), calls=%async_computation.1 | async-start | bytes 655360 | tf_op jit(solution)/shard_map/all_to_all | solution.py:55
  83.2 2.7 %copy-start.2 = (bf16[1280,2]{0,1:T(2,128)(2,1)S(1)}, bf16[1280,2]{0,1:T(2,128)(2,1)}, u32[]{:S(2)}) copy-start(bf16[1280,2]{0,1:T(2,128)(2,1)} %param.6) | copy-start | bytes 15364
where the time goes:
time: 150 us; the launch traced here: 149 us
  blocking collectives  101 us (67%)
  matrix products  23.8 us (16%)
  waiting for transfers between devices  12.4 us (8%)
  starting transfers between devices  7.09 us (5%)
  local copies, waits for them, and re-layouts  3.95 us (3%)
    psum x1, blocking collectives, per_device(): grad_router = lax.psum(router_terms, 'expert')  59.1 us
    all_gather x1, blocking collectives, per_device(): lax.all_gather(slot_in, 'expert', axis=0, tiled=True)  23.8 us
    all_gather x1, blocking collectives, per_device(): lax.all_gather(grad_slot_out, 'expert', axis=0, tiled=True)  18.1 us
    all_to_all x1, waiting for transfers between devices, per_device(): lax.all_to_all(to_owners(out_part), 'expert', split_axis=0, concat_axis=0...  7.61 us
    all_to_all x1, waiting for transfers between devices, per_device(): lax.all_to_all(to_owners(slot_part), 'expert', split_axis=0, concat_axis=...  4.77 us
    dot_general x1, matrix products, per_device(): jnp.einsum('bsm,ds->bmd', gl_b, router, preferred_element_type=f32)  4.27 us
    all_to_all x1, starting transfers between devices, per_device(): lax.all_to_all(to_owners(slot_part), 'expert', split_axis=0, concat_axis=...  3.54 us
    all_to_all x1, starting transfers between devices, per_device(): lax.all_to_all(to_owners(out_part), 'expert', split_axis=0, concat_axis=0...  3.54 us
  transfers between devices with their start and end apart: 2, of which 2 were waited for; matrix products, arithmetic and copies ran while one was open for 7% of the time, Pallas kernels for 0%

commit v1 on v0

v1 whole, which is shorter than its diff:
```python
import jax
import jax.numpy as jnp
from jax import lax
from jax.sharding import PartitionSpec as P


def gelu_grad(pre, grad):
    return jax.vjp(lambda value: jax.nn.gelu(value, approximate=True), pre)[1](grad)[0]


def exchange(blocks):
    return lax.all_to_all(blocks, "expert", split_axis=0, concat_axis=0, tiled=True)


def per_device(tokens, router, w_in, w_out, d_out):
    f32 = jnp.float32
    bf16 = jnp.bfloat16
    devices = lax.axis_size("expert")
    slots = router.shape[1]
    split_count = devices // slots
    images = tokens.shape[0]
    width = tokens.shape[2]
    logits = jnp.einsum("bmd,ds->bsm", tokens, router, preferred_element_type=f32)
    dispatch = jax.nn.softmax(logits, axis=2)
    combine = jax.nn.softmax(logits, axis=1)
    disp_b = dispatch.astype(bf16)
    comb_b = combine.astype(bf16)
    slot_in = jnp.einsum("bsm,bmd->sbd", disp_b, tokens, preferred_element_type=f32).astype(bf16)
    grad_slot_out = jnp.einsum("bsm,bmd->sbd", comb_b, d_out, preferred_element_type=f32).astype(
        bf16
    )
    rows = jnp.concatenate([slot_in, grad_slot_out], axis=1)
    rows = jnp.broadcast_to(rows[:, None], (slots, split_count, 2 * images, width))
    rows = exchange(rows.reshape(devices, 2 * images, width))
    rows_in = rows[:, :images].reshape(devices * images, width)
    rows_grad = rows[:, images:].reshape(devices * images, width)
    w_one = w_in[0]
    w_two = w_out[0]
    hidden_pre = jnp.dot(rows_in, w_one, preferred_element_type=f32)
    hidden = jax.nn.gelu(hidden_pre, approximate=True).astype(bf16)
    out_part = jnp.dot(hidden, w_two, preferred_element_type=f32)
    grad_hidden = jnp.einsum("bd,fd->bf", rows_grad, w_two, preferred_element_type=f32)
    grad_pre = gelu_grad(hidden_pre, grad_hidden).astype(bf16)
    slot_part = jnp.einsum("bf,df->bd", grad_pre, w_one, preferred_element_type=f32)
    grad_two = jnp.einsum("bf,bd->fd", hidden, rows_grad, preferred_element_type=f32).astype(bf16)
    grad_one = jnp.einsum("bd,bf->df", rows_in, grad_pre, preferred_element_type=f32).astype(bf16)
    grad_w_in, grad_w_out = (grad_one[None], grad_two[None])
    shares = jnp.concatenate(
        [
            out_part.astype(bf16).reshape(devices, images, width),
            slot_part.astype(bf16).reshape(devices, images, width),
        ],
        axis=1,
    )
    shares = exchange(shares).reshape(slots, split_count, 2 * images, width)
    summed = jnp.sum(shares.astype(f32), axis=1).astype(bf16)
    slot_out = summed[:, :images]
    grad_slot_in = summed[:, images:]
    grad_combine = jnp.einsum("bmd,sbd->bsm", d_out, slot_out, preferred_element_type=f32)
    grad_dispatch = jnp.einsum("sbd,bmd->bsm", grad_slot_in, tokens, preferred_element_type=f32)
    grad_logits = dispatch * (
        grad_dispatch - jnp.sum(dispatch * grad_dispatch, axis=2, keepdims=True)
    )
    grad_logits = grad_logits + combine * (
        grad_combine - jnp.sum(combine * grad_combine, axis=1, keepdims=True)
    )
    gl_b = grad_logits.astype(bf16)
    router_terms = jnp.einsum("bmd,bsm->sd", tokens, gl_b, preferred_element_type=f32)
    terms = exchange(jnp.broadcast_to(router_terms[None], (devices, slots, width)))
    grad_router = jnp.sum(terms, axis=0).T
    grad_tokens = jnp.einsum("bsm,sbd->bmd", disp_b, grad_slot_in, preferred_element_type=f32)
    grad_tokens = grad_tokens + jnp.einsum("bsm,ds->bmd", gl_b, router, preferred_element_type=f32)
    return (grad_tokens.astype(bf16), grad_w_in, grad_w_out, grad_router)


def solution(mesh):
    in_specs = (
        P(("groups", "expert"), None, None),
        P(None, "groups"),
        P(("groups", "expert"), None, None),
        P(("groups", "expert"), None, None),
        P(("groups", "expert"), None, None),
    )
    out_specs = (
        P(("groups", "expert"), None, None),
        P(("groups", "expert"), None, None),
        P(("groups", "expert"), None, None),
        P(None, "groups"),
    )
    return jax.shard_map(
        per_device, mesh=mesh, in_specs=in_specs, out_specs=out_specs, check_vma=False
    )
```

time: 150 us -> 63.9 us (0.43)
  blocking collectives: 101 us -> 18.3 us
  matrix products: 23.8 us -> 19.5 us
  other arithmetic: 0.39 us -> 1.96 us
    psum x1 -> x0, blocking collectives: 59.1 us -> none  [per_device(): grad_router = lax.psum(router_terms, 'expert')]
    all_gather x2 -> x0, blocking collectives: 41.8 us -> none  [the longest x1 23.8 us: per_device(): lax.all_gather(slot_in, 'expert', axis=0, tiled=True)]
    all_to_all x0 -> x1, blocking collectives: none -> 18.3 us  [exchange(): lax.all_to_all(blocks, 'expert', split_axis=0, concat_axis=0, tiled=True)]
    dot_general x4 -> x0, local copies, waits for them, and re-layouts: 1.89 us -> none  [the longest x2 0.96 us: per_device(): jnp.einsum('bf,df->bd', grad_pre, w_one, preferred_element_type=f32)]
    dot_general x6, matrix products: 8.42 us -> 6.85 us  [the longest x1 2.75 us: per_device(): jnp.einsum('bsm,sbd->bmd', disp_b, grad_slot_in, preferred_element_type=f32)]
  transfers between devices with their start and end apart: 2 -> 2, of which waited for: 2 -> 2; matrix products, arithmetic and copies ran while one was open for 7% -> 12% of each run, Pallas kernels for 0% -> 0%
where the time goes in v1:
time: 63.9 us; the launch traced here: 63.4 us
  matrix products  19.5 us (31%)
  blocking collectives  18.3 us (29%)
  waiting for transfers between devices  11.6 us (18%)
  starting transfers between devices  7.06 us (11%)
  local copies, waits for them, and re-layouts  4.17 us (7%)
  other arithmetic  1.96 us (3%)
  between operations  0.79 us (1%)
    all_to_all x1, blocking collectives, exchange(): lax.all_to_all(blocks, 'expert', split_axis=0, concat_axis=0, tiled=True)  18.3 us
    all_to_all x2, waiting for transfers between devices, exchange(): lax.all_to_all(blocks, 'expert', split_axis=0, concat_axis=0, tiled=True)  11.6 us
    all_to_all x2, starting transfers between devices, exchange(): lax.all_to_all(blocks, 'expert', split_axis=0, concat_axis=0, tiled=True)  7.06 us
    dot_general x1, matrix products, per_device(): jnp.einsum('bsm,ds->bmd', gl_b, router, preferred_element_type=f32)  4.25 us
    unnamed x10, local copies, waits for them, and re-layouts  2.93 us
    dot_general x1, matrix products, per_device(): jnp.einsum('bsm,sbd->bmd', disp_b, grad_slot_in, preferred_element_type=f32)  2.75 us
    dot_general x1, matrix products, per_device(): hidden_pre = jnp.dot(rows_in, w_one, preferred_element_type=f32)  1.95 us
    dot_general x1, matrix products, per_device(): jnp.einsum('bsm,bmd->sbd', comb_b, d_out, preferred_element_type=f32)  1.94 us
  transfers between devices with their start and end apart: 2, of which 2 were waited for; matrix products, arithmetic and copies ran while one was open for 12% of the time, Pallas kernels for 0%

profile of v1, /device:TPU:0, one launch (start us, length us, event | category | flops | bytes accessed | tf_op | source)
XLA Modules:
  0.0 63.4 jit_solution(11499193533659112877)
XLA Ops:
  0.6 1.5 %copy-done = bf16[3,256,1280]{2,1,0:T(8,128)(2,1)S(1)} copy-done((bf16[3,256,1280]{2,1,0:T(8,128)(2,1)S(1)}, bf16[3,256,1280]{2,1,0:T(8,128)(2,1)}, u32[]{:S(2)}) %copy-start) | copy-done | bytes 1966104
  2.2 1.3 %convolution_bitcast_fusion.1 = f32[3,2,256]{2,1,0:T(2,128)S(1)} fusion(bf16[3,256,1280]{2,1,0:T(8,128)(2,1)S(1)} %copy-done, bf16[1280,2]{0,1:T(2,128)(2,1)} %param.6), kind=kOutput, calls=%fused_computation.32 | convolution fusion | flops 3932160 | bytes 1977344 | tf_op jit(solution)/shard_map/bmd,ds->bsm/dot_general | solution.py:23
  3.7 0.4 fusion.7
  4.2 1.9 %fusion.8 = bf16[2,3,1280]{2,0,1:T(2,128)(2,1)S(1)} fusion(bf16[3,256,1280]{2,1,0:T(8,128)(2,1)} %param.9, f32[3,2,256]{2,1,0:T(2,128)S(1)} %get-tuple-element.9, f32[3,256]{1,0:T(4,128)S(1)} %get-tuple-element.8), kind=kOutput, calls=%fused_computation.15 | convolution fusion | flops 3942912 | bytes 1990656 | tf_op jit(solution)/shard_map/bsm,bmd->sbd/dot_general | solution.py:29
  6.2 18.3 %all_to_all.15 = bf16[16,6,1280]{2,1,0:T(8,128)(2,1)S(1)} all-to-all(bf16[16,6,1280]{2,1,0:T(8,128)(2,1)S(1)} %bitcast.49), channel_id=1, replica_groups=mesh['groups'=2,'expert'=16] {'expert'}, dimensions={0} | all-to-all | bytes 491520 | tf_op jit(solution)/shard_map/all_to_all | solution.py:12
  24.8 2.0 %fusion.13 = f32[48,640]{1,0:T(8,128)S(1)} fusion(bf16[48,1280]{1,0:T(8,128)(2,1)S(1)} %reshape.35, bf16[1,1280,640]{2,1,0:T(8,128)(2,1)} %param.7), kind=kOutput, calls=%fused_computation.21 | convolution fusion | flops 78643200 | bytes 1884160 | tf_op jit(solution)/shard_map/dot_general | solution.py:39
  27.2 0.6 fusion.31
  27.8 0.4 copy-done.3
  28.2 0.6 convolution_convert_fusion.2
  29.0 0.9 %pad_maximum_fusion = bf16[16,6,1280]{2,1,0:T(8,128)(2,1)} fusion(bf16[16,3,1280]{2,1,0:T(4,128)(2,1)S(1)} %reshape.38, bf16[16,3,1280]{2,1,0:T(4,128)(2,1)S(1)} %reshape.36), kind=kLoop, calls=%fused_computation.34 | loop fusion | flops 491520 | bytes 491520 | tf_op jit(solution)/shard_map/concatenate | solution.py:48
  29.9 3.5 %all-to-all-start.1 = ((bf16[16,6,1280]{2,1,0:T(8,128)(2,1)}), bf16[16,6,1280]{2,1,0:T(8,128)(2,1)S(1)}, u32[]{:S(2)}, u32[]{:S(2)}) async-start(bf16[16,6,1280]{2,1,0:T(8,128)(2,1)} %pad_maximum_fusion), calls=%async_computation.1 | async-start | bytes 655360 | tf_op jit(solution)/shard_map/all_to_all | solution.py:12
  33.4 1.8 %fusion.5 = bf16[1,1280,640]{2,1,0:T(8,128)(2,1)} fusion(bf16[48,1280]{1,0:T(8,128)(2,1)S(1)} %reshape.35, bf16[48,640]{1,0:T(8,128)(2,1)S(1)} %fusion.31), kind=kOutput, calls=%fused_computation.8 | convolution fusion | flops 79462400 | bytes 1822720 | tf_op jit(solution)/shard_map/bd,bf->df/dot_general | solution.py:46
  35.2 1.8 %fusion.6 = bf16[1,640,1280]{2,1,0:T(8,128)(2,1)} fusion(bf16[48,1280]{1,0:T(8,128)(2,1)S(1)} %reshape.37, f32[48,640]{1,0:T(8,128)S(1)} %fusion.13), kind=kOutput, calls=%fused_computation.9 | convolution fusion | flops 79738880 | bytes 1884160 | tf_op jit(solution)/shard_map/bf,bd->fd/dot_general | solution.py:45
  37.0 7.5 %all-to-all-done.1 = bf16[16,6,1280]{2,1,0:T(8,128)(2,1)S(1)} async-done(((bf16[16,6,1280]{2,1,0:T(8,128)(2,1)}), bf16[16,6,1280]{2,1,0:T(8,128)(2,1)S(1)}, u32[]{:S(2)}, u32[]{:S(2)}) %all-to-all-start.1) | async-done | bytes 245792 | tf_op jit(solution)/shard_map/all_to_all | solution.py:12
  44.6 2.7 %fusion.42 = f32[3,256,1280]{2,1,0:T(8,128)} fusion(bf16[2,3,1280]{2,1,0:T(4,128)(2,1)S(1)} %get-tuple-element.7, f32[3,2]{1,0:T(4,128)S(1)} %get-tuple-element.10, f32[3,2,256]{2,1,0:T(2,128)S(1)} %convolution_bitcast_fusion.1), kind=kOutput, calls=%fused_computation.54 | convolution fusion | flops 3937029 | bytes 3953688 | tf_op jit(solution)/shard_map/bsm,sbd->bmd/dot_general | solution.py:71
  47.3 0.6 fusion.40
  47.9 0.9 %copy-done.1 = bf16[3,256,1280]{2,1,0:T(8,128)(2,1)S(1)} copy-done((bf16[3,256,1280]{2,1,0:T(8,128)(2,1)S(1)}, bf16[3,256,1280]{2,1,0:T(8,128)(2,1)}, u32[]{:S(2)}) %copy-start.1) | copy-done | bytes 1966104
  48.9 0.6 fusion.34
  49.5 0.5 convolution_bitcast_fusion
  50.0 0.7 %broadcast_in_dim.11 = f32[16,2,1280]{2,1,0:T(2,128)} broadcast(f32[2,1280]{1,0:T(2,128)S(1)} %convolution_bitcast_fusion), dimensions={1,2} | broadcast | bytes 174080 | tf_op jit(solution)/shard_map/broadcast_in_dim | solution.py:69
  50.8 3.5 %all-to-all-start.2 = ((f32[16,2,1280]{2,1,0:T(2,128)}), f32[16,2,1280]{2,1,0:T(2,128)S(1)}, u32[]{:S(2)}, u32[]{:S(2)}) async-start(f32[16,2,1280]{2,1,0:T(2,128)} %broadcast_in_dim.11), calls=%async_computation.2 | async-start | bytes 327680 | tf_op jit(solution)/shard_map/all_to_all | solution.py:12
  54.3 4.3 %fusion.4 = bf16[3,256,1280]{2,1,0:T(8,128)(2,1)} fusion(f32[3,256,1280]{2,1,0:T(8,128)} %fusion.42, f32[3,2,256]{2,1,0:T(2,128)S(1)} %fusion.23, f32[3,2,256]{2,1,0:T(2,128)S(1)} %fusion.40, bf16[1280,2]{0,1:T(2,128)(2,1)S(1)} %copy-done.4, f32[3,2,256]{2,1,0:T(2,128)S(1)} %get-tuple-element.11, f32[3,2]{1,0:T(4,128)S(1)} %get-tuple-element.10), kind=kOutput, calls=%fused_computation.5 | convolution fusion | flops 5909253 | bytes 5921816 | tf_op jit(solution)/shard_map/bsm,ds->bmd/dot_general | solution.py:72
  58.5 4.2 %all-to-all-done.2 = f32[16,2,1280]{2,1,0:T(2,128)S(1)} async-done(((f32[16,2,1280]{2,1,0:T(2,128)}), f32[16,2,1280]{2,1,0:T(2,128)S(1)}, u32[]{:S(2)}, u32[]{:S(2)}) %all-to-all-start.2) | async-done | bytes 163872 | tf_op jit(solution)/shard_map/all_to_all | solution.py:12
  62.7 0.7 %reduce_sum.62 = f32[2,1280]{1,0:T(2,128)} reduce(f32[16,2,1280]{2,1,0:T(2,128)S(1)} %all-to-all-done.2, f32[]{:T(128)} %constant.3.clone.1), dimensions={0}, to_apply=%region_7.0 | reduce | flops 38400 | bytes 174084 | tf_op jit(solution)/shard_map/reduce_sum | solution.py:70
  (21 shorter events, 1.3 us)
Async XLA Ops:
  0.6 1.6 %copy-start = (bf16[3,256,1280]{2,1,0:T(8,128)(2,1)S(1)}, bf16[3,256,1280]{2,1,0:T(8,128)(2,1)}, u32[]{:S(2)}) copy-start(bf16[3,256,1280]{2,1,0:T(8,128)(2,1)} %param.5) | copy-start | bytes 5898244
  24.8 2.0 %copy-start.2 = (bf16[1,640,1280]{2,1,0:T(8,128)(2,1)S(1)}, bf16[1,640,1280]{2,1,0:T(8,128)(2,1)}, u32[]{:S(2)}) copy-start(bf16[1,640,1280]{2,1,0:T(8,128)(2,1)} %param.8) | copy-start | bytes 4915204
  26.8 1.4 %copy-start.3 = (bf16[1,1280,640]{2,1,0:T(8,128)(2,1)S(1)}, bf16[1,1280,640]{2,1,0:T(8,128)(2,1)}, u32[]{:S(2)}) copy-start(bf16[1,1280,640]{2,1,0:T(8,128)(2,1)} %param.7) | copy-start | bytes 4915204
  29.9 14.6 %all-to-all-start.1 = ((bf16[16,6,1280]{2,1,0:T(8,128)(2,1)}), bf16[16,6,1280]{2,1,0:T(8,128)(2,1)S(1)}, u32[]{:S(2)}, u32[]{:S(2)}) async-start(bf16[16,6,1280]{2,1,0:T(8,128)(2,1)} %pad_maximum_fusion), calls=%async_computation.1 | async-start | bytes 655360 | tf_op jit(solution)/shard_map/all_to_all | solution.py:12
  47.3 1.5 %copy-start.1 = (bf16[3,256,1280]{2,1,0:T(8,128)(2,1)S(1)}, bf16[3,256,1280]{2,1,0:T(8,128)(2,1)}, u32[]{:S(2)}) copy-start(bf16[3,256,1280]{2,1,0:T(8,128)(2,1)} %param.9) | copy-start | bytes 5898244
  48.9 5.4 %copy-start.4 = (bf16[1280,2]{0,1:T(2,128)(2,1)S(1)}, bf16[1280,2]{0,1:T(2,128)(2,1)}, u32[]{:S(2)}) copy-start(bf16[1280,2]{0,1:T(2,128)(2,1)} %param.6) | copy-start | bytes 15364
  50.8 11.9 %all-to-all-start.2 = ((f32[16,2,1280]{2,1,0:T(2,128)}), f32[16,2,1280]{2,1,0:T(2,128)S(1)}, u32[]{:S(2)}, u32[]{:S(2)}) async-start(f32[16,2,1280]{2,1,0:T(2,128)} %broadcast_in_dim.11), calls=%async_computation.2 | async-start | bytes 327680 | tf_op jit(solution)/shard_map/all_to_all | solution.py:12

commit v2 on v1

--- a/solution.py
+++ b/solution.py
@@ -8,8 +8,13 @@
     return jax.vjp(lambda value: jax.nn.gelu(value, approximate=True), pre)[1](grad)[0]
 
 
-def exchange(blocks):
-    return lax.all_to_all(blocks, "expert", split_axis=0, concat_axis=0, tiled=True)
+def permute(block, move):
+    count = lax.axis_size("expert")
+    return lax.ppermute(block, "expert", [(source, move(source)) for source in range(count)])
+
+
+def bits_of(count):
+    return [1 << place for place in range(count.bit_length() - 1)]
 
 
 def per_device(tokens, router, w_in, w_out, d_out):
@@ -30,8 +35,15 @@
         bf16
     )
     rows = jnp.concatenate([slot_in, grad_slot_out], axis=1)
-    rows = jnp.broadcast_to(rows[:, None], (slots, split_count, 2 * images, width))
-    rows = exchange(rows.reshape(devices, 2 * images, width))
+    own = lax.axis_index("expert") // split_count
+    held = [lax.dynamic_index_in_dim(rows, own, 0, keepdims=False)]
+    for far in range(1, slots):
+        sent = lax.dynamic_index_in_dim(rows, (own + far) % slots, 0, keepdims=False)
+        held.append(permute(sent, lambda d: (d + far * split_count) % devices))
+    rows = jnp.stack(held)
+    for bit in reversed(bits_of(split_count)):
+        rows = jnp.stack([rows, permute(rows, lambda d: d ^ bit)])
+    rows = rows.reshape(devices, 2 * images, width)
     rows_in = rows[:, :images].reshape(devices * images, width)
     rows_grad = rows[:, images:].reshape(devices * images, width)
     w_one = w_in[0]
@@ -52,8 +64,20 @@
         ],
         axis=1,
     )
-    shares = exchange(shares).reshape(slots, split_count, 2 * images, width)
-    summed = jnp.sum(shares.astype(f32), axis=1).astype(bf16)
+    for bit in bits_of(split_count):
+        shares = shares.reshape((2, -1) + shares.shape[1:])
+        received = permute(shares[1], lambda d: d ^ bit)
+        shares = (shares[0].astype(f32) + received.astype(f32)).astype(bf16)
+    held = [shares[0]]
+    for far in range(1, slots):
+        held.append(permute(shares[slots - far], lambda d: (d + far * split_count) % devices))
+    held = jnp.stack(held)
+    summed = jnp.stack(
+        [
+            lax.dynamic_index_in_dim(held, (own - slot) % slots, 0, keepdims=False)
+            for slot in range(slots)
+        ]
+    )
     slot_out = summed[:, :images]
     grad_slot_in = summed[:, images:]
     grad_combine = jnp.einsum("bmd,sbd->bsm", d_out, slot_out, preferred_element_type=f32)
@@ -66,8 +90,10 @@
     )
     gl_b = grad_logits.astype(bf16)
     router_terms = jnp.einsum("bmd,bsm->sd", tokens, gl_b, preferred_element_type=f32)
-    terms = exchange(jnp.broadcast_to(router_terms[None], (devices, slots, width)))
-    grad_router = jnp.sum(terms, axis=0).T
+    total = router_terms
+    for shift in range(1, devices):
+        total = total + permute(router_terms, lambda d: d ^ shift)
+    grad_router = total.T
     grad_tokens = jnp.einsum("bsm,sbd->bmd", disp_b, grad_slot_in, preferred_element_type=f32)
     grad_tokens = grad_tokens + jnp.einsum("bsm,ds->bmd", gl_b, router, preferred_element_type=f32)
     return (grad_tokens.astype(bf16), grad_w_in, grad_w_out, grad_router)

time: 63.9 us -> 76.1 us (1.19)
  starting transfers between devices: 7.06 us -> 36.2 us
  blocking collectives: 18.3 us -> 0 us
  local copies, waits for them, and re-layouts: 4.17 us -> 2.61 us
  matrix products: 19.5 us -> 21 us
  waiting for transfers between devices: 11.6 us -> 12.6 us
    ppermute x0 -> x23, starting transfers between devices: none -> 36.2 us  [permute(): lax.ppermute(block, 'expert', [(source, move(source)) for source in range...]
    all_to_all x1 -> x0, blocking collectives: 18.3 us -> none  [exchange(): lax.all_to_all(blocks, 'expert', split_axis=0, concat_axis=0, tiled=True)]
    ppermute x0 -> x23, waiting for transfers between devices: none -> 12.6 us  [permute(): lax.ppermute(block, 'expert', [(source, move(source)) for source in range...]
    all_to_all x2 -> x0, waiting for transfers between devices: 11.6 us -> none  [exchange(): lax.all_to_all(blocks, 'expert', split_axis=0, concat_axis=0, tiled=True)]
    all_to_all x2 -> x0, starting transfers between devices: 7.06 us -> none  [exchange(): lax.all_to_all(blocks, 'expert', split_axis=0, concat_axis=0, tiled=True)]
    dot_general x1, matrix products: 0.62 us -> 2.17 us  [per_device(): jnp.einsum('bd,fd->bf', rows_grad, w_two, preferred_element_type=f32)]
    unnamed x10 -> x13, local copies, waits for them, and re-layouts: 2.93 us -> 1.59 us
    another operation x0 -> x8, other arithmetic: none -> 1.25 us  [the longest x6 0.93 us: per_device(): rows = jnp.stack([rows, permute(rows, lambda d: d ^ bit)])]
  transfers between devices with their start and end apart: 2 -> 23, of which waited for: 2 -> 7; matrix products, arithmetic and copies ran while one was open for 12% -> 14% of each run, Pallas kernels for 0% -> 0%
where the time goes in v2:
time: 76.1 us; the launch traced here: 75.8 us
  starting transfers between devices  36.2 us (48%)
  matrix products  21 us (28%)
  waiting for transfers between devices  12.6 us (17%)
  local copies, waits for them, and re-layouts  2.61 us (3%)
  other arithmetic  2.4 us (3%)
  between operations  0.97 us (1%)
    ppermute x23, starting transfers between devices, permute(): lax.ppermute(block, 'expert', [(source, move(source)) for source in range...  36.2 us
    ppermute x23, waiting for transfers between devices, permute(): lax.ppermute(block, 'expert', [(source, move(source)) for source in range...  12.6 us
    dot_general x1, matrix products, per_device(): jnp.einsum('bsm,ds->bmd', gl_b, router, preferred_element_type=f32)  4.25 us
    dot_general x1, matrix products, per_device(): jnp.einsum('bsm,sbd->bmd', disp_b, grad_slot_in, preferred_element_type=f32)  2.74 us
    dot_general x1, matrix products, per_device(): jnp.einsum('bd,fd->bf', rows_grad, w_two, preferred_element_type=f32)  2.17 us
    dot_general x1, matrix products, per_device(): hidden_pre = jnp.dot(rows_in, w_one, preferred_element_type=f32)  1.95 us
    dot_general x1, matrix products, per_device(): jnp.einsum('bsm,bmd->sbd', comb_b, d_out, preferred_element_type=f32)  1.94 us
    dot_general x1, matrix products, per_device(): jnp.einsum('bf,bd->fd', hidden, rows_grad, preferred_element_type=f32)  1.8 us
  transfers between devices with their start and end apart: 23, of which 7 were waited for; matrix products, arithmetic and copies ran while one was open for 14% of the time, Pallas kernels for 0%

profile of v2, /device:TPU:0, one launch (start us, length us, event | category | flops | bytes accessed | tf_op | source)
XLA Modules:
  0.0 75.8 jit_solution(9514191196041770802)
XLA Ops:
  0.7 1.5 %copy-done = bf16[3,256,1280]{2,1,0:T(8,128)(2,1)S(1)} copy-done((bf16[3,256,1280]{2,1,0:T(8,128)(2,1)S(1)}, bf16[3,256,1280]{2,1,0:T(8,128)(2,1)}, u32[]{:S(2)}) %copy-start) | copy-done | bytes 1966104
  4.2 1.9 %fusion.8 = bf16[2,3,1280]{2,0,1:T(2,128)(2,1)S(1)} fusion(bf16[3,256,1280]{2,1,0:T(8,128)(2,1)} %param.9, f32[3,2,256]{2,1,0:T(2,128)S(1)} %get-tuple-element.13, f32[3,256]{1,0:T(4,128)S(1)} %get-tuple-element.12), kind=kOutput, calls=%fused_computation.15 | convolution fusion | flops 3942912 | bytes 1990656 | tf_op jit(solution)/shard_map/bsm,bmd->sbd/dot_general | solution.py:34
  6.2 4.1 %collective-permute-start = (bf16[6,1280]{1,0:T(8,128)(2,1)S(1)}, bf16[6,1280]{1,0:T(8,128)(2,1)S(1)}, u32[]{:S(2)}, u32[]{:S(2)}) collective-permute-start(bf16[6,1280]{1,0:T(8,128)(2,1)S(1)} %bitcast.73), channel_id=1, source_target_pairs={{0,8},{1,9},{2,10},{3,11},{4,12},{5,13},{6,14},{7,15},{8,0},{9,1},... | collective-permute-start | bytes 46088 | tf_op jit(solution)/shard_map/ppermute | solution.py:13
  10.3 1.8 %collective-permute-done = bf16[6,1280]{1,0:T(8,128)(2,1)S(1)} collective-permute-done((bf16[6,1280]{1,0:T(8,128)(2,1)S(1)}, bf16[6,1280]{1,0:T(8,128)(2,1)S(1)}, u32[]{:S(2)}, u32[]{:S(2)}) %collective-permute-start) | collective-permute-done | bytes 15392 | tf_op jit(solution)/shard_map/ppermute | solution.py:13
  12.2 2.0 %collective-permute-start.1 = (bf16[2,6,1280]{2,0,1:T(2,128)(2,1)S(1)}, bf16[2,6,1280]{2,0,1:T(2,128)(2,1)S(1)}, u32[]{:S(2)}, u32[]{:S(2)}) collective-permute-start(bf16[2,6,1280]{2,0,1:T(2,128)(2,1)S(1)} %pad_maximum_fusion.3), channel_id=1, source_target_pairs={{0,4},{1,5},{2,6},{3,7},{4,0},{5,1},{6,2},{7,3},{8,12},{9,13},{10,... | collective-permute-start | bytes 92168 | tf_op jit(solution)/shard_map/ppermute | solution.py:13
  14.2 1.9 %collective-permute-done.1 = bf16[2,6,1280]{2,0,1:T(2,128)(2,1)S(1)} collective-permute-done((bf16[2,6,1280]{2,0,1:T(2,128)(2,1)S(1)}, bf16[2,6,1280]{2,0,1:T(2,128)(2,1)S(1)}, u32[]{:S(2)}, u32[]{:S(2)}) %collective-permute-start.1) | collective-permute-done | bytes 30752 | tf_op jit(solution)/shard_map/ppermute | solution.py:13
  16.2 2.0 %collective-permute-start.2 = (bf16[2,2,6,1280]{3,1,2,0:T(2,128)(2,1)S(1)}, bf16[2,2,6,1280]{3,1,2,0:T(2,128)(2,1)S(1)}, u32[]{:S(2)}, u32[]{:S(2)}) collective-permute-start(bf16[2,2,6,1280]{3,1,2,0:T(2,128)(2,1)S(1)} %pad_maximum_fusion.2), channel_id=1, source_target_pairs={{0,2},{1,3},{2,0},{3,1},{4,6},{5,7},{6,4},{7,5},{8,10},{9,11},{10,... | collective-permute-start | bytes 184328 | tf_op jit(solution)/shard_map/ppermute | solution.py:13
  18.3 2.2 %collective-permute-done.2 = bf16[2,2,6,1280]{3,1,2,0:T(2,128)(2,1)S(1)} collective-permute-done((bf16[2,2,6,1280]{3,1,2,0:T(2,128)(2,1)S(1)}, bf16[2,2,6,1280]{3,1,2,0:T(2,128)(2,1)S(1)}, u32[]{:S(2)}, u32[]{:S(2)}) %collective-permute-start.2) | collective-permute-done | bytes 61472 | tf_op jit(solution)/shard_map/ppermute | solution.py:13
  23.0 1.9 %fusion.13 = f32[48,640]{1,0:T(8,128)S(1)} fusion(bf16[48,1280]{1,0:T(8,128)(2,1)S(1)} %reshape.45, bf16[1,1280,640]{2,1,0:T(8,128)(2,1)} %param.7), kind=kOutput, calls=%fused_computation.21 | convolution fusion | flops 78643200 | bytes 1884160 | tf_op jit(solution)/shard_map/dot_general | solution.py:51
  25.6 2.2 %fusion.31 = bf16[48,640]{1,0:T(8,128)(2,1)S(1)} fusion(f32[48,640]{1,0:T(8,128)S(1)} %fusion.13, bf16[48,1280]{1,0:T(8,128)(2,1)S(1)} %reshape.47, bf16[1,640,1280]{2,1,0:T(8,128)(2,1)} %param.8), kind=kOutput, calls=%fused_computation.44 | convolution fusion | flops 79257600 | bytes 1945600 | tf_op jit(solution)/shard_map/bd,fd->bf/dot_general | solution.py:54
  30.0 2.0 %collective-permute-start.5 = (bf16[4,6,1280]{2,0,1:T(4,128)(2,1)S(1)}, bf16[4,6,1280]{2,0,1:T(4,128)(2,1)S(1)}, u32[]{:S(2)}, u32[]{:S(2)}) collective-permute-start(bf16[4,6,1280]{2,0,1:T(4,128)(2,1)S(1)} %slice.59), channel_id=1, source_target_pairs={{0,2},{1,3},{2,0},{3,1},{4,6},{5,7},{6,4},{7,5},{8,10},{9,11},{10,... | collective-permute-start | bytes 184328 | tf_op jit(solution)/shard_map/ppermute | solution.py:13
  32.0 2.3 %collective-permute-done.5 = bf16[4,6,1280]{2,0,1:T(4,128)(2,1)S(1)} collective-permute-done((bf16[4,6,1280]{2,0,1:T(4,128)(2,1)S(1)}, bf16[4,6,1280]{2,0,1:T(4,128)(2,1)S(1)}, u32[]{:S(2)}, u32[]{:S(2)}) %collective-permute-start.5) | collective-permute-done | bytes 61472 | tf_op jit(solution)/shard_map/ppermute | solution.py:13
  34.4 1.9 %collective-permute-start.6 = (bf16[2,6,1280]{2,0,1:T(2,128)(2,1)S(1)}, bf16[2,6,1280]{2,0,1:T(2,128)(2,1)S(1)}, u32[]{:S(2)}, u32[]{:S(2)}) collective-permute-start(bf16[2,6,1280]{2,0,1:T(2,128)(2,1)S(1)} %slice.61), channel_id=1, source_target_pairs={{0,4},{1,5},{2,6},{3,7},{4,0},{5,1},{6,2},{7,3},{8,12},{9,13},{10,... | collective-permute-start | bytes 92168 | tf_op jit(solution)/shard_map/ppermute | solution.py:13
  36.3 2.0 %collective-permute-done.6 = bf16[2,6,1280]{2,0,1:T(2,128)(2,1)S(1)} collective-permute-done((bf16[2,6,1280]{2,0,1:T(2,128)(2,1)S(1)}, bf16[2,6,1280]{2,0,1:T(2,128)(2,1)S(1)}, u32[]{:S(2)}, u32[]{:S(2)}) %collective-permute-start.6) | collective-permute-done | bytes 30752 | tf_op jit(solution)/shard_map/ppermute | solution.py:13
  38.5 2.9 %collective-permute-start.7 = (bf16[6,1280]{1,0:T(8,128)(2,1)S(1)}, bf16[6,1280]{1,0:T(8,128)(2,1)S(1)}, u32[]{:S(2)}, u32[]{:S(2)}) collective-permute-start(bf16[6,1280]{1,0:T(8,128)(2,1)S(1)} %bitcast.71), channel_id=1, source_target_pairs={{0,8},{1,9},{2,10},{3,11},{4,12},{5,13},{6,14},{7,15},{8,0},{9,1},... | collective-permute-start | bytes 46088 | tf_op jit(solution)/shard_map/ppermute | solution.py:13
  41.4 1.8 %fusion.6 = bf16[1,640,1280]{2,1,0:T(8,128)(2,1)} fusion(bf16[48,1280]{1,0:T(8,128)(2,1)S(1)} %reshape.47, f32[48,640]{1,0:T(8,128)S(1)} %fusion.13), kind=kOutput, calls=%fused_computation.9 | convolution fusion | flops 79738880 | bytes 1884160 | tf_op jit(solution)/shard_map/bf,bd->fd/dot_general | solution.py:57
  46.6 3.7 %collective-permute-start.21 = (f32[2,1280]{1,0:T(2,128)S(1)}, f32[2,1280]{1,0:T(2,128)S(1)}, u32[]{:S(2)}, u32[]{:S(2)}) collective-permute-start(f32[2,1280]{1,0:T(2,128)S(1)} %convolution_bitcast_fusion), channel_id=1, source_target_pairs={{0,14},{1,15},{2,12},{3,13},{4,10},{5,11},{6,8},{7,9},{8,6},{9,7},... | collective-permute-start | bytes 30728 | tf_op jit(solution)/shard_map/ppermute | solution.py:13
  50.4 3.2 %collective-permute-start.20 = (f32[2,1280]{1,0:T(2,128)S(1)}, f32[2,1280]{1,0:T(2,128)S(1)}, u32[]{:S(2)}, u32[]{:S(2)}) collective-permute-start(f32[2,1280]{1,0:T(2,128)S(1)} %convolution_bitcast_fusion), channel_id=1, source_target_pairs={{0,13},{1,12},{2,15},{3,14},{4,9},{5,8},{6,11},{7,10},{8,5},{9,4},... | collective-permute-start | bytes 30728 | tf_op jit(solution)/shard_map/ppermute | solution.py:13
  53.9 1.8 %fusion.5 = bf16[1,1280,640]{2,1,0:T(8,128)(2,1)} fusion(bf16[48,1280]{1,0:T(8,128)(2,1)S(1)} %reshape.45, bf16[48,640]{1,0:T(8,128)(2,1)S(1)} %fusion.31), kind=kOutput, calls=%fused_computation.8 | convolution fusion | flops 79462400 | bytes 1822720 | tf_op jit(solution)/shard_map/bd,bf->df/dot_general | solution.py:58
  55.7 3.6 %collective-permute-start.17 = (f32[2,1280]{1,0:T(2,128)S(1)}, f32[2,1280]{1,0:T(2,128)S(1)}, u32[]{:S(2)}, u32[]{:S(2)}) collective-permute-start(f32[2,1280]{1,0:T(2,128)S(1)} %convolution_bitcast_fusion), channel_id=1, source_target_pairs={{0,10},{1,11},{2,8},{3,9},{4,14},{5,15},{6,12},{7,13},{8,2},{9,3},... | collective-permute-start | bytes 30728 | tf_op jit(solution)/shard_map/ppermute | solution.py:13
  59.3 2.6 %collective-permute-start.15 = (f32[2,1280]{1,0:T(2,128)S(1)}, f32[2,1280]{1,0:T(2,128)S(1)}, u32[]{:S(2)}, u32[]{:S(2)}) collective-permute-start(f32[2,1280]{1,0:T(2,128)S(1)} %convolution_bitcast_fusion), channel_id=1, source_target_pairs={{0,8},{1,9},{2,10},{3,11},{4,12},{5,13},{6,14},{7,15},{8,0},{9,1},... | collective-permute-start | bytes 30728 | tf_op jit(solution)/shard_map/ppermute | solution.py:13
  61.9 1.9 %collective-permute-start.14 = (f32[2,1280]{1,0:T(2,128)S(1)}, f32[2,1280]{1,0:T(2,128)S(1)}, u32[]{:S(2)}, u32[]{:S(2)}) collective-permute-start(f32[2,1280]{1,0:T(2,128)S(1)} %convolution_bitcast_fusion), channel_id=1, source_target_pairs={{0,7},{1,6},{2,5},{3,4},{4,3},{5,2},{6,1},{7,0},{8,15},{9,14},{10,... | collective-permute-start | bytes 30728 | tf_op jit(solution)/shard_map/ppermute | solution.py:13
  64.5 2.7 %fusion.34 = f32[3,256,1280]{2,1,0:T(8,128)} fusion(bf16[1,6,1280]{2,0,1:T(2,128)(2,1)S(1)} %get-tuple-element.7, bf16[1,6,1280]{2,0,1:T(2,128)(2,1)S(1)} %get-tuple-element.6, f32[3,2]{1,0:T(4,128)S(1)} %get-tuple-element.14, f32[3,2,256]{2,1,0:T(2,128)S(1)} %convolution_bitcast_fusion.1), kind=kOutput, calls=%fused_computation.60 | convolution fusion | flops 3967749 | bytes 3969048 | tf_op jit(solution)/shard_map/bsm,sbd->bmd/dot_general | solution.py:97
  70.9 4.3 %fusion.4 = bf16[3,256,1280]{2,1,0:T(8,128)(2,1)} fusion(f32[3,256,1280]{2,1,0:T(8,128)} %fusion.34, f32[3,2,256]{2,1,0:T(2,128)S(1)} %fusion.23, f32[3,2,256]{2,1,0:T(2,128)S(1)} %fusion.52, bf16[1280,2]{0,1:T(2,128)(2,1)S(1)} %copy-done.4, f32[3,2,256]{2,1,0:T(2,128)S(1)} %get-tuple-element.15, f32[3,2]{1,0:T(4,128)S(1)} %get-tuple-element.14), kind=kOutput, calls=%fused_computation.5 | convolution fusion | flops 5909253 | bytes 5921816 | tf_op jit(solution)/shard_map/bsm,ds->bmd/dot_general | solution.py:98
  (81 shorter events, 16.6 us)
Async XLA Ops:
  6.2 5.9 %collective-permute-start = (bf16[6,1280]{1,0:T(8,128)(2,1)S(1)}, bf16[6,1280]{1,0:T(8,128)(2,1)S(1)}, u32[]{:S(2)}, u32[]{:S(2)}) collective-permute-start(bf16[6,1280]{1,0:T(8,128)(2,1)S(1)} %bitcast.73), channel_id=1, source_target_pairs={{0,8},{1,9},{2,10},{3,11},{4,12},{5,13},{6,14},{7,15},{8,0},{9,1},... | collective-permute-start | bytes 46088 | tf_op jit(solution)/shard_map/ppermute | solution.py:13
  12.2 4.0 %collective-permute-start.1 = (bf16[2,6,1280]{2,0,1:T(2,128)(2,1)S(1)}, bf16[2,6,1280]{2,0,1:T(2,128)(2,1)S(1)}, u32[]{:S(2)}, u32[]{:S(2)}) collective-permute-start(bf16[2,6,1280]{2,0,1:T(2,128)(2,1)S(1)} %pad_maximum_fusion.3), channel_id=1, source_target_pairs={{0,4},{1,5},{2,6},{3,7},{4,0},{5,1},{6,2},{7,3},{8,12},{9,13},{10,... | collective-permute-start | bytes 92168 | tf_op jit(solution)/shard_map/ppermute | solution.py:13
  16.2 4.3 %collective-permute-start.2 = (bf16[2,2,6,1280]{3,1,2,0:T(2,128)(2,1)S(1)}, bf16[2,2,6,1280]{3,1,2,0:T(2,128)(2,1)S(1)}, u32[]{:S(2)}, u32[]{:S(2)}) collective-permute-start(bf16[2,2,6,1280]{3,1,2,0:T(2,128)(2,1)S(1)} %pad_maximum_fusion.2), channel_id=1, source_target_pairs={{0,2},{1,3},{2,0},{3,1},{4,6},{5,7},{6,4},{7,5},{8,10},{9,11},{10,... | collective-permute-start | bytes 184328 | tf_op jit(solution)/shard_map/ppermute | solution.py:13
  20.7 1.4 %collective-permute-start.3 = (bf16[2,2,2,6,1280]{4,2,3,1,0:T(2,128)(2,1)S(1)}, bf16[2,2,2,6,1280]{4,2,3,1,0:T(2,128)(2,1)S(1)}, u32[]{:S(2)}, u32[]{:S(2)}) collective-permute-start(bf16[2,2,2,6,1280]{4,2,3,1,0:T(2,128)(2,1)S(1)} %pad_maximum_fusion.1), channel_id=1, source_target_pairs={{0,1},{1,0},{2,3},{3,2},{4,5},{5,4},{6,7},{7,6},{8,9},{9,8},{10,11... | collective-permute-start | bytes 368648 | tf_op jit(solution)/shard_map/ppermute | solution.py:13
  28.5 1.4 %collective-permute-start.4 = (bf16[8,6,1280]{2,0,1:T(8,128)(2,1)S(1)}, bf16[8,6,1280]{2,0,1:T(8,128)(2,1)S(1)}, u32[]{:S(2)}, u32[]{:S(2)}) collective-permute-start(bf16[8,6,1280]{2,0,1:T(8,128)(2,1)S(1)} %slice.57), channel_id=1, source_target_pairs={{0,1},{1,0},{2,3},{3,2},{4,5},{5,4},{6,7},{7,6},{8,9},{9,8},{10,11... | collective-permute-start | bytes 368648 | tf_op jit(solution)/shard_map/ppermute | solution.py:13
  30.0 4.3 %collective-permute-start.5 = (bf16[4,6,1280]{2,0,1:T(4,128)(2,1)S(1)}, bf16[4,6,1280]{2,0,1:T(4,128)(2,1)S(1)}, u32[]{:S(2)}, u32[]{:S(2)}) collective-permute-start(bf16[4,6,1280]{2,0,1:T(4,128)(2,1)S(1)} %slice.59), channel_id=1, source_target_pairs={{0,2},{1,3},{2,0},{3,1},{4,6},{5,7},{6,4},{7,5},{8,10},{9,11},{10,... | collective-permute-start | bytes 184328 | tf_op jit(solution)/shard_map/ppermute | solution.py:13
  34.4 4.0 %collective-permute-start.6 = (bf16[2,6,1280]{2,0,1:T(2,128)(2,1)S(1)}, bf16[2,6,1280]{2,0,1:T(2,128)(2,1)S(1)}, u32[]{:S(2)}, u32[]{:S(2)}) collective-permute-start(bf16[2,6,1280]{2,0,1:T(2,128)(2,1)S(1)} %slice.61), channel_id=1, source_target_pairs={{0,4},{1,5},{2,6},{3,7},{4,0},{5,1},{6,2},{7,3},{8,12},{9,13},{10,... | collective-permute-start | bytes 92168 | tf_op jit(solution)/shard_map/ppermute | solution.py:13
  38.5 4.8 %collective-permute-start.7 = (bf16[6,1280]{1,0:T(8,128)(2,1)S(1)}, bf16[6,1280]{1,0:T(8,128)(2,1)S(1)}, u32[]{:S(2)}, u32[]{:S(2)}) collective-permute-start(bf16[6,1280]{1,0:T(8,128)(2,1)S(1)} %bitcast.71), channel_id=1, source_target_pairs={{0,8},{1,9},{2,10},{3,11},{4,12},{5,13},{6,14},{7,15},{8,0},{9,1},... | collective-permute-start | bytes 46088 | tf_op jit(solution)/shard_map/ppermute | solution.py:13
  45.4 10.3 %collective-permute-start.22 = (f32[2,1280]{1,0:T(2,128)S(1)}, f32[2,1280]{1,0:T(2,128)S(1)}, u32[]{:S(2)}, u32[]{:S(2)}) collective-permute-start(f32[2,1280]{1,0:T(2,128)S(1)} %convolution_bitcast_fusion), channel_id=1, source_target_pairs={{0,15},{1,14},{2,13},{3,12},{4,11},{5,10},{6,9},{7,8},{8,7},{9,6},... | collective-permute-start | bytes 30728 | tf_op jit(solution)/shard_map/ppermute | solution.py:13
  46.6 12.6 %collective-permute-start.21 = (f32[2,1280]{1,0:T(2,128)S(1)}, f32[2,1280]{1,0:T(2,128)S(1)}, u32[]{:S(2)}, u32[]{:S(2)}) collective-permute-start(f32[2,1280]{1,0:T(2,128)S(1)} %convolution_bitcast_fusion), channel_id=1, source_target_pairs={{0,14},{1,15},{2,12},{3,13},{4,10},{5,11},{6,8},{7,9},{8,6},{9,7},... | collective-permute-start | bytes 30728 | tf_op jit(solution)/shard_map/ppermute | solution.py:13
  50.4 8.9 %collective-permute-start.20 = (f32[2,1280]{1,0:T(2,128)S(1)}, f32[2,1280]{1,0:T(2,128)S(1)}, u32[]{:S(2)}, u32[]{:S(2)}) collective-permute-start(f32[2,1280]{1,0:T(2,128)S(1)} %convolution_bitcast_fusion), channel_id=1, source_target_pairs={{0,13},{1,12},{2,15},{3,14},{4,9},{5,8},{6,11},{7,10},{8,5},{9,4},... | collective-permute-start | bytes 30728 | tf_op jit(solution)/shard_map/ppermute | solution.py:13
  53.5 8.3 %collective-permute-start.19 = (f32[2,1280]{1,0:T(2,128)S(1)}, f32[2,1280]{1,0:T(2,128)S(1)}, u32[]{:S(2)}, u32[]{:S(2)}) collective-permute-start(f32[2,1280]{1,0:T(2,128)S(1)} %convolution_bitcast_fusion), channel_id=1, source_target_pairs={{0,12},{1,13},{2,14},{3,15},{4,8},{5,9},{6,10},{7,11},{8,4},{9,5},... | collective-permute-start | bytes 30728 | tf_op jit(solution)/shard_map/ppermute | solution.py:13
  53.9 9.9 %collective-permute-start.18 = (f32[2,1280]{1,0:T(2,128)S(1)}, f32[2,1280]{1,0:T(2,128)S(1)}, u32[]{:S(2)}, u32[]{:S(2)}) collective-permute-start(f32[2,1280]{1,0:T(2,128)S(1)} %convolution_bitcast_fusion), channel_id=1, source_target_pairs={{0,11},{1,10},{2,9},{3,8},{4,15},{5,14},{6,13},{7,12},{8,3},{9,2},... | collective-permute-start | bytes 30728 | tf_op jit(solution)/shard_map/ppermute | solution.py:13
  55.7 15.2 %copy-start.4 = (bf16[1280,2]{0,1:T(2,128)(2,1)S(1)}, bf16[1280,2]{0,1:T(2,128)(2,1)}, u32[]{:S(2)}) copy-start(bf16[1280,2]{0,1:T(2,128)(2,1)} %param.6) | copy-start | bytes 15364
  55.7 11.6 %collective-permute-start.17 = (f32[2,1280]{1,0:T(2,128)S(1)}, f32[2,1280]{1,0:T(2,128)S(1)}, u32[]{:S(2)}, u32[]{:S(2)}) collective-permute-start(f32[2,1280]{1,0:T(2,128)S(1)} %convolution_bitcast_fusion), channel_id=1, source_target_pairs={{0,10},{1,11},{2,8},{3,9},{4,14},{5,15},{6,12},{7,13},{8,2},{9,3},... | collective-permute-start | bytes 30728 | tf_op jit(solution)/shard_map/ppermute | solution.py:13
  59.2 9.3 %collective-permute-start.16 = (f32[2,1280]{1,0:T(2,128)S(1)}, f32[2,1280]{1,0:T(2,128)S(1)}, u32[]{:S(2)}, u32[]{:S(2)}) collective-permute-start(f32[2,1280]{1,0:T(2,128)S(1)} %convolution_bitcast_fusion), channel_id=1, source_target_pairs={{0,9},{1,8},{2,11},{3,10},{4,13},{5,12},{6,15},{7,14},{8,1},{9,0},... | collective-permute-start | bytes 30728 | tf_op jit(solution)/shard_map/ppermute | solution.py:13
  59.3 9.7 %collective-permute-start.15 = (f32[2,1280]{1,0:T(2,128)S(1)}, f32[2,1280]{1,0:T(2,128)S(1)}, u32[]{:S(2)}, u32[]{:S(2)}) collective-permute-start(f32[2,1280]{1,0:T(2,128)S(1)} %convolution_bitcast_fusion), channel_id=1, source_target_pairs={{0,8},{1,9},{2,10},{3,11},{4,12},{5,13},{6,14},{7,15},{8,0},{9,1},... | collective-permute-start | bytes 30728 | tf_op jit(solution)/shard_map/ppermute | solution.py:13
  61.9 8.1 %collective-permute-start.14 = (f32[2,1280]{1,0:T(2,128)S(1)}, f32[2,1280]{1,0:T(2,128)S(1)}, u32[]{:S(2)}, u32[]{:S(2)}) collective-permute-start(f32[2,1280]{1,0:T(2,128)S(1)} %convolution_bitcast_fusion), channel_id=1, source_target_pairs={{0,7},{1,6},{2,5},{3,4},{4,3},{5,2},{6,1},{7,0},{8,15},{9,14},{10,... | collective-permute-start | bytes 30728 | tf_op jit(solution)/shard_map/ppermute | solution.py:13
  63.7 7.1 %collective-permute-start.13 = (f32[2,1280]{1,0:T(2,128)S(1)}, f32[2,1280]{1,0:T(2,128)S(1)}, u32[]{:S(2)}, u32[]{:S(2)}) collective-permute-start(f32[2,1280]{1,0:T(2,128)S(1)} %convolution_bitcast_fusion), channel_id=1, source_target_pairs={{0,6},{1,7},{2,4},{3,5},{4,2},{5,3},{6,0},{7,1},{8,14},{9,15},{10,... | collective-permute-start | bytes 30728 | tf_op jit(solution)/shard_map/ppermute | solution.py:13
  67.3 7.8 %collective-permute-start.12 = (f32[2,1280]{1,0:T(2,128)S(1)}, f32[2,1280]{1,0:T(2,128)S(1)}, u32[]{:S(2)}, u32[]{:S(2)}) collective-permute-start(f32[2,1280]{1,0:T(2,128)S(1)} %convolution_bitcast_fusion), channel_id=1, source_target_pairs={{0,5},{1,4},{2,7},{3,6},{4,1},{5,0},{6,3},{7,2},{8,13},{9,12},{10,... | collective-permute-start | bytes 30728 | tf_op jit(solution)/shard_map/ppermute | solution.py:13
  68.5 6.6 %collective-permute-start.11 = (f32[2,1280]{1,0:T(2,128)S(1)}, f32[2,1280]{1,0:T(2,128)S(1)}, u32[]{:S(2)}, u32[]{:S(2)}) collective-permute-start(f32[2,1280]{1,0:T(2,128)S(1)} %convolution_bitcast_fusion), channel_id=1, source_target_pairs={{0,4},{1,5},{2,6},{3,7},{4,0},{5,1},{6,2},{7,3},{8,12},{9,13},{10,... | collective-permute-start | bytes 30728 | tf_op jit(solution)/shard_map/ppermute | solution.py:13
  69.0 6.1 %collective-permute-start.10 = (f32[2,1280]{1,0:T(2,128)S(1)}, f32[2,1280]{1,0:T(2,128)S(1)}, u32[]{:S(2)}, u32[]{:S(2)}) collective-permute-start(f32[2,1280]{1,0:T(2,128)S(1)} %convolution_bitcast_fusion), channel_id=1, source_target_pairs={{0,3},{1,2},{2,1},{3,0},{4,7},{5,6},{6,5},{7,4},{8,11},{9,10},{10,... | collective-permute-start | bytes 30728 | tf_op jit(solution)/shard_map/ppermute | solution.py:13
  70.0 5.2 %collective-permute-start.9 = (f32[2,1280]{1,0:T(2,128)S(1)}, f32[2,1280]{1,0:T(2,128)S(1)}, u32[]{:S(2)}, u32[]{:S(2)}) collective-permute-start(f32[2,1280]{1,0:T(2,128)S(1)} %convolution_bitcast_fusion), channel_id=1, source_target_pairs={{0,2},{1,3},{2,0},{3,1},{4,6},{5,7},{6,4},{7,5},{8,10},{9,11},{10,... | collective-permute-start | bytes 30728 | tf_op jit(solution)/shard_map/ppermute | solution.py:13
  70.8 4.4 %collective-permute-start.8 = (f32[2,1280]{1,0:T(2,128)S(1)}, f32[2,1280]{1,0:T(2,128)S(1)}, u32[]{:S(2)}, u32[]{:S(2)}) collective-permute-start(f32[2,1280]{1,0:T(2,128)S(1)} %convolution_bitcast_fusion), channel_id=1, source_target_pairs={{0,1},{1,0},{2,3},{3,2},{4,5},{5,4},{6,7},{7,6},{8,9},{9,8},{10,11... | collective-permute-start | bytes 30728 | tf_op jit(solution)/shard_map/ppermute | solution.py:13
  (4 other events, 12.9 us)

commit v3 on v1

--- a/solution.py
+++ b/solution.py
@@ -9,7 +9,16 @@
 
 
 def exchange(blocks):
-    return lax.all_to_all(blocks, "expert", split_axis=0, concat_axis=0, tiled=True)
+    count = lax.axis_size("expert")
+    groups = [list(range(core, count, 2)) for core in range(2)]
+    return lax.all_to_all(
+        blocks, "expert", split_axis=0, concat_axis=0, axis_index_groups=groups, tiled=True
+    )
+
+
+def other_core(block):
+    count = lax.axis_size("expert")
+    return lax.ppermute(block, "expert", [(device, device ^ 1) for device in range(count)])
 
 
 def per_device(tokens, router, w_in, w_out, d_out):
@@ -29,9 +38,11 @@
     grad_slot_out = jnp.einsum("bsm,bmd->sbd", comb_b, d_out, preferred_element_type=f32).astype(
         bf16
     )
+    chips = devices // 2
     rows = jnp.concatenate([slot_in, grad_slot_out], axis=1)
-    rows = jnp.broadcast_to(rows[:, None], (slots, split_count, 2 * images, width))
-    rows = exchange(rows.reshape(devices, 2 * images, width))
+    rows = jnp.broadcast_to(rows[:, None], (slots, split_count // 2, 2 * images, width))
+    rows = exchange(rows.reshape(chips, 2 * images, width))
+    rows = jnp.stack([rows, other_core(rows)]).reshape(devices, 2 * images, width)
     rows_in = rows[:, :images].reshape(devices * images, width)
     rows_grad = rows[:, images:].reshape(devices * images, width)
     w_one = w_in[0]
@@ -52,7 +63,9 @@
         ],
         axis=1,
     )
-    shares = exchange(shares).reshape(slots, split_count, 2 * images, width)
+    shares = shares.reshape(2, chips, 2 * images, width)
+    shares = shares[0].astype(f32) + other_core(shares[1]).astype(f32)
+    shares = exchange(shares.astype(bf16)).reshape(slots, split_count // 2, 2 * images, width)
     summed = jnp.sum(shares.astype(f32), axis=1).astype(bf16)
     slot_out = summed[:, :images]
     grad_slot_in = summed[:, images:]
@@ -66,7 +79,8 @@
     )
     gl_b = grad_logits.astype(bf16)
     router_terms = jnp.einsum("bmd,bsm->sd", tokens, gl_b, preferred_element_type=f32)
-    terms = exchange(jnp.broadcast_to(router_terms[None], (devices, slots, width)))
+    terms = router_terms + other_core(router_terms)
+    terms = exchange(jnp.broadcast_to(terms[None], (chips, slots, width)))
     grad_router = jnp.sum(terms, axis=0).T
     grad_tokens = jnp.einsum("bsm,sbd->bmd", disp_b, grad_slot_in, preferred_element_type=f32)
     grad_tokens = grad_tokens + jnp.einsum("bsm,ds->bmd", gl_b, router, preferred_element_type=f32)

time: 63.9 us -> 59.1 us (0.925)
  blocking collectives: 18.3 us -> 14.6 us
  waiting for transfers between devices: 11.6 us -> 9.93 us
  matrix products: 19.5 us -> 21.1 us
  local copies, waits for them, and re-layouts: 4.17 us -> 3.18 us
    all_to_all x2, waiting for transfers between devices: 11.6 us -> 7.29 us  [exchange(): lax.all_to_all(blocks, 'expert', split_axis=0, concat_axis=0, axis_index_...]
    all_to_all x1, blocking collectives: 18.3 us -> 14.6 us  [exchange(): lax.all_to_all(blocks, 'expert', split_axis=0, concat_axis=0, axis_index_...]
    ppermute x0 -> x3, waiting for transfers between devices: none -> 2.65 us  [other_core(): lax.ppermute(block, 'expert', [(device, device ^ 1) for device in range(c...]
    dot_general x1, matrix products: 0.62 us -> 2.16 us  [per_device(): jnp.einsum('bmd,sbd->bsm', d_out, slot_out, preferred_element_type=f32)]
    unnamed x10 -> x8, local copies, waits for them, and re-layouts: 2.93 us -> 2 us
    concatenate x1, other arithmetic: 0.89 us -> 0.09 us  [per_device(): jnp.concatenate([out_part.astype(bf16).reshape(devices, images, width), s...]
    convert_element_type x0 -> x1, other arithmetic: none -> 0.77 us  [per_device(): shares.astype(bf16)]
  transfers between devices with their start and end apart: 2 -> 5, of which waited for: 2 -> 4; matrix products, arithmetic and copies ran while one was open for 12% -> 18% of each run, Pallas kernels for 0% -> 0%
where the time goes in v3:
time: 59.1 us; the launch traced here: 58.5 us
  matrix products  21.1 us (36%)
  blocking collectives  14.6 us (25%)
  waiting for transfers between devices  9.93 us (17%)
  starting transfers between devices  6.95 us (12%)
  local copies, waits for them, and re-layouts  3.18 us (5%)
  other arithmetic  1.95 us (3%)
  between operations  0.81 us (1%)
    all_to_all x1, blocking collectives, exchange(): lax.all_to_all(blocks, 'expert', split_axis=0, concat_axis=0, axis_index_...  14.6 us
    all_to_all x2, waiting for transfers between devices, exchange(): lax.all_to_all(blocks, 'expert', split_axis=0, concat_axis=0, axis_index_...  7.29 us
    all_to_all x2, starting transfers between devices, exchange(): lax.all_to_all(blocks, 'expert', split_axis=0, concat_axis=0, axis_index_...  6.74 us
    dot_general x1, matrix products, per_device(): jnp.einsum('bsm,ds->bmd', gl_b, router, preferred_element_type=f32)  4.25 us
    dot_general x1, matrix products, per_device(): jnp.einsum('bsm,sbd->bmd', disp_b, grad_slot_in, preferred_element_type=f32)  2.76 us
    ppermute x3, waiting for transfers between devices, other_core(): lax.ppermute(block, 'expert', [(device, device ^ 1) for device in range(c...  2.65 us
    dot_general x1, matrix products, per_device(): jnp.einsum('bmd,sbd->bsm', d_out, slot_out, preferred_element_type=f32)  2.16 us
    unnamed x8, local copies, waits for them, and re-layouts  2 us
  transfers between devices with their start and end apart: 5, of which 4 were waited for; matrix products, arithmetic and copies ran while one was open for 18% of the time, Pallas kernels for 0%

profile of v3, /device:TPU:0, one launch (start us, length us, event | category | flops | bytes accessed | tf_op | source)
XLA Modules:
  0.0 58.5 jit_solution(11483381939769854802)
XLA Ops:
  0.6 1.5 %copy-done = bf16[3,256,1280]{2,1,0:T(8,128)(2,1)S(1)} copy-done((bf16[3,256,1280]{2,1,0:T(8,128)(2,1)S(1)}, bf16[3,256,1280]{2,1,0:T(8,128)(2,1)}, u32[]{:S(2)}) %copy-start) | copy-done | bytes 1966104
  2.2 1.3 %convolution_bitcast_fusion.1 = f32[3,2,256]{2,1,0:T(2,128)S(1)} fusion(bf16[3,256,1280]{2,1,0:T(8,128)(2,1)S(1)} %copy-done, bf16[1280,2]{0,1:T(2,128)(2,1)} %param.6), kind=kOutput, calls=%fused_computation.32 | convolution fusion | flops 3932160 | bytes 1977344 | tf_op jit(solution)/shard_map/bmd,ds->bsm/dot_general | solution.py:32
  4.2 1.9 %fusion.8 = bf16[2,3,1280]{2,0,1:T(2,128)(2,1)S(1)} fusion(bf16[3,256,1280]{2,1,0:T(8,128)(2,1)} %param.9, f32[3,2,256]{2,1,0:T(2,128)S(1)} %get-tuple-element.9, f32[3,256]{1,0:T(4,128)S(1)} %get-tuple-element.8), kind=kOutput, calls=%fused_computation.15 | convolution fusion | flops 3942912 | bytes 1990656 | tf_op jit(solution)/shard_map/bsm,bmd->sbd/dot_general | solution.py:38
  6.2 14.6 %all_to_all.15 = bf16[8,6,1280]{2,1,0:T(8,128)(2,1)S(1)} all-to-all(bf16[8,6,1280]{2,1,0:T(8,128)(2,1)S(1)} %bitcast.54), channel_id=1, replica_groups={{0,2,4,6,8,10,12,14},{1,3,5,7,9,11,13,15},{16,18,20,22,24,26,28,30},{17..., dimensions={0} | all-to-all | bytes 245760 | tf_op jit(solution)/shard_map/all_to_all | solution.py:14
  20.8 1.4 %collective-permute-done = bf16[8,6,1280]{2,1,0:T(8,128)(2,1)S(1)} collective-permute-done((bf16[8,6,1280]{2,1,0:T(8,128)(2,1)S(1)}, bf16[8,6,1280]{2,1,0:T(8,128)(2,1)S(1)}, u32[]{:S(2)}, u32[]{:S(2)}) %collective-permute-start) | collective-permute-done | bytes 122912 | tf_op jit(solution)/shard_map/ppermute | solution.py:21
  22.7 2.0 %fusion.13 = f32[48,640]{1,0:T(8,128)S(1)} fusion(bf16[48,1280]{1,0:T(8,128)(2,1)S(1)} %reshape.44, bf16[1,1280,640]{2,1,0:T(8,128)(2,1)} %param.7), kind=kOutput, calls=%fused_computation.21 | convolution fusion | flops 78643200 | bytes 1884160 | tf_op jit(solution)/shard_map/dot_general | solution.py:50
  25.0 0.6 %fusion.32 = bf16[48,640]{1,0:T(8,128)(2,1)S(1)} fusion(f32[48,640]{1,0:T(8,128)S(1)} %fusion.13, bf16[48,1280]{1,0:T(8,128)(2,1)S(1)} %reshape.46, bf16[1,640,1280]{2,1,0:T(8,128)(2,1)S(1)} %copy-done.1), kind=kOutput, calls=%fused_computation.49 | convolution fusion | flops 79257600 | bytes 1945600 | tf_op jit(solution)/shard_map/bd,fd->bf/dot_general | solution.py:53
  25.6 0.4 copy-done.2
  26.1 0.6 convolution_convert_fusion.2
  27.1 1.3 %collective-permute-done.1 = bf16[8,6,1280]{2,1,0:T(8,128)(2,1)S(1)} collective-permute-done((bf16[8,6,1280]{2,1,0:T(8,128)(2,1)S(1)}, bf16[8,6,1280]{2,1,0:T(8,128)(2,1)S(1)}, u32[]{:S(2)}, u32[]{:S(2)}) %collective-permute-start.1) | collective-permute-done | bytes 122912 | tf_op jit(solution)/shard_map/ppermute | solution.py:21
  28.3 0.8 %add_convert_fusion = bf16[8,6,1280]{2,1,0:T(8,128)(2,1)} fusion(bf16[8,6,1280]{2,1,0:T(8,128)(2,1)S(1)} %collective-permute-done.1, bf16[16,3,1280]{2,1,0:T(4,128)(2,1)S(1)} %reshape.45, bf16[16,3,1280]{2,1,0:T(4,128)(2,1)S(1)} %reshape.47), kind=kLoop, calls=%fused_computation.37 | loop fusion | flops 430080 | bytes 491520 | tf_op jit(solution)/shard_map/convert_element_type | solution.py:68
  29.1 3.4 %all-to-all-start.1 = ((bf16[8,6,1280]{2,1,0:T(8,128)(2,1)}), bf16[8,6,1280]{2,1,0:T(8,128)(2,1)S(1)}, u32[]{:S(2)}, u32[]{:S(2)}) async-start(bf16[8,6,1280]{2,1,0:T(8,128)(2,1)} %add_convert_fusion), calls=%async_computation.1 | async-start | bytes 327680 | tf_op jit(solution)/shard_map/all_to_all | solution.py:14
  32.5 1.8 %fusion.5 = bf16[1,1280,640]{2,1,0:T(8,128)(2,1)} fusion(bf16[48,1280]{1,0:T(8,128)(2,1)S(1)} %reshape.44, bf16[48,640]{1,0:T(8,128)(2,1)S(1)} %fusion.32), kind=kOutput, calls=%fused_computation.8 | convolution fusion | flops 79462400 | bytes 1822720 | tf_op jit(solution)/shard_map/bd,bf->df/dot_general | solution.py:57
  34.3 1.8 %fusion.6 = bf16[1,640,1280]{2,1,0:T(8,128)(2,1)} fusion(bf16[48,1280]{1,0:T(8,128)(2,1)S(1)} %reshape.46, f32[48,640]{1,0:T(8,128)S(1)} %fusion.13), kind=kOutput, calls=%fused_computation.9 | convolution fusion | flops 79738880 | bytes 1884160 | tf_op jit(solution)/shard_map/bf,bd->fd/dot_general | solution.py:56
  36.1 4.4 %all-to-all-done.1 = bf16[8,6,1280]{2,1,0:T(8,128)(2,1)S(1)} async-done(((bf16[8,6,1280]{2,1,0:T(8,128)(2,1)}), bf16[8,6,1280]{2,1,0:T(8,128)(2,1)S(1)}, u32[]{:S(2)}, u32[]{:S(2)}) %all-to-all-start.1) | async-done | bytes 122912 | tf_op jit(solution)/shard_map/all_to_all | solution.py:14
  40.6 2.2 %fusion.35 = f32[3,2,256]{2,1,0:T(2,128)S(1)} fusion(bf16[3,256,1280]{2,1,0:T(8,128)(2,1)} %param.9, bf16[2,3,1280]{2,1,0:T(4,128)(2,1)S(1)} %get-tuple-element.6), kind=kOutput, calls=%fused_computation.52 | convolution fusion | flops 3932160 | bytes 1987584 | tf_op jit(solution)/shard_map/bmd,sbd->bsm/dot_general | solution.py:72
  42.8 0.6 %fusion.41 = f32[3,2,256]{2,1,0:T(2,128)S(1)} fusion(bf16[3,256,1280]{2,1,0:T(8,128)(2,1)S(1)} %copy-done, bf16[2,3,1280]{2,1,0:T(4,128)(2,1)S(1)} %get-tuple-element.7), kind=kOutput, calls=%fused_computation.57 | convolution fusion | flops 3932160 | bytes 1987584 | tf_op jit(solution)/shard_map/sbd,bmd->bsm/dot_general | solution.py:73
  43.4 0.5 convolution_bitcast_fusion
  44.0 2.8 %fusion.43 = f32[3,256,1280]{2,1,0:T(8,128)} fusion(bf16[2,3,1280]{2,1,0:T(4,128)(2,1)S(1)} %get-tuple-element.7, f32[3,2]{1,0:T(4,128)S(1)} %get-tuple-element.10, f32[3,2,256]{2,1,0:T(2,128)S(1)} %convolution_bitcast_fusion.1), kind=kOutput, calls=%fused_computation.59 | convolution fusion | flops 3937029 | bytes 3953688 | tf_op jit(solution)/shard_map/bsm,sbd->bmd/dot_general | solution.py:85
  46.7 0.7 %broadcast_in_dim.11 = f32[8,2,1280]{2,1,0:T(2,128)} broadcast(f32[2,1280]{1,0:T(2,128)S(1)} %add.26), dimensions={1,2} | broadcast | bytes 92160 | tf_op jit(solution)/shard_map/broadcast_in_dim | solution.py:83
  47.4 3.4 %all-to-all-start.2 = ((f32[8,2,1280]{2,1,0:T(2,128)}), f32[8,2,1280]{2,1,0:T(2,128)S(1)}, u32[]{:S(2)}, u32[]{:S(2)}) async-start(f32[8,2,1280]{2,1,0:T(2,128)} %broadcast_in_dim.11), calls=%async_computation.2 | async-start | bytes 163840 | tf_op jit(solution)/shard_map/all_to_all | solution.py:14
  50.8 4.3 %fusion.4 = bf16[3,256,1280]{2,1,0:T(8,128)(2,1)} fusion(f32[3,256,1280]{2,1,0:T(8,128)} %fusion.43, f32[3,2,256]{2,1,0:T(2,128)S(1)} %fusion.23, f32[3,2,256]{2,1,0:T(2,128)S(1)} %fusion.41, bf16[1280,2]{0,1:T(2,128)(2,1)S(1)} %copy-done.3, f32[3,2,256]{2,1,0:T(2,128)S(1)} %get-tuple-element.11, f32[3,2]{1,0:T(4,128)S(1)} %get-tuple-element.10), kind=kOutput, calls=%fused_computation.5 | convolution fusion | flops 5909253 | bytes 5921816 | tf_op jit(solution)/shard_map/bsm,ds->bmd/dot_general | solution.py:86
  55.0 2.9 %all-to-all-done.2 = f32[8,2,1280]{2,1,0:T(2,128)S(1)} async-done(((f32[8,2,1280]{2,1,0:T(2,128)}), f32[8,2,1280]{2,1,0:T(2,128)S(1)}, u32[]{:S(2)}, u32[]{:S(2)}) %all-to-all-start.2) | async-done | bytes 81952 | tf_op jit(solution)/shard_map/all_to_all | solution.py:14
  57.9 0.6 %reduce_sum.62 = f32[2,1280]{1,0:T(2,128)} reduce(f32[8,2,1280]{2,1,0:T(2,128)S(1)} %all-to-all-done.2, f32[]{:T(128)} %constant.3.clone.1), dimensions={0}, to_apply=%region_7.0 | reduce | flops 17920 | bytes 92164 | tf_op jit(solution)/shard_map/reduce_sum | solution.py:84
  (28 shorter events, 2.1 us)
Async XLA Ops:
  0.6 1.6 %copy-start = (bf16[3,256,1280]{2,1,0:T(8,128)(2,1)S(1)}, bf16[3,256,1280]{2,1,0:T(8,128)(2,1)}, u32[]{:S(2)}) copy-start(bf16[3,256,1280]{2,1,0:T(8,128)(2,1)} %param.5) | copy-start | bytes 5898244
  20.8 1.4 %collective-permute-start = (bf16[8,6,1280]{2,1,0:T(8,128)(2,1)S(1)}, bf16[8,6,1280]{2,1,0:T(8,128)(2,1)S(1)}, u32[]{:S(2)}, u32[]{:S(2)}) collective-permute-start(bf16[8,6,1280]{2,1,0:T(8,128)(2,1)S(1)} %all_to_all.15), channel_id=1, source_target_pairs={{0,1},{1,0},{2,3},{3,2},{4,5},{5,4},{6,7},{7,6},{8,9},{9,8},{10,11... | collective-permute-start | bytes 368648 | tf_op jit(solution)/shard_map/ppermute | solution.py:21
  22.6 2.0 %copy-start.1 = (bf16[1,640,1280]{2,1,0:T(8,128)(2,1)S(1)}, bf16[1,640,1280]{2,1,0:T(8,128)(2,1)}, u32[]{:S(2)}) copy-start(bf16[1,640,1280]{2,1,0:T(8,128)(2,1)} %param.8) | copy-start | bytes 4915204
  24.6 1.4 %copy-start.2 = (bf16[1,1280,640]{2,1,0:T(8,128)(2,1)S(1)}, bf16[1,1280,640]{2,1,0:T(8,128)(2,1)}, u32[]{:S(2)}) copy-start(bf16[1,1280,640]{2,1,0:T(8,128)(2,1)} %param.7) | copy-start | bytes 4915204
  26.9 1.5 %collective-permute-start.1 = (bf16[8,6,1280]{2,1,0:T(8,128)(2,1)S(1)}, bf16[8,6,1280]{2,1,0:T(8,128)(2,1)S(1)}, u32[]{:S(2)}, u32[]{:S(2)}) collective-permute-start(bf16[8,6,1280]{2,1,0:T(8,128)(2,1)S(1)} %pad_maximum_fusion.1), channel_id=1, source_target_pairs={{0,1},{1,0},{2,3},{3,2},{4,5},{5,4},{6,7},{7,6},{8,9},{9,8},{10,11... | collective-permute-start | bytes 368648 | tf_op jit(solution)/shard_map/ppermute | solution.py:21
  29.1 11.4 %all-to-all-start.1 = ((bf16[8,6,1280]{2,1,0:T(8,128)(2,1)}), bf16[8,6,1280]{2,1,0:T(8,128)(2,1)S(1)}, u32[]{:S(2)}, u32[]{:S(2)}) async-start(bf16[8,6,1280]{2,1,0:T(8,128)(2,1)} %add_convert_fusion), calls=%async_computation.1 | async-start | bytes 327680 | tf_op jit(solution)/shard_map/all_to_all | solution.py:14
  43.9 6.8 %copy-start.3 = (bf16[1280,2]{0,1:T(2,128)(2,1)S(1)}, bf16[1280,2]{0,1:T(2,128)(2,1)}, u32[]{:S(2)}) copy-start(bf16[1280,2]{0,1:T(2,128)(2,1)} %param.6) | copy-start | bytes 15364
  43.9 2.8 %collective-permute-start.2 = (f32[2,1280]{1,0:T(2,128)S(1)}, f32[2,1280]{1,0:T(2,128)S(1)}, u32[]{:S(2)}, u32[]{:S(2)}) collective-permute-start(f32[2,1280]{1,0:T(2,128)S(1)} %convolution_bitcast_fusion), channel_id=1, source_target_pairs={{0,1},{1,0},{2,3},{3,2},{4,5},{5,4},{6,7},{7,6},{8,9},{9,8},{10,11... | collective-permute-start | bytes 30728 | tf_op jit(solution)/shard_map/ppermute | solution.py:21
  47.4 10.5 %all-to-all-start.2 = ((f32[8,2,1280]{2,1,0:T(2,128)}), f32[8,2,1280]{2,1,0:T(2,128)S(1)}, u32[]{:S(2)}, u32[]{:S(2)}) async-start(f32[8,2,1280]{2,1,0:T(2,128)} %broadcast_in_dim.11), calls=%async_computation.2 | async-start | bytes 163840 | tf_op jit(solution)/shard_map/all_to_all | solution.py:14

commit v4 on v3

v4 whole, which is shorter than its diff:
```python
import functools

import jax
import jax.numpy as jnp
from jax import lax
from jax.experimental import pallas as pl
from jax.experimental.pallas import tpu as pltpu
from jax.sharding import PartitionSpec as P

F32 = jnp.float32
BF16 = jnp.bfloat16
NT = (((1,), (1,)), ((), ()))
TN = (((0,), (0,)), ((), ()))
NN = (((1,), (0,)), ((), ()))

VMEM = pl.BlockSpec(memory_space=pltpu.VMEM)
HBM = pl.BlockSpec(memory_space=pltpu.HBM)
VMEM_LIMIT = 40 * 1024 * 1024


def dot(left, right, dims=NN):
    return lax.dot_general(left, right, dims, preferred_element_type=F32)


def in_vmem(array):
    return pltpu.with_memory_space_constraint(array, pltpu.VMEM)


def in_hbm(array):
    return pltpu.with_memory_space_constraint(array, pltpu.HBM)


def vmem_out(shape, dtype):
    return pltpu.VMEM(shape, dtype)


def call(kernel, outs, ins, out_specs, in_specs, scratch=(), cost=None):
    return pl.pallas_call(
        kernel,
        out_shape=outs,
        in_specs=in_specs,
        out_specs=out_specs,
        scratch_shapes=list(scratch),
        compiler_params=pltpu.CompilerParams(vmem_limit_bytes=VMEM_LIMIT),
        cost_estimate=pl.CostEstimate(flops=cost[0], bytes_accessed=cost[1], transcendentals=0),
    )(*ins)


def block_rows(images):
    return -(-2 * images // 8) * 8


def rows_kernel(
    split_chips, tokens, router_t, d_out, send, tok, dout, disp_out, comb_out, block, sems
):
    images = tok.shape[0]
    slots = router_t.shape[0]
    fetch_tok = [
        pltpu.make_async_copy(tokens.at[b], tok.at[b], sems.at[b]) for b in range(images)
    ]
    fetch_dout = [
        pltpu.make_async_copy(d_out.at[b], dout.at[b], sems.at[images + b]) for b in range(images)
    ]
    for copy in fetch_tok + fetch_dout:
        copy.start()
    block[...] = jnp.zeros_like(block)
    combs = []
    for b in range(images):
        fetch_tok[b].wait()
        logits = dot(router_t[...], tok[b], NT)
        exps = jnp.exp(logits - jnp.max(logits, axis=1, keepdims=True))
        disp = exps / jnp.sum(exps, axis=1, keepdims=True)
        exps = jnp.exp(logits - jnp.max(logits, axis=0, keepdims=True))
        comb = exps / jnp.sum(exps, axis=0, keepdims=True)
        disp_out[b] = disp
        comb_out[b] = comb
        combs.append(comb.astype(BF16))
        block[:, b, :] = dot(disp.astype(BF16), tok[b])
    for b in range(images):
        fetch_dout[b].wait()
        block[:, images + b, :] = dot(combs[b], dout[b])
    for slot in range(slots):
        rows = block[slot].astype(BF16)
        for chip in range(split_chips):
            send[slot * split_chips + chip] = rows


def experts_kernel(images, near, far, w_in, w_out, own, other, hid_out, grad_out):
    chips, rows, width = near.shape
    half = chips * rows
    x = jnp.concatenate([near[...].reshape(half, width), far[...].reshape(half, width)], axis=0)
    pre = dot(x, w_in[...])
    grad_hidden = dot(x, w_out[...], NT)
    place = lax.broadcasted_iota(jnp.int32, pre.shape, 0) % rows
    slot_row = place < images
    grad_hidden = pltpu.roll(grad_hidden, 2 * half - images, 0)
    scale = 0.7978845608028654
    square = pre * pre
    tanh = jnp.tanh(scale * pre * (1.0 + 0.044715 * square))
    cdf = 0.5 * (1.0 + tanh)
    slope = cdf + (0.5 * scale) * pre * (1.0 - tanh * tanh) * (1.0 + (3 * 0.044715) * square)
    hidden = jnp.where(slot_row, pre * cdf, 0.0)
    grad_pre = jnp.where(slot_row, slope * grad_hidden, 0.0)
    grad_low = pltpu.roll(grad_pre, images, 0).astype(BF16)
    shares = dot(hidden.astype(BF16), w_out[...]) + dot(grad_low, w_in[...], NT)
    own[...] = shares[:half].reshape(own.shape)
    other[...] = shares[half:].astype(BF16).reshape(other.shape)
    hid_out[...] = pltpu.roll(hidden, images, 0).astype(BF16)
    grad_out[...] = grad_pre.astype(BF16)


def add_kernel(own, received, total):
    total[...] = (own[...] + received[...].astype(F32)).astype(BF16)


def weights_kernel(near, far, hid, grad, g_in, g_out, buf_in, buf_out, sem_in, sem_out):
    chips, rows, width = near.shape
    half = chips * rows
    parts = buf_in.shape[0]
    step_in = g_in.shape[0] // parts
    step_out = g_out.shape[0] // parts
    x = jnp.concatenate([near[...].reshape(half, width), far[...].reshape(half, width)], axis=0)
    copies = []
    for i in range(parts):
        buf_out[i] = dot(hid[:, i * step_out : (i + 1) * step_out], x, TN).astype(BF16)
        copy = pltpu.make_async_copy(
            buf_out.at[i], g_out.at[pl.ds(i * step_out, step_out)], sem_out.at[i]
        )
        copy.start()
        copies.append(copy)
        buf_in[i] = dot(x[:, i * step_in : (i + 1) * step_in], grad[...], TN).astype(BF16)
        copy = pltpu.make_async_copy(
            buf_in.at[i], g_in.at[pl.ds(i * step_in, step_in)], sem_in.at[i]
        )
        copy.start()
        copies.append(copy)
    for copy in copies:
        copy.wait()


def logits_kernel(split_chips, shares, tok, dout, disp, comb, router_t, terms_out, left, right):
    images, slots, _ = disp.shape
    rows = shares.shape[1]
    summed = []
    for slot in range(slots):
        total = shares[slot * split_chips].astype(F32)
        for chip in range(1, split_chips):
            total = total + shares[slot * split_chips + chip].astype(F32)
        summed.append(total)
    stacked = jnp.concatenate(summed, axis=0).astype(BF16)
    terms = None
    for b in range(images):
        by_dout = dot(stacked, dout[b], NT)
        by_tok = dot(stacked, tok[b], NT)
        grad_comb = jnp.concatenate(
            [by_dout[s * rows + b : s * rows + b + 1] for s in range(slots)], axis=0
        )
        grad_disp = jnp.concatenate(
            [by_tok[s * rows + images + b : s * rows + images + b + 1] for s in range(slots)],
            axis=0,
        )
        dispatch = disp[b]
        combine = comb[b]
        grad_logits = dispatch * (
            grad_disp - jnp.sum(dispatch * grad_disp, axis=1, keepdims=True)
        ) + combine * (grad_comb - jnp.sum(combine * grad_comb, axis=0, keepdims=True))
        term = dot(grad_logits.astype(BF16), tok[b])
        terms = term if terms is None else terms + term
        left[b] = jnp.concatenate([dispatch, grad_logits], axis=0)
        right[b] = jnp.concatenate(
            [summed[s][images + b : images + b + 1] for s in range(slots)]
            + [router_t[...].astype(F32)],
            axis=0,
        )
    terms_out[...] = jnp.broadcast_to(terms.astype(BF16)[None], terms_out.shape)


def tokens_kernel(left, right, grad_tokens, buf, sems):
    images, parts = buf.shape[:2]
    step = buf.shape[2]
    copies = []
    for b in range(images):
        rhs = right[b].astype(BF16)
        for i in range(parts):
            lhs = left[b, :, i * step : (i + 1) * step].astype(BF16)
            buf[b, i] = dot(lhs, rhs, TN).astype(BF16)
            copy = pltpu.make_async_copy(
                buf.at[b, i], grad_tokens.at[b, pl.ds(i * step, step)], sems.at[b, i]
            )
            copy.start()
            copies.append(copy)
    for copy in copies:
        copy.wait()


def swap_chips(blocks):
    count = lax.axis_size("expert")
    groups = [list(range(core, count, 2)) for core in range(2)]
    return lax.all_to_all(
        blocks, "expert", split_axis=0, concat_axis=0, axis_index_groups=groups, tiled=True
    )


def swap_cores(block):
    count = lax.axis_size("expert")
    return lax.ppermute(block, "expert", [(device, device ^ 1) for device in range(count)])


def per_device(tokens, router, w_in, w_out, d_out):
    devices = lax.axis_size("expert")
    chips = devices // 2
    slots = router.shape[1]
    split_chips = chips // slots
    images, count, width = tokens.shape
    hidden_units = w_in.shape[2]
    rows = block_rows(images)
    router_t = router.T
    big = images * count * width

    send, tok, dout, disp, comb = call(
        functools.partial(rows_kernel, split_chips),
        (
            vmem_out((chips, rows, width), BF16),
            vmem_out((images, count, width), BF16),
            vmem_out((images, count, width), BF16),
            vmem_out((images, slots, count), F32),
            vmem_out((images, slots, count), F32),
        ),
        (in_hbm(tokens), router_t, in_hbm(d_out)),
        (VMEM,) * 5,
        (HBM, VMEM, HBM),
        [pltpu.VMEM((slots, rows, width), F32), pltpu.SemaphoreType.DMA((2 * images,))],
        (6 * slots * big, 4 * big),
    )
    near = swap_chips(send)
    far = swap_cores(near)
    near, far = in_vmem(near), in_vmem(far)
    half = chips * rows
    own, other, hid, grad = call(
        functools.partial(experts_kernel, images),
        (
            vmem_out((chips, rows, width), F32),
            vmem_out((chips, rows, width), BF16),
            vmem_out((2 * half, hidden_units), BF16),
            vmem_out((2 * half, hidden_units), BF16),
        ),
        (near, far, in_vmem(w_in[0]), in_vmem(w_out[0])),
        (VMEM,) * 4,
        (VMEM,) * 4,
        (),
        (8 * 2 * half * width * hidden_units, 4 * width * hidden_units),
    )
    total = call(
        add_kernel,
        vmem_out((chips, rows, width), BF16),
        (in_vmem(own), in_vmem(swap_cores(other))),
        VMEM,
        (VMEM,) * 2,
        (),
        (half * width, 8 * half * width),
    )
    shares = swap_chips(total)
    parts = 5
    g_in, g_out = call(
        weights_kernel,
        (
            jax.ShapeDtypeStruct((width, hidden_units), BF16),
            jax.ShapeDtypeStruct((hidden_units, width), BF16),
        ),
        (near, far, in_vmem(hid), in_vmem(grad)),
        (HBM,) * 2,
        (VMEM,) * 4,
        [
            pltpu.VMEM((parts, width // parts, hidden_units), BF16),
            pltpu.VMEM((parts, hidden_units // parts, width), BF16),
            pltpu.SemaphoreType.DMA((parts,)),
            pltpu.SemaphoreType.DMA((parts,)),
        ],
        (8 * half * width * hidden_units, 4 * width * hidden_units),
    )
    terms, left, right = call(
        functools.partial(logits_kernel, split_chips),
        (
            vmem_out((devices, slots, width), BF16),
            vmem_out((images, 2 * slots, count), F32),
            vmem_out((images, 2 * slots, width), F32),
        ),
        (
            in_vmem(shares),
            in_vmem(tok),
            in_vmem(dout),
            in_vmem(disp),
            in_vmem(comb),
            router_t,
        ),
        (VMEM,) * 3,
        (VMEM,) * 6,
        (),
        (6 * slots * big, 4 * big),
    )
    terms = lax.all_to_all(terms, "expert", split_axis=0, concat_axis=0, tiled=True)
    pieces = 2
    grad_tokens = call(
        tokens_kernel,
        jax.ShapeDtypeStruct(tokens.shape, BF16),
        (in_vmem(left), in_vmem(right)),
        HBM,
        (VMEM,) * 2,
        [
            pltpu.VMEM((images, pieces, count // pieces, width), BF16),
            pltpu.SemaphoreType.DMA((images, pieces)),
        ],
        (4 * slots * big, 2 * big),
    )
    grad_router = jnp.sum(terms.astype(F32), axis=0).T
    return (grad_tokens, g_in[None], g_out[None], grad_router)


def solution(mesh):
    in_specs = (
        P(("groups", "expert"), None, None),
        P(None, "groups"),
        P(("groups", "expert"), None, None),
        P(("groups", "expert"), None, None),
        P(("groups", "expert"), None, None),
    )
    out_specs = (
        P(("groups", "expert"), None, None),
        P(("groups", "expert"), None, None),
        P(("groups", "expert"), None, None),
        P(None, "groups"),
    )
    return jax.shard_map(
        per_device, mesh=mesh, in_specs=in_specs, out_specs=out_specs, check_vma=False
    )
```

time: 59.1 us -> 50.1 us (0.85)
  matrix products: 21.1 us -> 0 us
  Pallas kernels: 0 us -> 12.8 us
  blocking collectives: 14.6 us -> 25.1 us
  waiting for transfers between devices: 9.93 us -> 6.06 us
  starting transfers between devices: 6.95 us -> 3.71 us
  local copies, waits for them, and re-layouts: 3.18 us -> 0.7 us
  other arithmetic: 1.95 us -> 0.68 us
    dot_general x14 -> x0, matrix products: 21.1 us -> none  [the longest x1 4.25 us: per_device(): jnp.einsum('bsm,ds->bmd', gl_b, router, preferred_element_type=f32)]
    pallas_call x0 -> x6, Pallas kernels: none -> 12.8 us  [call(): pl.pallas_call(kernel, out_shape=outs, in_specs=in_specs, out_specs=out_s...]
    all_to_all x1 -> x2, blocking collectives: 14.6 us -> 25.1 us  [swap_chips(): lax.all_to_all(blocks, 'expert', split_axis=0, concat_axis=0, axis_index_...]
    all_to_all x2 -> x1, waiting for transfers between devices: 7.29 us -> 3.41 us  [per_device(): lax.all_to_all(terms, 'expert', split_axis=0, concat_axis=0, tiled=True)]
    all_to_all x2 -> x1, starting transfers between devices: 6.74 us -> 3.5 us  [per_device(): lax.all_to_all(terms, 'expert', split_axis=0, concat_axis=0, tiled=True)]
    unnamed x8, local copies, waits for them, and re-layouts: 2 us -> 0.7 us
    convert_element_type x1 -> x0, other arithmetic: 0.77 us -> none  [per_device(): shares.astype(bf16)]
    broadcast_in_dim x2 -> x0, local copies, waits for them, and re-layouts: 0.67 us -> none  [the longest x1 0.65 us: per_device(): terms = exchange(jnp.broadcast_to(terms[None], (chips, slots, width)))]
  transfers between devices with their start and end apart: 5 -> 3, of which waited for: 4 -> 3; matrix products, arithmetic and copies ran while one was open for 18% -> 0% of each run, Pallas kernels for 0% -> 7%
where the time goes in v4:
time: 50.1 us; the launch traced here: 49.8 us
  blocking collectives  25.1 us (50%)
  Pallas kernels  12.8 us (26%)
  waiting for transfers between devices  6.06 us (12%)
  starting transfers between devices  3.71 us (7%)
  local copies, waits for them, and re-layouts  0.7 us (1%)
  between operations  0.69 us (1%)
  other arithmetic  0.68 us (1%)
    all_to_all x2, blocking collectives, swap_chips(): lax.all_to_all(blocks, 'expert', split_axis=0, concat_axis=0, axis_index_...  25.1 us
    pallas_call x6, Pallas kernels, call(): pl.pallas_call(kernel, out_shape=outs, in_specs=in_specs, out_specs=out_s...  12.8 us
    all_to_all x1, starting transfers between devices, per_device(): lax.all_to_all(terms, 'expert', split_axis=0, concat_axis=0, tiled=True)  3.5 us
    all_to_all x1, waiting for transfers between devices, per_device(): lax.all_to_all(terms, 'expert', split_axis=0, concat_axis=0, tiled=True)  3.41 us
    ppermute x2, waiting for transfers between devices, swap_cores(): lax.ppermute(block, 'expert', [(device, device ^ 1) for device in range(c...  2.65 us
  transfers between devices with their start and end apart: 3, of which 3 were waited for; matrix products, arithmetic and copies ran while one was open for 0% of the time, Pallas kernels for 7%

profile of v4, /device:TPU:0, one launch (start us, length us, event | category | flops | bytes accessed | tf_op | source)
XLA Modules:
  0.0 49.8 jit_solution(1724879056441156744)
XLA Ops:
  0.6 0.0 copy-start.2
  0.6 0.7 %copy-done.2 = bf16[1280,2]{0,1:T(2,128)(2,1)S(1)} copy-done((bf16[1280,2]{0,1:T(2,128)(2,1)S(1)}, bf16[1280,2]{0,1:T(2,128)(2,1)}, u32[]{:S(2)}) %copy-start.2) | copy-done | bytes 5144
  1.3 0.0 copy-start
  1.3 0.0 copy-start.1
  1.3 4.7 %shard_map.84 = (bf16[8,8,1280]{2,1,0:T(8,128)(2,1)S(1)}, bf16[3,256,1280]{2,1,0:T(8,128)(2,1)S(1)}, bf16[3,256,1280]{2,1,0:T(8,128)(2,1)S(1)}, f32[3,2,256]{2,1,0:T(2,128)S(1)}, f32[3,2,256]{2,1,0:T(2,128)S(1)}) custom-call(bf16[3,256,1280]{2,1,0:T(8,128)(2,1)} %tokens.1, bf16[2,1280]{1,0:T(2,128)(2,1)S(1)} %bitcast.8, bf16[3,256,1280]{2,1,0:T(8,128)(2,1)} %d_out.1), custom_call_target="tpu_custom_call" | custom-call | flops 11796480 | bytes 3932160 | tf_op jit(solution)/shard_map/pallas_call | solution.py:38
  6.0 14.6 %all_to_all.15.near = bf16[8,8,1280]{2,1,0:T(8,128)(2,1)S(1)} all-to-all(bf16[8,8,1280]{2,1,0:T(8,128)(2,1)S(1)} %get-tuple-element.18), channel_id=1, replica_groups={{0,2,4,6,8,10,12,14},{1,3,5,7,9,11,13,15},{16,18,20,22,24,26,28,30},{17..., dimensions={0} | all-to-all | bytes 327680 | tf_op jit(solution)/shard_map/all_to_all | solution.py:199
  20.6 0.0 collective-permute-start
  20.6 1.4 %collective-permute-done.far = bf16[8,8,1280]{2,1,0:T(8,128)(2,1)S(1)} collective-permute-done((bf16[8,8,1280]{2,1,0:T(8,128)(2,1)S(1)}, bf16[8,8,1280]{2,1,0:T(8,128)(2,1)S(1)}, u32[]{:S(2)}, u32[]{:S(2)}) %collective-permute-start) | collective-permute-done | bytes 163872 | tf_op jit(solution)/shard_map/ppermute | solution.py:206
  22.0 0.0 copy-done
  22.0 0.0 copy-done.1
  22.0 0.0 copy-start.3
  22.0 2.0 %shard_map.85 = (f32[8,8,1280]{2,1,0:T(8,128)S(1)}, bf16[8,8,1280]{2,1,0:T(8,128)(2,1)S(1)}, bf16[128,640]{1,0:T(8,128)(2,1)S(1)}, bf16[128,640]{1,0:T(8,128)(2,1)S(1)}) custom-call(bf16[8,8,1280]{2,1,0:T(8,128)(2,1)S(1)} %all_to_all.15.near, bf16[8,8,1280]{2,1,0:T(8,128)(2,1)S(1)} %collective-permute-done.far, bf16[1280,640]{1,0:T(8,128)(2,1)S(1)} %bitcast.6, ...), custom_call_target="tpu_custom_call" | custom-call | flops 838860800 | bytes 3276800 | tf_op jit(solution)/shard_map/pallas_call | solution.py:38
  24.0 0.2 collective-permute-start.1
  24.2 1.3 %collective-permute-done.1.received = bf16[8,8,1280]{2,1,0:T(8,128)(2,1)S(1)} collective-permute-done((bf16[8,8,1280]{2,1,0:T(8,128)(2,1)S(1)}, bf16[8,8,1280]{2,1,0:T(8,128)(2,1)S(1)}, u32[]{:S(2)}, u32[]{:S(2)}) %collective-permute-start.1) | collective-permute-done | bytes 163872 | tf_op jit(solution)/shard_map/ppermute | solution.py:206
  25.5 10.5 %all_to_all.16.shares = bf16[8,8,1280]{2,1,0:T(8,128)(2,1)S(1)} all-to-all(bf16[8,8,1280]{2,1,0:T(8,128)(2,1)S(1)} %shard_map.86), channel_id=1, replica_groups={{0,2,4,6,8,10,12,14},{1,3,5,7,9,11,13,15},{16,18,20,22,24,26,28,30},{17..., dimensions={0} | all-to-all | bytes 327680 | tf_op jit(solution)/shard_map/all_to_all | solution.py:199
  36.0 0.0 copy-done.3
  36.0 2.5 %shard_map.87 = (bf16[16,2,1280]{2,1,0:T(2,128)(2,1)}, f32[3,4,256]{2,1,0:T(4,128)S(1)}, f32[3,4,1280]{2,1,0:T(4,128)S(1)}) custom-call(bf16[8,8,1280]{2,1,0:T(8,128)(2,1)S(1)} %all_to_all.16.shares, bf16[3,256,1280]{2,1,0:T(8,128)(2,1)S(1)} %get-tuple-element.21.tok, bf16[3,256,1280]{2,1,0:T(8,128)(2,1)S(1)} %get-tuple-element.22.dout, ...), custom_call_target="tpu_custom_call" | custom-call | flops 11796480 | bytes 3932160 | tf_op jit(solution)/shard_map/pallas_call | solution.py:38
  38.5 3.5 %all-to-all-start.2 = ((bf16[16,2,1280]{2,1,0:T(2,128)(2,1)}), bf16[16,2,1280]{2,1,0:T(2,128)(2,1)S(1)}, u32[]{:S(2)}, u32[]{:S(2)}) async-start(bf16[16,2,1280]{2,1,0:T(2,128)(2,1)} %get-tuple-element.31), calls=%async_computation.2 | async-start | bytes 163840 | tf_op jit(solution)/shard_map/all_to_all | solution.py:301
  42.0 2.1 %shard_map.89 = (bf16[1280,640]{1,0:T(8,128)(2,1)}, bf16[640,1280]{1,0:T(8,128)(2,1)}) custom-call(bf16[8,8,1280]{2,1,0:T(8,128)(2,1)S(1)} %all_to_all.15.near, bf16[8,8,1280]{2,1,0:T(8,128)(2,1)S(1)} %collective-permute-done.far, bf16[128,640]{1,0:T(8,128)(2,1)S(1)} %get-tuple-element.27.hid, bf16[128,640]{1,0:T(8,128)(2,1)S(1)} %get-tuple-element.28.grad), custom_call_target="tpu_custom_call" | custom-call | flops 419430400 | bytes 3276800 | tf_op jit(solution)/shard_map/pallas_call | solution.py:38
  44.1 1.6 %shard_map.88 = bf16[3,256,1280]{2,1,0:T(8,128)(2,1)} custom-call(f32[3,4,256]{2,1,0:T(4,128)S(1)} %get-tuple-element.25.left, f32[3,4,1280]{2,1,0:T(4,128)S(1)} %get-tuple-element.26.right), custom_call_target="tpu_custom_call" | custom-call | flops 7864320 | bytes 1966080 | tf_op jit(solution)/shard_map/pallas_call | solution.py:38
  45.7 3.4 %all-to-all-done.2 = bf16[16,2,1280]{2,1,0:T(2,128)(2,1)S(1)} async-done(((bf16[16,2,1280]{2,1,0:T(2,128)(2,1)}), bf16[16,2,1280]{2,1,0:T(2,128)(2,1)S(1)}, u32[]{:S(2)}, u32[]{:S(2)}) %all-to-all-start.2) | async-done | bytes 81952 | tf_op jit(solution)/shard_map/all_to_all | solution.py:301
  49.1 0.7 %convert_reduce_fusion = f32[2,1280]{1,0:T(2,128)} fusion(bf16[16,2,1280]{2,1,0:T(2,128)(2,1)S(1)} %all-to-all-done.2), kind=kLoop, calls=%fused_computation | loop fusion | flops 79360 | bytes 92160 | tf_op jit(solution)/shard_map/reduce_sum | solution.py:315
  (1 shorter events, 0.0 us)
Async XLA Ops:
  0.6 0.7 %copy-start.2 = (bf16[1280,2]{0,1:T(2,128)(2,1)S(1)}, bf16[1280,2]{0,1:T(2,128)(2,1)}, u32[]{:S(2)}) copy-start(bf16[1280,2]{0,1:T(2,128)(2,1)} %param.6) | copy-start | bytes 15364
  1.3 20.7 %copy-start = (bf16[1,1280,640]{2,1,0:T(8,128)(2,1)S(1)}, bf16[1,1280,640]{2,1,0:T(8,128)(2,1)}, u32[]{:S(2)}) copy-start(bf16[1,1280,640]{2,1,0:T(8,128)(2,1)} %param.7) | copy-start | bytes 4915204
  1.3 20.7 %copy-start.1 = (bf16[1,640,1280]{2,1,0:T(8,128)(2,1)S(1)}, bf16[1,640,1280]{2,1,0:T(8,128)(2,1)}, u32[]{:S(2)}) copy-start(bf16[1,640,1280]{2,1,0:T(8,128)(2,1)} %param.8) | copy-start | bytes 4915204
  20.6 1.4 %collective-permute-start = (bf16[8,8,1280]{2,1,0:T(8,128)(2,1)S(1)}, bf16[8,8,1280]{2,1,0:T(8,128)(2,1)S(1)}, u32[]{:S(2)}, u32[]{:S(2)}) collective-permute-start(bf16[8,8,1280]{2,1,0:T(8,128)(2,1)S(1)} %all_to_all.15.near), channel_id=1, source_target_pairs={{0,1},{1,0},{2,3},{3,2},{4,5},{5,4},{6,7},{7,6},{8,9},{9,8},{10,11... | collective-permute-start | bytes 491528 | tf_op jit(solution)/shard_map/ppermute | solution.py:206
  22.0 13.9 %copy-start.3 = (bf16[1280,2]{0,1:T(2,128)(2,1)S(1)}, bf16[1280,2]{0,1:T(2,128)(2,1)}, u32[]{:S(2)}) copy-start(bf16[1280,2]{0,1:T(2,128)(2,1)} %param.6) | copy-start | bytes 15364
  24.0 1.5 %collective-permute-start.1 = (bf16[8,8,1280]{2,1,0:T(8,128)(2,1)S(1)}, bf16[8,8,1280]{2,1,0:T(8,128)(2,1)S(1)}, u32[]{:S(2)}, u32[]{:S(2)}) collective-permute-start(bf16[8,8,1280]{2,1,0:T(8,128)(2,1)S(1)} %get-tuple-element.20), channel_id=1, source_target_pairs={{0,1},{1,0},{2,3},{3,2},{4,5},{5,4},{6,7},{7,6},{8,9},{9,8},{10,11... | collective-permute-start | bytes 491528 | tf_op jit(solution)/shard_map/ppermute | solution.py:206
  38.5 10.6 %all-to-all-start.2 = ((bf16[16,2,1280]{2,1,0:T(2,128)(2,1)}), bf16[16,2,1280]{2,1,0:T(2,128)(2,1)S(1)}, u32[]{:S(2)}, u32[]{:S(2)}) async-start(bf16[16,2,1280]{2,1,0:T(2,128)(2,1)} %get-tuple-element.31), calls=%async_computation.2 | async-start | bytes 163840 | tf_op jit(solution)/shard_map/all_to_all | solution.py:301

commit v5 on v4

v5 whole, which is shorter than its diff:
```python
import functools

import jax
import jax.numpy as jnp
from jax import lax
from jax.experimental import pallas as pl
from jax.experimental.pallas import tpu as pltpu
from jax.sharding import PartitionSpec as P

F32 = jnp.float32
BF16 = jnp.bfloat16
NT = (((1,), (1,)), ((), ()))
TN = (((0,), (0,)), ((), ()))
NN = (((1,), (0,)), ((), ()))

VMEM = pl.BlockSpec(memory_space=pltpu.VMEM)
HBM = pl.BlockSpec(memory_space=pltpu.HBM)
VMEM_LIMIT = 40 * 1024 * 1024


def dot(left, right, dims=NN):
    return lax.dot_general(left, right, dims, preferred_element_type=F32)


def in_vmem(array):
    return pltpu.with_memory_space_constraint(array, pltpu.VMEM)


def in_hbm(array):
    return pltpu.with_memory_space_constraint(array, pltpu.HBM)


def vmem_out(shape, dtype):
    return pltpu.VMEM(shape, dtype)


def call(kernel, outs, ins, out_specs, in_specs, scratch=(), cost=None):
    return pl.pallas_call(
        kernel,
        out_shape=outs,
        in_specs=in_specs,
        out_specs=out_specs,
        scratch_shapes=list(scratch),
        compiler_params=pltpu.CompilerParams(vmem_limit_bytes=VMEM_LIMIT),
        cost_estimate=pl.CostEstimate(flops=cost[0], bytes_accessed=cost[1], transcendentals=0),
    )(*ins)


def block_shape(images, width):
    extra = width // 5
    main = width - extra
    ends = -(-2 * images * extra // main)
    return -(-(2 * images + ends) // 8) * 8, main, extra


def end_place(images, main, extra, row):
    per = main // extra
    return 2 * images + row // per, row % per * extra


def pack(images, scratch, values):
    main = scratch.shape[2]
    extra = values.shape[2] - main
    scratch[...] = values[:, :, :main]
    for row in range(2 * images):
        to, column = end_place(images, main, extra, row)
        scratch[:, to, column : column + extra] = values[:, row, main:]


def unpack(images, scratch, values):
    main = values.shape[2]
    extra = scratch.shape[2]
    scratch[...] = jnp.zeros_like(scratch)
    for row in range(2 * images):
        at, column = end_place(images, main, extra, row)
        scratch[:, row, :] = values[:, at, column : column + extra]


def rows_kernel(
    split_chips,
    tokens,
    router_hbm,
    d_out,
    send,
    tok,
    dout,
    disp_out,
    comb_out,
    router_t,
    block,
    sems,
    router_sem,
):
    images = tok.shape[0]
    slots = router_t.shape[0]
    main = send.shape[2]
    extra = tok.shape[2] - main
    fetch_router = pltpu.make_async_copy(router_hbm, router_t, router_sem)
    fetch_router.start()
    fetch_tok = [
        pltpu.make_async_copy(tokens.at[b], tok.at[b], sems.at[b]) for b in range(images)
    ]
    fetch_dout = [
        pltpu.make_async_copy(d_out.at[b], dout.at[b], sems.at[images + b]) for b in range(images)
    ]
    for copy in fetch_tok + fetch_dout:
        copy.start()
    block[...] = jnp.zeros_like(block)

    def put(row, values):
        to, column = end_place(images, main, extra, row)
        block[:, row, :] = values[:, :main]
        block[:, to, column : column + extra] = values[:, main:]

    fetch_router.wait()
    logits = []
    for b in range(images):
        fetch_tok[b].wait()
        logits.append(dot(router_t[...], tok[b], NT))
    disps = []
    combs = []
    for b in range(images):
        exps = jnp.exp(logits[b] - jnp.max(logits[b], axis=1, keepdims=True))
        disps.append(exps / jnp.sum(exps, axis=1, keepdims=True))
        exps = jnp.exp(logits[b] - jnp.max(logits[b], axis=0, keepdims=True))
        combs.append(exps / jnp.sum(exps, axis=0, keepdims=True))
        disp_out[b] = disps[b]
        comb_out[b] = combs[b]
    for b in range(images):
        put(b, dot(disps[b].astype(BF16), tok[b]))
    for b in range(images):
        fetch_dout[b].wait()
        put(images + b, dot(combs[b].astype(BF16), dout[b]))
    for slot in range(slots):
        rows = block[slot].astype(BF16)
        for chip in range(split_chips):
            send[slot * split_chips + chip] = rows


def experts_kernel(images, near, far, w_in, w_out, other, x_out, hid_out, grad_out, ends, packed):
    chips, rows, main = near.shape
    half = chips * rows
    width = x_out.shape[1]
    for i, blocks in enumerate((near, far)):
        unpack(images, ends.at[pl.ds(i * chips, chips)], blocks[...].astype(F32))
    x = jnp.concatenate(
        [
            jnp.concatenate(
                [near[...].reshape(half, main), far[...].reshape(half, main)], axis=0
            ),
            ends[...].reshape(2 * half, width - main).astype(BF16),
        ],
        axis=1,
    )
    x_out[...] = x
    pre = dot(x, w_in[...])
    grad_hidden = dot(x, w_out[...], NT)
    place = lax.broadcasted_iota(jnp.int32, pre.shape, 0) % rows
    slot_row = place < images
    grad_hidden = pltpu.roll(grad_hidden, 2 * half - images, 0)
    scale = 0.7978845608028654
    square = pre * pre
    tanh = jnp.tanh(scale * pre * (1.0 + 0.044715 * square))
    cdf = 0.5 * (1.0 + tanh)
    slope = cdf + (0.5 * scale) * pre * (1.0 - tanh * tanh) * (1.0 + (3 * 0.044715) * square)
    hidden = jnp.where(slot_row, pre * cdf, 0.0).astype(BF16)
    grad_pre = jnp.where(slot_row, slope * grad_hidden, 0.0)
    grad_low = pltpu.roll(grad_pre, images, 0).astype(BF16)
    hid_out[...] = hidden
    grad_out[...] = grad_low
    shares = dot(hidden[half:], w_out[...]) + dot(grad_low[half:], w_in[...], NT)
    pack(images, packed, shares.reshape(chips, rows, width))
    other[...] = packed[...].astype(BF16)


def own_kernel(images, hid, grad, w_in, w_out, own):
    chips, rows, _ = own.shape
    half = chips * rows
    shares = dot(hid[:half], w_out[...]) + dot(grad[:half], w_in[...], NT)
    pack(images, own, shares.reshape(chips, rows, shares.shape[1]))


def add_kernel(own, received, total):
    total[...] = (own[...] + received[...].astype(F32)).astype(BF16)


def weights_kernel(images, x, hid, grad, g_in, g_out, buf_in, buf_out, sem_in, sem_out):
    parts = buf_in.shape[0]
    step_in = g_in.shape[0] // parts
    step_out = g_out.shape[0] // parts
    count = x.shape[0]
    hid_low = pltpu.roll(hid[...].astype(F32), images, 0).astype(BF16)
    grad_high = pltpu.roll(grad[...].astype(F32), count - images, 0).astype(BF16)
    copies = []
    for i in range(parts):
        buf_out[i] = dot(hid_low[:, i * step_out : (i + 1) * step_out], x[...], TN).astype(BF16)
        copy = pltpu.make_async_copy(
            buf_out.at[i], g_out.at[pl.ds(i * step_out, step_out)], sem_out.at[i]
        )
        copy.start()
        copies.append(copy)
        buf_in[i] = dot(x[:, i * step_in : (i + 1) * step_in], grad_high, TN).astype(BF16)
        copy = pltpu.make_async_copy(
            buf_in.at[i], g_in.at[pl.ds(i * step_in, step_in)], sem_in.at[i]
        )
        copy.start()
        copies.append(copy)
    for copy in copies:
        copy.wait()


def logits_kernel(
    split_chips, shares, tok, dout, disp, comb, router_t, terms_out, left, right, ends
):
    images, slots, count = disp.shape
    chips, rows, main = shares.shape
    width = tok.shape[2]
    summed = []
    for slot in range(slots):
        total = shares[slot * split_chips].astype(F32)
        for chip in range(1, split_chips):
            total = total + shares[slot * split_chips + chip].astype(F32)
        summed.append(total)
    unpack(images, ends, jnp.stack(summed))
    stacked = jnp.concatenate(
        [
            jnp.concatenate(summed, axis=0),
            ends[...].reshape(slots * rows, width - main),
        ],
        axis=1,
    )
    stacked_b = stacked.astype(BF16)
    tok_all = tok[...].reshape(images * count, width)
    by_dout = dot(stacked_b, dout[...].reshape(images * count, width), NT)
    by_tok = dot(stacked_b, tok_all, NT)
    grads = []
    for b in range(images):
        span = slice(b * count, (b + 1) * count)
        grad_comb = jnp.concatenate(
            [by_dout[s * rows + b : s * rows + b + 1, span] for s in range(slots)], axis=0
        )
        grad_disp = jnp.concatenate(
            [
                by_tok[s * rows + images + b : s * rows + images + b + 1, span]
                for s in range(slots)
            ],
            axis=0,
        )
        dispatch = disp[b]
        combine = comb[b]
        grads.append(
            dispatch * (grad_disp - jnp.sum(dispatch * grad_disp, axis=1, keepdims=True))
            + combine * (grad_comb - jnp.sum(combine * grad_comb, axis=0, keepdims=True))
        )
    terms = dot(jnp.concatenate(grads, axis=1).astype(BF16), tok_all).astype(BF16)
    terms_out[...] = jnp.broadcast_to(terms[None], terms_out.shape)
    for b in range(images):
        left[b] = jnp.concatenate([disp[b], grads[b]], axis=0)
        right[b] = jnp.concatenate(
            [stacked[s * rows + images + b : s * rows + images + b + 1] for s in range(slots)]
            + [router_t[...].astype(F32)],
            axis=0,
        )


def tokens_kernel(left, right, grad_tokens, buf, sems):
    images, parts = buf.shape[:2]
    step = buf.shape[2]
    copies = []
    for b in range(images):
        rhs = right[b].astype(BF16)
        for i in range(parts):
            lhs = left[b, :, i * step : (i + 1) * step].astype(BF16)
            buf[b, i] = dot(lhs, rhs, TN).astype(BF16)
            copy = pltpu.make_async_copy(
                buf.at[b, i], grad_tokens.at[b, pl.ds(i * step, step)], sems.at[b, i]
            )
            copy.start()
            copies.append(copy)
    for copy in copies:
        copy.wait()


def sum_kernel(terms, total):
    total[...] = jnp.sum(terms[...].astype(F32), axis=0)


def swap_chips(blocks):
    count = lax.axis_size("expert")
    groups = [list(range(core, count, 2)) for core in range(2)]
    return lax.all_to_all(
        blocks, "expert", split_axis=0, concat_axis=0, axis_index_groups=groups, tiled=True
    )


def swap_cores(block):
    count = lax.axis_size("expert")
    return lax.ppermute(block, "expert", [(device, device ^ 1) for device in range(count)])


def per_device(tokens, router, w_in, w_out, d_out):
    devices = lax.axis_size("expert")
    chips = devices // 2
    slots = router.shape[1]
    split_chips = chips // slots
    images, count, width = tokens.shape
    hidden_units = w_in.shape[2]
    rows, main, extra = block_shape(images, width)
    half = chips * rows
    router_t = router.T
    big = images * count * width
    weight = width * hidden_units

    send, tok, dout, disp, comb = call(
        functools.partial(rows_kernel, split_chips),
        (
            vmem_out((chips, rows, main), BF16),
            vmem_out((images, count, width), BF16),
            vmem_out((images, count, width), BF16),
            vmem_out((images, slots, count), F32),
            vmem_out((images, slots, count), F32),
        ),
        (in_hbm(tokens), in_hbm(router_t), in_hbm(d_out)),
        (VMEM,) * 5,
        (HBM,) * 3,
        [
            pltpu.VMEM((slots, width), BF16),
            pltpu.VMEM((slots, rows, main), F32),
            pltpu.SemaphoreType.DMA((2 * images,)),
            pltpu.SemaphoreType.DMA,
        ],
        (6 * slots * big, 4 * big),
    )
    send, w_one, w_two = lax.optimization_barrier((send, w_in, w_out))
    w_one, w_two = in_vmem(w_one[0]), in_vmem(w_two[0])
    near = swap_chips(send)
    far = swap_cores(near)
    other, x, hid, grad = call(
        functools.partial(experts_kernel, images),
        (
            vmem_out((chips, rows, main), BF16),
            vmem_out((2 * half, width), BF16),
            vmem_out((2 * half, hidden_units), BF16),
            vmem_out((2 * half, hidden_units), BF16),
        ),
        (in_vmem(near), in_vmem(far), w_one, w_two),
        (VMEM,) * 4,
        (VMEM,) * 4,
        [
            pltpu.VMEM((2 * chips, rows, extra), F32),
            pltpu.VMEM((chips, rows, main), F32),
        ],
        (12 * half * weight, 4 * weight),
    )
    received = swap_cores(other)
    own = call(
        functools.partial(own_kernel, images),
        vmem_out((chips, rows, main), F32),
        (in_vmem(hid), in_vmem(grad), w_one, w_two),
        VMEM,
        (VMEM,) * 4,
        (),
        (4 * half * weight, 4 * weight),
    )
    total = call(
        add_kernel,
        vmem_out((chips, rows, main), BF16),
        (in_vmem(own), in_vmem(received)),
        VMEM,
        (VMEM,) * 2,
        (),
        (half * main, 8 * half * main),
    )
    shares = swap_chips(total)
    parts = 5
    g_in, g_out = call(
        functools.partial(weights_kernel, images),
        (
            jax.ShapeDtypeStruct((width, hidden_units), BF16),
            jax.ShapeDtypeStruct((hidden_units, width), BF16),
        ),
        (in_vmem(x), in_vmem(hid), in_vmem(grad)),
        (HBM,) * 2,
        (VMEM,) * 3,
        [
            pltpu.VMEM((parts, width // parts, hidden_units), BF16),
            pltpu.VMEM((parts, hidden_units // parts, width), BF16),
            pltpu.SemaphoreType.DMA((parts,)),
            pltpu.SemaphoreType.DMA((parts,)),
        ],
        (8 * half * weight, 4 * weight),
    )
    terms, left, right = call(
        functools.partial(logits_kernel, split_chips),
        (
            vmem_out((devices, slots, width), BF16),
            vmem_out((images, 2 * slots, count), F32),
            vmem_out((images, 2 * slots, width), F32),
        ),
        (
            in_vmem(shares),
            in_vmem(tok),
            in_vmem(dout),
            in_vmem(disp),
            in_vmem(comb),
            router_t,
        ),
        (VMEM,) * 3,
        (VMEM,) * 6,
        [pltpu.VMEM((slots, rows, extra), F32)],
        (6 * slots * big, 4 * big),
    )
    terms = lax.all_to_all(terms, "expert", split_axis=0, concat_axis=0, tiled=True)
    pieces = 2
    grad_tokens = call(
        tokens_kernel,
        jax.ShapeDtypeStruct(tokens.shape, BF16),
        (in_vmem(left), in_vmem(right)),
        HBM,
        (VMEM,) * 2,
        [
            pltpu.VMEM((images, pieces, count // pieces, width), BF16),
            pltpu.SemaphoreType.DMA((images, pieces)),
        ],
        (4 * slots * big, 2 * big),
    )
    grad_router = call(
        sum_kernel,
        jax.ShapeDtypeStruct((slots, width), F32),
        (in_vmem(terms),),
        VMEM,
        (VMEM,),
        (),
        (devices * slots * width, 2 * devices * slots * width),
    )
    return (grad_tokens, g_in[None], g_out[None], grad_router.T)


def solution(mesh):
    in_specs = (
        P(("groups", "expert"), None, None),
        P(None, "groups"),
        P(("groups", "expert"), None, None),
        P(("groups", "expert"), None, None),
        P(("groups", "expert"), None, None),
    )
    out_specs = (
        P(("groups", "expert"), None, None),
        P(("groups", "expert"), None, None),
        P(("groups", "expert"), None, None),
        P(None, "groups"),
    )
    return jax.shard_map(
        per_device, mesh=mesh, in_specs=in_specs, out_specs=out_specs, check_vma=False
    )
```

time: 50.1 us -> 47.9 us (0.956)
  waiting for transfers between devices: 6.06 us -> 5.12 us
  Pallas kernels: 12.8 us -> 13.7 us
  blocking collectives: 25.1 us -> 24.4 us
  local copies, waits for them, and re-layouts: 0.7 us -> 0.01 us
  other arithmetic: 0.68 us -> 0 us
    ppermute x2, waiting for transfers between devices: 2.65 us -> 1.71 us  [swap_cores(): lax.ppermute(block, 'expert', [(device, device ^ 1) for device in range(c...]
    pallas_call x6 -> x8, Pallas kernels: 12.8 us -> 13.7 us  [call(): pl.pallas_call(kernel, out_shape=outs, in_specs=in_specs, out_specs=out_s...]
    all_to_all x2, blocking collectives: 25.1 us -> 24.4 us  [swap_chips(): lax.all_to_all(blocks, 'expert', split_axis=0, concat_axis=0, axis_index_...]
    unnamed x8 -> x6, local copies, waits for them, and re-layouts: 0.7 us -> 0.01 us
    reduce_sum x1 -> x0, other arithmetic: 0.68 us -> none  [per_device(): grad_router = jnp.sum(terms.astype(F32), axis=0).T]
  transfers between devices with their start and end apart: 3 -> 3, of which waited for: 3 -> 3; matrix products, arithmetic and copies ran while one was open for 0% -> 0% of each run, Pallas kernels for 7% -> 9%
where the time goes in v5:
time: 47.9 us; the launch traced here: 47.6 us
  blocking collectives  24.4 us (51%)
  Pallas kernels  13.7 us (29%)
  waiting for transfers between devices  5.12 us (11%)
  starting transfers between devices  3.72 us (8%)
  between operations  0.7 us (1%)
    all_to_all x2, blocking collectives, swap_chips(): lax.all_to_all(blocks, 'expert', split_axis=0, concat_axis=0, axis_index_...  24.4 us
    pallas_call x8, Pallas kernels, call(): pl.pallas_call(kernel, out_shape=outs, in_specs=in_specs, out_specs=out_s...  13.7 us
    all_to_all x1, starting transfers between devices, per_device(): lax.all_to_all(terms, 'expert', split_axis=0, concat_axis=0, tiled=True)  3.5 us
    all_to_all x1, waiting for transfers between devices, per_device(): lax.all_to_all(terms, 'expert', split_axis=0, concat_axis=0, tiled=True)  3.41 us
    ppermute x2, waiting for transfers between devices, swap_cores(): lax.ppermute(block, 'expert', [(device, device ^ 1) for device in range(c...  1.71 us
  transfers between devices with their start and end apart: 3, of which 3 were waited for; matrix products, arithmetic and copies ran while one was open for 0% of the time, Pallas kernels for 9%

profile of v5, /device:TPU:0, one launch (start us, length us, event | category | flops | bytes accessed | tf_op | source)
XLA Modules:
  0.0 47.6 jit_solution(8426874480559238023)
XLA Ops:
  0.6 0.0 copy-start
  0.6 0.0 copy-start.1
  0.7 4.3 %shard_map.84 = (bf16[8,8,1024]{2,1,0:T(8,128)(2,1)S(1)}, bf16[3,256,1280]{2,1,0:T(8,128)(2,1)S(1)}, bf16[3,256,1280]{2,1,0:T(8,128)(2,1)S(1)}, f32[3,2,256]{2,1,0:T(2,128)S(1)}, f32[3,2,256]{2,1,0:T(2,128)S(1)}) custom-call(bf16[3,256,1280]{2,1,0:T(8,128)(2,1)} %tokens.1, bf16[2,1280]{1,0:T(2,128)(2,1)} %bitcast.10, bf16[3,256,1280]{2,1,0:T(8,128)(2,1)} %d_out.1), custom_call_target="tpu_custom_call" | custom-call | flops 11796480 | bytes 3932160 | tf_op jit(solution)/shard_map/pallas_call | solution.py:38
  4.9 14.4 %all_to_all.15.near = bf16[8,8,1024]{2,1,0:T(8,128)(2,1)S(1)} all-to-all(bf16[8,8,1024]{2,1,0:T(8,128)(2,1)S(1)} %get-tuple-element.22), channel_id=1, replica_groups={{0,2,4,6,8,10,12,14},{1,3,5,7,9,11,13,15},{16,18,20,22,24,26,28,30},{17..., dimensions={0} | all-to-all | bytes 262144 | tf_op jit(solution)/shard_map/all_to_all | solution.py:291
  19.4 0.0 collective-permute-start
  19.4 1.3 %collective-permute-done.far = bf16[8,8,1024]{2,1,0:T(8,128)(2,1)S(1)} collective-permute-done((bf16[8,8,1024]{2,1,0:T(8,128)(2,1)S(1)}, bf16[8,8,1024]{2,1,0:T(8,128)(2,1)S(1)}, u32[]{:S(2)}, u32[]{:S(2)}) %collective-permute-start) | collective-permute-done | bytes 131104 | tf_op jit(solution)/shard_map/ppermute | solution.py:298
  20.7 0.0 copy-done
  20.7 0.0 copy-done.1
  20.7 1.9 %shard_map.85 = (bf16[8,8,1024]{2,1,0:T(8,128)(2,1)S(1)}, bf16[128,1280]{1,0:T(8,128)(2,1)S(1)}, bf16[128,640]{1,0:T(8,128)(2,1)S(1)}, bf16[128,640]{1,0:T(8,128)(2,1)S(1)}) custom-call(bf16[8,8,1024]{2,1,0:T(8,128)(2,1)S(1)} %all_to_all.15.near, bf16[8,8,1024]{2,1,0:T(8,128)(2,1)S(1)} %collective-permute-done.far, bf16[1280,640]{1,0:T(8,128)(2,1)S(1)} %bitcast.6, ...), custom_call_target="tpu_custom_call" | custom-call | flops 629145600 | bytes 3276800 | tf_op jit(solution)/shard_map/pallas_call | solution.py:38
  22.7 0.2 collective-permute-start.1
  22.9 0.0 copy-start.2
  22.9 0.8 %shard_map.86.own = f32[8,8,1024]{2,1,0:T(8,128)S(1)} custom-call(bf16[128,640]{1,0:T(8,128)(2,1)S(1)} %get-tuple-element.25.hid, bf16[128,640]{1,0:T(8,128)(2,1)S(1)} %get-tuple-element.26.grad, bf16[1280,640]{1,0:T(8,128)(2,1)S(1)} %bitcast.7, bf16[640,1280]{1,0:T(8,128)(2,1)S(1)} %bitcast.9), custom_call_target="tpu_custom_call" | custom-call | flops 209715200 | bytes 3276800 | tf_op jit(solution)/shard_map/pallas_call | solution.py:38
  23.7 0.4 collective-permute-done.1.received
  24.1 10.0 %all_to_all.16.shares = bf16[8,8,1024]{2,1,0:T(8,128)(2,1)S(1)} all-to-all(bf16[8,8,1024]{2,1,0:T(8,128)(2,1)S(1)} %shard_map.87), channel_id=1, replica_groups={{0,2,4,6,8,10,12,14},{1,3,5,7,9,11,13,15},{16,18,20,22,24,26,28,30},{17..., dimensions={0} | all-to-all | bytes 262144 | tf_op jit(solution)/shard_map/all_to_all | solution.py:291
  34.1 0.0 copy-done.2
  34.1 2.3 %shard_map.88 = (bf16[16,2,1280]{2,1,0:T(2,128)(2,1)}, f32[3,4,256]{2,1,0:T(4,128)S(1)}, f32[3,4,1280]{2,1,0:T(4,128)S(1)}) custom-call(bf16[8,8,1024]{2,1,0:T(8,128)(2,1)S(1)} %all_to_all.16.shares, bf16[3,256,1280]{2,1,0:T(8,128)(2,1)S(1)} %get-tuple-element.28.tok, bf16[3,256,1280]{2,1,0:T(8,128)(2,1)S(1)} %get-tuple-element.29.dout, ...), custom_call_target="tpu_custom_call" | custom-call | flops 11796480 | bytes 3932160 | tf_op jit(solution)/shard_map/pallas_call | solution.py:38
  36.3 3.5 %all-to-all-start.2 = ((bf16[16,2,1280]{2,1,0:T(2,128)(2,1)}), bf16[16,2,1280]{2,1,0:T(2,128)(2,1)S(1)}, u32[]{:S(2)}, u32[]{:S(2)}) async-start(bf16[16,2,1280]{2,1,0:T(2,128)(2,1)} %get-tuple-element.37), calls=%async_computation.2 | async-start | bytes 163840 | tf_op jit(solution)/shard_map/all_to_all | solution.py:413
  39.8 2.1 %shard_map.90 = (bf16[1280,640]{1,0:T(8,128)(2,1)}, bf16[640,1280]{1,0:T(8,128)(2,1)}) custom-call(bf16[128,1280]{1,0:T(8,128)(2,1)S(1)} %get-tuple-element.34.x, bf16[128,640]{1,0:T(8,128)(2,1)S(1)} %get-tuple-element.25.hid, bf16[128,640]{1,0:T(8,128)(2,1)S(1)} %get-tuple-element.26.grad), custom_call_target="tpu_custom_call" | custom-call | flops 419430400 | bytes 3276800 | tf_op jit(solution)/shard_map/pallas_call | solution.py:38
  41.9 1.6 %shard_map.89 = bf16[3,256,1280]{2,1,0:T(8,128)(2,1)} custom-call(f32[3,4,256]{2,1,0:T(4,128)S(1)} %get-tuple-element.32.left, f32[3,4,1280]{2,1,0:T(4,128)S(1)} %get-tuple-element.33.right), custom_call_target="tpu_custom_call" | custom-call | flops 7864320 | bytes 1966080 | tf_op jit(solution)/shard_map/pallas_call | solution.py:38
  43.5 3.4 %all-to-all-done.2.terms = bf16[16,2,1280]{2,1,0:T(2,128)(2,1)S(1)} async-done(((bf16[16,2,1280]{2,1,0:T(2,128)(2,1)}), bf16[16,2,1280]{2,1,0:T(2,128)(2,1)S(1)}, u32[]{:S(2)}, u32[]{:S(2)}) %all-to-all-start.2) | async-done | bytes 81952 | tf_op jit(solution)/shard_map/all_to_all | solution.py:413
  47.0 0.7 %shard_map.91 = f32[2,1280]{1,0:T(2,128)} custom-call(bf16[16,2,1280]{2,1,0:T(2,128)(2,1)S(1)} %all-to-all-done.2.terms), custom_call_target="tpu_custom_call" | custom-call | flops 40960 | bytes 81920 | tf_op jit(solution)/shard_map/pallas_call | solution.py:38
  (1 shorter events, 0.0 us)
Async XLA Ops:
  0.6 20.1 %copy-start = (bf16[1,1280,640]{2,1,0:T(8,128)(2,1)S(1)}, bf16[1,1280,640]{2,1,0:T(8,128)(2,1)}, u32[]{:S(2)}) copy-start(bf16[1,1280,640]{2,1,0:T(8,128)(2,1)} %param.7) | copy-start | bytes 4915204
  0.6 20.1 %copy-start.1 = (bf16[1,640,1280]{2,1,0:T(8,128)(2,1)S(1)}, bf16[1,640,1280]{2,1,0:T(8,128)(2,1)}, u32[]{:S(2)}) copy-start(bf16[1,640,1280]{2,1,0:T(8,128)(2,1)} %param.8) | copy-start | bytes 4915204
  19.4 1.3 %collective-permute-start = (bf16[8,8,1024]{2,1,0:T(8,128)(2,1)S(1)}, bf16[8,8,1024]{2,1,0:T(8,128)(2,1)S(1)}, u32[]{:S(2)}, u32[]{:S(2)}) collective-permute-start(bf16[8,8,1024]{2,1,0:T(8,128)(2,1)S(1)} %all_to_all.15.near), channel_id=1, source_target_pairs={{0,1},{1,0},{2,3},{3,2},{4,5},{5,4},{6,7},{7,6},{8,9},{9,8},{10,11... | collective-permute-start | bytes 393224 | tf_op jit(solution)/shard_map/ppermute | solution.py:298
  22.7 1.4 %collective-permute-start.1 = (bf16[8,8,1024]{2,1,0:T(8,128)(2,1)S(1)}, bf16[8,8,1024]{2,1,0:T(8,128)(2,1)S(1)}, u32[]{:S(2)}, u32[]{:S(2)}) collective-permute-start(bf16[8,8,1024]{2,1,0:T(8,128)(2,1)S(1)} %get-tuple-element.27), channel_id=1, source_target_pairs={{0,1},{1,0},{2,3},{3,2},{4,5},{5,4},{6,7},{7,6},{8,9},{9,8},{10,11... | collective-permute-start | bytes 393224 | tf_op jit(solution)/shard_map/ppermute | solution.py:298
  22.9 11.2 %copy-start.2 = (bf16[1280,2]{0,1:T(2,128)(2,1)S(1)}, bf16[1280,2]{0,1:T(2,128)(2,1)}, u32[]{:S(2)}) copy-start(bf16[1280,2]{0,1:T(2,128)(2,1)} %param.6) | copy-start | bytes 15364
  36.3 10.6 %all-to-all-start.2 = ((bf16[16,2,1280]{2,1,0:T(2,128)(2,1)}), bf16[16,2,1280]{2,1,0:T(2,128)(2,1)S(1)}, u32[]{:S(2)}, u32[]{:S(2)}) async-start(bf16[16,2,1280]{2,1,0:T(2,128)(2,1)} %get-tuple-element.37), calls=%async_computation.2 | async-start | bytes 163840 | tf_op jit(solution)/shard_map/all_to_all | solution.py:413

commit v6 on v5

--- a/solution.py
+++ b/solution.py
@@ -15,7 +15,7 @@
 
 VMEM = pl.BlockSpec(memory_space=pltpu.VMEM)
 HBM = pl.BlockSpec(memory_space=pltpu.HBM)
-VMEM_LIMIT = 40 * 1024 * 1024
+MIB = 1024 * 1024
 
 
 def dot(left, right, dims=NN):
@@ -34,14 +34,14 @@
     return pltpu.VMEM(shape, dtype)
 
 
-def call(kernel, outs, ins, out_specs, in_specs, scratch=(), cost=None):
+def call(kernel, outs, ins, out_specs, in_specs, scratch=(), cost=None, limit=40 * MIB):
     return pl.pallas_call(
         kernel,
         out_shape=outs,
         in_specs=in_specs,
         out_specs=out_specs,
         scratch_shapes=list(scratch),
-        compiler_params=pltpu.CompilerParams(vmem_limit_bytes=VMEM_LIMIT),
+        compiler_params=pltpu.CompilerParams(vmem_limit_bytes=limit),
         cost_estimate=pl.CostEstimate(flops=cost[0], bytes_accessed=cost[1], transcendentals=0),
     )(*ins)
 
@@ -81,21 +81,25 @@
     tokens,
     router_hbm,
     d_out,
+    w_in,
+    w_out,
     send,
     tok,
     dout,
     disp_out,
     comb_out,
+    w_one,
+    w_two,
     router_t,
     block,
     sems,
-    router_sem,
+    other_sems,
 ):
     images = tok.shape[0]
     slots = router_t.shape[0]
     main = send.shape[2]
     extra = tok.shape[2] - main
-    fetch_router = pltpu.make_async_copy(router_hbm, router_t, router_sem)
+    fetch_router = pltpu.make_async_copy(router_hbm, router_t, other_sems.at[0])
     fetch_router.start()
     fetch_tok = [
         pltpu.make_async_copy(tokens.at[b], tok.at[b], sems.at[b]) for b in range(images)
@@ -103,7 +107,11 @@
     fetch_dout = [
         pltpu.make_async_copy(d_out.at[b], dout.at[b], sems.at[images + b]) for b in range(images)
     ]
-    for copy in fetch_tok + fetch_dout:
+    fetch_weights = [
+        pltpu.make_async_copy(w_in, w_one, other_sems.at[1]),
+        pltpu.make_async_copy(w_out, w_two, other_sems.at[2]),
+    ]
+    for copy in fetch_tok:
         copy.start()
     block[...] = jnp.zeros_like(block)
 
@@ -116,14 +124,20 @@
     logits = []
     for b in range(images):
         fetch_tok[b].wait()
+        if b == 0:
+            for copy in fetch_dout:
+                copy.start()
+        if b == images - 1:
+            for copy in fetch_weights:
+                copy.start()
         logits.append(dot(router_t[...], tok[b], NT))
     disps = []
     combs = []
     for b in range(images):
         exps = jnp.exp(logits[b] - jnp.max(logits[b], axis=1, keepdims=True))
-        disps.append(exps / jnp.sum(exps, axis=1, keepdims=True))
+        disps.append(exps * (1.0 / jnp.sum(exps, axis=1, keepdims=True)))
         exps = jnp.exp(logits[b] - jnp.max(logits[b], axis=0, keepdims=True))
-        combs.append(exps / jnp.sum(exps, axis=0, keepdims=True))
+        combs.append(exps * (1.0 / jnp.sum(exps, axis=0, keepdims=True)))
         disp_out[b] = disps[b]
         comb_out[b] = combs[b]
     for b in range(images):
@@ -135,6 +149,8 @@
         rows = block[slot].astype(BF16)
         for chip in range(split_chips):
             send[slot * split_chips + chip] = rows
+    for copy in fetch_weights:
+        copy.wait()
 
 
 def experts_kernel(images, near, far, w_in, w_out, other, x_out, hid_out, grad_out, ends, packed):
@@ -311,7 +327,7 @@
     big = images * count * width
     weight = width * hidden_units
 
-    send, tok, dout, disp, comb = call(
+    send, tok, dout, disp, comb, w_one, w_two = call(
         functools.partial(rows_kernel, split_chips),
         (
             vmem_out((chips, rows, main), BF16),
@@ -319,20 +335,21 @@
             vmem_out((images, count, width), BF16),
             vmem_out((images, slots, count), F32),
             vmem_out((images, slots, count), F32),
+            vmem_out(w_in.shape[1:], BF16),
+            vmem_out(w_out.shape[1:], BF16),
         ),
-        (in_hbm(tokens), in_hbm(router_t), in_hbm(d_out)),
-        (VMEM,) * 5,
-        (HBM,) * 3,
+        tuple(in_hbm(array) for array in (tokens, router_t, d_out, w_in[0], w_out[0])),
+        (VMEM,) * 7,
+        (HBM,) * 5,
         [
             pltpu.VMEM((slots, width), BF16),
             pltpu.VMEM((slots, rows, main), F32),
             pltpu.SemaphoreType.DMA((2 * images,)),
-            pltpu.SemaphoreType.DMA,
+            pltpu.SemaphoreType.DMA((3,)),
         ],
         (6 * slots * big, 4 * big),
     )
-    send, w_one, w_two = lax.optimization_barrier((send, w_in, w_out))
-    w_one, w_two = in_vmem(w_one[0]), in_vmem(w_two[0])
+    w_one, w_two = in_vmem(w_one), in_vmem(w_two)
     near = swap_chips(send)
     far = swap_cores(near)
     other, x, hid, grad = call(

time: 47.9 us -> 47.8 us (level)
  no operation moved by 1% of the time
where the time goes in v6:
time: 47.8 us; the launch traced here: 47.5 us
  blocking collectives  24.4 us (51%)
  Pallas kernels  13.6 us (28%)
  waiting for transfers between devices  5.12 us (11%)
  starting transfers between devices  3.72 us (8%)
  between operations  0.69 us (1%)
    all_to_all x2, blocking collectives, swap_chips(): lax.all_to_all(blocks, 'expert', split_axis=0, concat_axis=0, axis_index_...  24.4 us
    pallas_call x8, Pallas kernels, call(): pl.pallas_call(kernel, out_shape=outs, in_specs=in_specs, out_specs=out_s...  13.6 us
    all_to_all x1, starting transfers between devices, per_device(): lax.all_to_all(terms, 'expert', split_axis=0, concat_axis=0, tiled=True)  3.5 us
    all_to_all x1, waiting for transfers between devices, per_device(): lax.all_to_all(terms, 'expert', split_axis=0, concat_axis=0, tiled=True)  3.41 us
    ppermute x2, waiting for transfers between devices, swap_cores(): lax.ppermute(block, 'expert', [(device, device ^ 1) for device in range(c...  1.71 us
  transfers between devices with their start and end apart: 3, of which 3 were waited for; matrix products, arithmetic and copies ran while one was open for 0% of the time, Pallas kernels for 9%

profile of v6, /device:TPU:0, one launch (start us, length us, event | category | flops | bytes accessed | tf_op | source)
XLA Modules:
  0.0 47.5 jit_solution(13060718818443397019)
XLA Ops:
  0.6 4.2 %shard_map.84 = (bf16[8,8,1024]{2,1,0:T(8,128)(2,1)S(1)}, bf16[3,256,1280]{2,1,0:T(8,128)(2,1)S(1)}, bf16[3,256,1280]{2,1,0:T(8,128)(2,1)S(1)}, f32[3,2,256]{2,1...) custom-call(bf16[3,256,1280]{2,1,0:T(8,128)(2,1)} %tokens.1, ...), custom_call_target="tpu_custom_call" | custom-call | flops 11796480 | bytes 3932160 | tf_op jit(solution)/shard_map/pallas_call | solution.py:38
  4.8 14.4 %all_to_all.15.near = bf16[8,8,1024]{2,1,0:T(8,128)(2,1)S(1)} all-to-all(bf16[8,8,1024]{2,1,0:T(8,128)(2,1)S(1)} %get-tuple-element.20), channel_id=1, replica_groups={{0,2,4,6,8,10,12,14},{1,3,5,7,9,11,13,15},{16,18,20,22,24,26,28,30},{17..., dimensions={0} | all-to-all | bytes 262144 | tf_op jit(solution)/shard_map/all_to_all | solution.py:307
  19.2 0.0 collective-permute-start
  19.2 1.3 %collective-permute-done.far = bf16[8,8,1024]{2,1,0:T(8,128)(2,1)S(1)} collective-permute-done((bf16[8,8,1024]{2,1,0:T(8,128)(2,1)S(1)}, bf16[8,8,1024]{2,1,0:T(8,128)(2,1)S(1)}, u32[]{:S(2)}, u32[]{:S(2)}) %collective-permute-start) | collective-permute-done | bytes 131104 | tf_op jit(solution)/shard_map/ppermute | solution.py:314
  20.6 1.9 %shard_map.85 = (bf16[8,8,1024]{2,1,0:T(8,128)(2,1)S(1)}, bf16[128,1280]{1,0:T(8,128)(2,1)S(1)}, bf16[128,640]{1,0:T(8,128)(2,1)S(1)}, bf16[128,640]{1,0:T(8,128)(2,1)S(1)}) custom-call(bf16[8,8,1024]{2,1,0:T(8,128)(2,1)S(1)} %all_to_all.15.near, bf16[8,8,1024]{2,1,0:T(8,128)(2,1)S(1)} %collective-permute-done.far, ...), custom_call_target="tpu_custom_call" | custom-call | flops 629145600 | bytes 3276800 | tf_op jit(solution)/shard_map/pallas_call | solution.py:38
  22.5 0.2 collective-permute-start.1
  22.7 0.0 copy-start
  22.7 0.8 %shard_map.86.own = f32[8,8,1024]{2,1,0:T(8,128)S(1)} custom-call(bf16[128,640]{1,0:T(8,128)(2,1)S(1)} %get-tuple-element.23.hid, bf16[128,640]{1,0:T(8,128)(2,1)S(1)} %get-tuple-element.24.grad, bf16[1280,640]{1,0:T(8,128)(2,1)S(1)} %get-tuple-element.21.w_in, bf16[640,1280]{1,0:T(8,128)(2,1)S(1)} %get-tuple-element.22.w_out), custom_call_target="tpu_custom_call" | custom-call | flops 209715200 | bytes 3276800 | tf_op jit(solution)/shard_map/pallas_call | solution.py:38
  23.6 0.4 collective-permute-done.1.received
  23.9 10.0 %all_to_all.16.shares = bf16[8,8,1024]{2,1,0:T(8,128)(2,1)S(1)} all-to-all(bf16[8,8,1024]{2,1,0:T(8,128)(2,1)S(1)} %shard_map.87), channel_id=1, replica_groups={{0,2,4,6,8,10,12,14},{1,3,5,7,9,11,13,15},{16,18,20,22,24,26,28,30},{17..., dimensions={0} | all-to-all | bytes 262144 | tf_op jit(solution)/shard_map/all_to_all | solution.py:307
  33.9 0.0 copy-done
  33.9 2.3 %shard_map.88 = (bf16[16,2,1280]{2,1,0:T(2,128)(2,1)}, f32[3,4,256]{2,1,0:T(4,128)S(1)}, f32[3,4,1280]{2,1,0:T(4,128)S(1)}) custom-call(bf16[8,8,1024]{2,1,0:T(8,128)(2,1)S(1)} %all_to_all.16.shares, bf16[3,256,1280]{2,1,0:T(8,128)(2,1)S(1)} %get-tuple-element.26.tok, bf16[3,256,1280]{2,1,0:T(8,128)(2,1)S(1)} %get-tuple-element.27.dout, ...), custom_call_target="tpu_custom_call" | custom-call | flops 11796480 | bytes 3932160 | tf_op jit(solution)/shard_map/pallas_call | solution.py:38
  36.2 3.5 %all-to-all-start.2 = ((bf16[16,2,1280]{2,1,0:T(2,128)(2,1)}), bf16[16,2,1280]{2,1,0:T(2,128)(2,1)S(1)}, u32[]{:S(2)}, u32[]{:S(2)}) async-start(bf16[16,2,1280]{2,1,0:T(2,128)(2,1)} %get-tuple-element.35), calls=%async_computation.2 | async-start | bytes 163840 | tf_op jit(solution)/shard_map/all_to_all | solution.py:430
  39.7 2.1 %shard_map.90 = (bf16[1280,640]{1,0:T(8,128)(2,1)}, bf16[640,1280]{1,0:T(8,128)(2,1)}) custom-call(bf16[128,1280]{1,0:T(8,128)(2,1)S(1)} %get-tuple-element.32.x, bf16[128,640]{1,0:T(8,128)(2,1)S(1)} %get-tuple-element.23.hid, bf16[128,640]{1,0:T(8,128)(2,1)S(1)} %get-tuple-element.24.grad), custom_call_target="tpu_custom_call" | custom-call | flops 419430400 | bytes 3276800 | tf_op jit(solution)/shard_map/pallas_call | solution.py:38
  41.8 1.6 %shard_map.89 = bf16[3,256,1280]{2,1,0:T(8,128)(2,1)} custom-call(f32[3,4,256]{2,1,0:T(4,128)S(1)} %get-tuple-element.30.left, f32[3,4,1280]{2,1,0:T(4,128)S(1)} %get-tuple-element.31.right), custom_call_target="tpu_custom_call" | custom-call | flops 7864320 | bytes 1966080 | tf_op jit(solution)/shard_map/pallas_call | solution.py:38
  43.4 3.4 %all-to-all-done.2.terms = bf16[16,2,1280]{2,1,0:T(2,128)(2,1)S(1)} async-done(((bf16[16,2,1280]{2,1,0:T(2,128)(2,1)}), bf16[16,2,1280]{2,1,0:T(2,128)(2,1)S(1)}, u32[]{:S(2)}, u32[]{:S(2)}) %all-to-all-start.2) | async-done | bytes 81952 | tf_op jit(solution)/shard_map/all_to_all | solution.py:430
  46.8 0.7 %shard_map.91 = f32[2,1280]{1,0:T(2,128)} custom-call(bf16[16,2,1280]{2,1,0:T(2,128)(2,1)S(1)} %all-to-all-done.2.terms), custom_call_target="tpu_custom_call" | custom-call | flops 40960 | bytes 81920 | tf_op jit(solution)/shard_map/pallas_call | solution.py:38
  (1 shorter events, 0.0 us)
Async XLA Ops:
  19.2 1.3 %collective-permute-start = (bf16[8,8,1024]{2,1,0:T(8,128)(2,1)S(1)}, bf16[8,8,1024]{2,1,0:T(8,128)(2,1)S(1)}, u32[]{:S(2)}, u32[]{:S(2)}) collective-permute-start(bf16[8,8,1024]{2,1,0:T(8,128)(2,1)S(1)} %all_to_all.15.near), channel_id=1, source_target_pairs={{0,1},{1,0},{2,3},{3,2},{4,5},{5,4},{6,7},{7,6},{8,9},{9,8},{10,11... | collective-permute-start | bytes 393224 | tf_op jit(solution)/shard_map/ppermute | solution.py:314
  22.5 1.4 %collective-permute-start.1 = (bf16[8,8,1024]{2,1,0:T(8,128)(2,1)S(1)}, bf16[8,8,1024]{2,1,0:T(8,128)(2,1)S(1)}, u32[]{:S(2)}, u32[]{:S(2)}) collective-permute-start(bf16[8,8,1024]{2,1,0:T(8,128)(2,1)S(1)} %get-tuple-element.25), channel_id=1, source_target_pairs={{0,1},{1,0},{2,3},{3,2},{4,5},{5,4},{6,7},{7,6},{8,9},{9,8},{10,11... | collective-permute-start | bytes 393224 | tf_op jit(solution)/shard_map/ppermute | solution.py:314
  22.7 11.2 %copy-start = (bf16[1280,2]{0,1:T(2,128)(2,1)S(1)}, bf16[1280,2]{0,1:T(2,128)(2,1)}, u32[]{:S(2)}) copy-start(bf16[1280,2]{0,1:T(2,128)(2,1)} %param.6) | copy-start | bytes 15364
  36.2 10.6 %all-to-all-start.2 = ((bf16[16,2,1280]{2,1,0:T(2,128)(2,1)}), bf16[16,2,1280]{2,1,0:T(2,128)(2,1)S(1)}, u32[]{:S(2)}, u32[]{:S(2)}) async-start(bf16[16,2,1280]{2,1,0:T(2,128)(2,1)} %get-tuple-element.35), calls=%async_computation.2 | async-start | bytes 163840 | tf_op jit(solution)/shard_map/all_to_all | solution.py:430

commit v7 on v5

--- a/solution.py
+++ b/solution.py
@@ -15,7 +15,7 @@
 
 VMEM = pl.BlockSpec(memory_space=pltpu.VMEM)
 HBM = pl.BlockSpec(memory_space=pltpu.HBM)
-VMEM_LIMIT = 40 * 1024 * 1024
+MIB = 1024 * 1024
 
 
 def dot(left, right, dims=NN):
@@ -34,14 +34,14 @@
     return pltpu.VMEM(shape, dtype)
 
 
-def call(kernel, outs, ins, out_specs, in_specs, scratch=(), cost=None):
+def call(kernel, outs, ins, out_specs, in_specs, scratch=(), cost=None, limit=40 * MIB):
     return pl.pallas_call(
         kernel,
         out_shape=outs,
         in_specs=in_specs,
         out_specs=out_specs,
         scratch_shapes=list(scratch),
-        compiler_params=pltpu.CompilerParams(vmem_limit_bytes=VMEM_LIMIT),
+        compiler_params=pltpu.CompilerParams(vmem_limit_bytes=limit),
         cost_estimate=pl.CostEstimate(flops=cost[0], bytes_accessed=cost[1], transcendentals=0),
     )(*ins)
 
@@ -92,7 +92,6 @@
     router_sem,
 ):
     images = tok.shape[0]
-    slots = router_t.shape[0]
     main = send.shape[2]
     extra = tok.shape[2] - main
     fetch_router = pltpu.make_async_copy(router_hbm, router_t, router_sem)
@@ -103,7 +102,7 @@
     fetch_dout = [
         pltpu.make_async_copy(d_out.at[b], dout.at[b], sems.at[images + b]) for b in range(images)
     ]
-    for copy in fetch_tok + fetch_dout:
+    for copy in fetch_tok:
         copy.start()
     block[...] = jnp.zeros_like(block)
 
@@ -116,14 +115,17 @@
     logits = []
     for b in range(images):
         fetch_tok[b].wait()
+        if b == 0:
+            for copy in fetch_dout:
+                copy.start()
         logits.append(dot(router_t[...], tok[b], NT))
     disps = []
     combs = []
     for b in range(images):
         exps = jnp.exp(logits[b] - jnp.max(logits[b], axis=1, keepdims=True))
-        disps.append(exps / jnp.sum(exps, axis=1, keepdims=True))
+        disps.append(exps * (1.0 / jnp.sum(exps, axis=1, keepdims=True)))
         exps = jnp.exp(logits[b] - jnp.max(logits[b], axis=0, keepdims=True))
-        combs.append(exps / jnp.sum(exps, axis=0, keepdims=True))
+        combs.append(exps * (1.0 / jnp.sum(exps, axis=0, keepdims=True)))
         disp_out[b] = disps[b]
         comb_out[b] = combs[b]
     for b in range(images):
@@ -131,13 +133,52 @@
     for b in range(images):
         fetch_dout[b].wait()
         put(images + b, dot(combs[b].astype(BF16), dout[b]))
-    for slot in range(slots):
+    for slot in range(block.shape[0]):
         rows = block[slot].astype(BF16)
         for chip in range(split_chips):
             send[slot * split_chips + chip] = rows
 
 
-def experts_kernel(images, near, far, w_in, w_out, other, x_out, hid_out, grad_out, ends, packed):
+def fetch_kernel(source, _, target, sems):
+    parts = sems.shape[0]
+    step = source.shape[0] // parts
+    copies = [
+        pltpu.make_async_copy(
+            source.at[pl.ds(i * step, step)], target.at[pl.ds(i * step, step)], sems.at[i]
+        )
+        for i in range(parts)
+    ]
+    for copy in copies:
+        copy.start()
+    for copy in copies:
+        copy.wait()
+
+
+def experts_kernel(
+    images,
+    near,
+    far,
+    w_in,
+    w_out_hbm,
+    other,
+    x_out,
+    hid_out,
+    grad_out,
+    w_out,
+    ends,
+    packed,
+    sems,
+):
+    parts = sems.shape[0]
+    step = w_out.shape[0] // parts
+    copies = [
+        pltpu.make_async_copy(
+            w_out_hbm.at[pl.ds(i * step, step)], w_out.at[pl.ds(i * step, step)], sems.at[i]
+        )
+        for i in range(parts)
+    ]
+    for copy in copies:
+        copy.start()
     chips, rows, main = near.shape
     half = chips * rows
     width = x_out.shape[1]
@@ -154,6 +195,8 @@
     )
     x_out[...] = x
     pre = dot(x, w_in[...])
+    for copy in copies:
+        copy.wait()
     grad_hidden = dot(x, w_out[...], NT)
     place = lax.broadcasted_iota(jnp.int32, pre.shape, 0) % rows
     slot_row = place < images
@@ -331,27 +374,38 @@
         ],
         (6 * slots * big, 4 * big),
     )
-    send, w_one, w_two = lax.optimization_barrier((send, w_in, w_out))
-    w_one, w_two = in_vmem(w_one[0]), in_vmem(w_two[0])
     near = swap_chips(send)
     far = swap_cores(near)
-    other, x, hid, grad = call(
+    w_one = call(
+        fetch_kernel,
+        vmem_out(w_in.shape[1:], BF16),
+        (in_hbm(w_in[0]), in_vmem(near)),
+        VMEM,
+        (HBM, VMEM),
+        [pltpu.SemaphoreType.DMA((5,))],
+        (0, 4 * weight),
+    )
+    w_one = in_vmem(w_one)
+    other, x, hid, grad, w_two = call(
         functools.partial(experts_kernel, images),
         (
             vmem_out((chips, rows, main), BF16),
             vmem_out((2 * half, width), BF16),
             vmem_out((2 * half, hidden_units), BF16),
             vmem_out((2 * half, hidden_units), BF16),
+            vmem_out(w_out.shape[1:], BF16),
         ),
-        (in_vmem(near), in_vmem(far), w_one, w_two),
-        (VMEM,) * 4,
-        (VMEM,) * 4,
+        (in_vmem(near), in_vmem(far), w_one, in_hbm(w_out[0])),
+        (VMEM,) * 5,
+        (VMEM, VMEM, VMEM, HBM),
         [
             pltpu.VMEM((2 * chips, rows, extra), F32),
             pltpu.VMEM((chips, rows, main), F32),
+            pltpu.SemaphoreType.DMA((5,)),
         ],
         (12 * half * weight, 4 * weight),
     )
+    w_two = in_vmem(w_two)
     received = swap_cores(other)
     own = call(
         functools.partial(own_kernel, images),

time: 47.9 us -> 48.8 us (1.019)
  Pallas kernels: 13.7 us -> 15.5 us
  waiting for transfers between devices: 5.12 us -> 3.56 us
    pallas_call x8 -> x9, Pallas kernels: 13.7 us -> 15.5 us  [call(): pl.pallas_call(kernel, out_shape=outs, in_specs=in_specs, out_specs=out_s...]
    ppermute x2, waiting for transfers between devices: 1.71 us -> 0.15 us  [swap_cores(): lax.ppermute(block, 'expert', [(device, device ^ 1) for device in range(c...]
  transfers between devices with their start and end apart: 3 -> 3, of which waited for: 3 -> 2; matrix products, arithmetic and copies ran while one was open for 0% -> 0% of each run, Pallas kernels for 9% -> 12%
where the time goes in v7:
time: 48.8 us; the launch traced here: 48.5 us
  blocking collectives  24.6 us (50%)
  Pallas kernels  15.5 us (32%)
  starting transfers between devices  4.08 us (8%)
  waiting for transfers between devices  3.56 us (7%)
  between operations  0.7 us (1%)
    all_to_all x2, blocking collectives, swap_chips(): lax.all_to_all(blocks, 'expert', split_axis=0, concat_axis=0, axis_index_...  24.6 us
    pallas_call x9, Pallas kernels, call(): pl.pallas_call(kernel, out_shape=outs, in_specs=in_specs, out_specs=out_s...  15.5 us
    all_to_all x1, starting transfers between devices, per_device(): lax.all_to_all(terms, 'expert', split_axis=0, concat_axis=0, tiled=True)  3.5 us
    all_to_all x1, waiting for transfers between devices, per_device(): lax.all_to_all(terms, 'expert', split_axis=0, concat_axis=0, tiled=True)  3.41 us
  transfers between devices with their start and end apart: 3, of which 2 were waited for; matrix products, arithmetic and copies ran while one was open for 0% of the time, Pallas kernels for 12%

profile of v7, /device:TPU:0, one launch (start us, length us, event | category | flops | bytes accessed | tf_op | source)
XLA Modules:
  0.0 48.5 jit_solution(7485732005272324395)
XLA Ops:
  0.6 3.5 %shard_map.84 = (bf16[8,8,1024]{2,1,0:T(8,128)(2,1)S(1)}, bf16[3,256,1280]{2,1,0:T(8,128)(2,1)S(1)}, bf16[3,256,1280]{2,1,0:T(8,128)(2,1)S(1)}, f32[3,2,256]{2,1,0:T(2,128)S(1)}, f32[3,2,256]{2,1,0:T(2,128)S(1)}) custom-call(bf16[3,256,1280]{2,1,0:T(8,128)(2,1)} %tokens.1, bf16[2,1280]{1,0:T(2,128)(2,1)} %bitcast.6, bf16[3,256,1280]{2,1,0:T(8,128)(2,1)} %d_out.1), custom_call_target="tpu_custom_call" | custom-call | flops 11796480 | bytes 3932160 | tf_op jit(solution)/shard_map/pallas_call | solution.py:38
  4.2 14.4 %all_to_all.15._.near = bf16[8,8,1024]{2,1,0:T(8,128)(2,1)S(1)} all-to-all(bf16[8,8,1024]{2,1,0:T(8,128)(2,1)S(1)} %get-tuple-element.19), channel_id=1, replica_groups={{0,2,4,6,8,10,12,14},{1,3,5,7,9,11,13,15},{16,18,20,22,24,26,28,30},{17..., dimensions={0} | all-to-all | bytes 262144 | tf_op jit(solution)/shard_map/all_to_all | solution.py:334
  18.6 0.0 collective-permute-start
  18.6 1.4 %shard_map.85.w_in = bf16[1280,640]{1,0:T(8,128)(2,1)S(1)} custom-call(bf16[1280,640]{1,0:T(8,128)(2,1)} %bitcast.9, bf16[8,8,1024]{2,1,0:T(8,128)(2,1)S(1)} %all_to_all.15._.near), custom_call_target="tpu_custom_call" | custom-call | bytes 3276800 | tf_op jit(solution)/shard_map/pallas_call | solution.py:38
  20.0 0.0 collective-permute-done.far
  20.0 3.1 %shard_map.86 = (bf16[8,8,1024]{2,1,0:T(8,128)(2,1)S(1)}, bf16[128,1280]{1,0:T(8,128)(2,1)S(1)}, bf16[128,640]{1,0:T(8,128)(2,1)S(1)}, bf16[128,640]{1,0:T(8,128)(2,1)S(1)}, bf16[640,1280]{1,0:T(8,128)(2,1)S(1)}) custom-call(bf16[8,8,1024]{2,1,0:T(8,128)(2,1)S(1)} %all_to_all.15._.near, bf16[8,8,1024]{2,1,0:T(8,128)(2,1)S(1)} %collective-permute-done.far, ...), custom_call_target="tpu_custom_call" | custom-call | flops 629145600 | bytes 3276800 | tf_op jit(solution)/shard_map/pallas_call | solution.py:38
  23.2 0.6 %collective-permute-start.1 = (bf16[8,8,1024]{2,1,0:T(8,128)(2,1)S(1)}, bf16[8,8,1024]{2,1,0:T(8,128)(2,1)S(1)}, u32[]{:S(2)}, u32[]{:S(2)}) collective-permute-start(bf16[8,8,1024]{2,1,0:T(8,128)(2,1)S(1)} %get-tuple-element.23), channel_id=1, source_target_pairs={{0,1},{1,0},{2,3},{3,2},{4,5},{5,4},{6,7},{7,6},{8,9},{9,8},{10,11... | collective-permute-start | bytes 393224 | tf_op jit(solution)/shard_map/ppermute | solution.py:341
  23.7 0.0 copy-start
  23.7 0.8 %shard_map.87.own = f32[8,8,1024]{2,1,0:T(8,128)S(1)} custom-call(bf16[128,640]{1,0:T(8,128)(2,1)S(1)} %get-tuple-element.20.hid, bf16[128,640]{1,0:T(8,128)(2,1)S(1)} %get-tuple-element.21.grad, bf16[1280,640]{1,0:T(8,128)(2,1)S(1)} %shard_map.85.w_in, bf16[640,1280]{1,0:T(8,128)(2,1)S(1)} %get-tuple-element.22.w_out), custom_call_target="tpu_custom_call" | custom-call | flops 209715200 | bytes 3276800 | tf_op jit(solution)/shard_map/pallas_call | solution.py:38
  24.6 0.1 collective-permute-done.1.received
  24.7 10.2 %all_to_all.16.shares = bf16[8,8,1024]{2,1,0:T(8,128)(2,1)S(1)} all-to-all(bf16[8,8,1024]{2,1,0:T(8,128)(2,1)S(1)} %shard_map.88), channel_id=1, replica_groups={{0,2,4,6,8,10,12,14},{1,3,5,7,9,11,13,15},{16,18,20,22,24,26,28,30},{17..., dimensions={0} | all-to-all | bytes 262144 | tf_op jit(solution)/shard_map/all_to_all | solution.py:334
  34.9 0.0 copy-done
  34.9 2.3 %shard_map.89 = (bf16[16,2,1280]{2,1,0:T(2,128)(2,1)}, f32[3,4,256]{2,1,0:T(4,128)S(1)}, f32[3,4,1280]{2,1,0:T(4,128)S(1)}) custom-call(bf16[8,8,1024]{2,1,0:T(8,128)(2,1)S(1)} %all_to_all.16.shares, bf16[3,256,1280]{2,1,0:T(8,128)(2,1)S(1)} %get-tuple-element.24.tok, bf16[3,256,1280]{2,1,0:T(8,128)(2,1)S(1)} %get-tuple-element.25.dout, ...), custom_call_target="tpu_custom_call" | custom-call | flops 11796480 | bytes 3932160 | tf_op jit(solution)/shard_map/pallas_call | solution.py:38
  37.2 3.5 %all-to-all-start.2 = ((bf16[16,2,1280]{2,1,0:T(2,128)(2,1)}), bf16[16,2,1280]{2,1,0:T(2,128)(2,1)S(1)}, u32[]{:S(2)}, u32[]{:S(2)}) async-start(bf16[16,2,1280]{2,1,0:T(2,128)(2,1)} %get-tuple-element.33), calls=%async_computation.2 | async-start | bytes 163840 | tf_op jit(solution)/shard_map/all_to_all | solution.py:467
  40.7 2.1 %shard_map.91 = (bf16[1280,640]{1,0:T(8,128)(2,1)}, bf16[640,1280]{1,0:T(8,128)(2,1)}) custom-call(bf16[128,1280]{1,0:T(8,128)(2,1)S(1)} %get-tuple-element.30.x, bf16[128,640]{1,0:T(8,128)(2,1)S(1)} %get-tuple-element.20.hid, bf16[128,640]{1,0:T(8,128)(2,1)S(1)} %get-tuple-element.21.grad), custom_call_target="tpu_custom_call" | custom-call | flops 419430400 | bytes 3276800 | tf_op jit(solution)/shard_map/pallas_call | solution.py:38
  42.8 1.6 %shard_map.90 = bf16[3,256,1280]{2,1,0:T(8,128)(2,1)} custom-call(f32[3,4,256]{2,1,0:T(4,128)S(1)} %get-tuple-element.28.left, f32[3,4,1280]{2,1,0:T(4,128)S(1)} %get-tuple-element.29.right), custom_call_target="tpu_custom_call" | custom-call | flops 7864320 | bytes 1966080 | tf_op jit(solution)/shard_map/pallas_call | solution.py:38
  44.4 3.4 %all-to-all-done.2.terms = bf16[16,2,1280]{2,1,0:T(2,128)(2,1)S(1)} async-done(((bf16[16,2,1280]{2,1,0:T(2,128)(2,1)}), bf16[16,2,1280]{2,1,0:T(2,128)(2,1)S(1)}, u32[]{:S(2)}, u32[]{:S(2)}) %all-to-all-start.2) | async-done | bytes 81952 | tf_op jit(solution)/shard_map/all_to_all | solution.py:467
  47.8 0.7 %shard_map.92 = f32[2,1280]{1,0:T(2,128)} custom-call(bf16[16,2,1280]{2,1,0:T(2,128)(2,1)S(1)} %all-to-all-done.2.terms), custom_call_target="tpu_custom_call" | custom-call | flops 40960 | bytes 81920 | tf_op jit(solution)/shard_map/pallas_call | solution.py:38
  (1 shorter events, 0.0 us)
Async XLA Ops:
  18.6 1.4 %collective-permute-start = (bf16[8,8,1024]{2,1,0:T(8,128)(2,1)S(1)}, bf16[8,8,1024]{2,1,0:T(8,128)(2,1)S(1)}, u32[]{:S(2)}, u32[]{:S(2)}) collective-permute-start(bf16[8,8,1024]{2,1,0:T(8,128)(2,1)S(1)} %all_to_all.15._.near), channel_id=1, source_target_pairs={{0,1},{1,0},{2,3},{3,2},{4,5},{5,4},{6,7},{7,6},{8,9},{9,8},{10,11... | collective-permute-start | bytes 393224 | tf_op jit(solution)/shard_map/ppermute | solution.py:341
  23.2 1.6 %collective-permute-start.1 = (bf16[8,8,1024]{2,1,0:T(8,128)(2,1)S(1)}, bf16[8,8,1024]{2,1,0:T(8,128)(2,1)S(1)}, u32[]{:S(2)}, u32[]{:S(2)}) collective-permute-start(bf16[8,8,1024]{2,1,0:T(8,128)(2,1)S(1)} %get-tuple-element.23), channel_id=1, source_target_pairs={{0,1},{1,0},{2,3},{3,2},{4,5},{5,4},{6,7},{7,6},{8,9},{9,8},{10,11... | collective-permute-start | bytes 393224 | tf_op jit(solution)/shard_map/ppermute | solution.py:341
  23.7 11.2 %copy-start = (bf16[1280,2]{0,1:T(2,128)(2,1)S(1)}, bf16[1280,2]{0,1:T(2,128)(2,1)}, u32[]{:S(2)}) copy-start(bf16[1280,2]{0,1:T(2,128)(2,1)} %param.6) | copy-start | bytes 15364
  37.2 10.6 %all-to-all-start.2 = ((bf16[16,2,1280]{2,1,0:T(2,128)(2,1)}), bf16[16,2,1280]{2,1,0:T(2,128)(2,1)S(1)}, u32[]{:S(2)}, u32[]{:S(2)}) async-start(bf16[16,2,1280]{2,1,0:T(2,128)(2,1)} %get-tuple-element.33), calls=%async_computation.2 | async-start | bytes 163840 | tf_op jit(solution)/shard_map/all_to_all | solution.py:467

commit v8 on v6

--- a/solution.py
+++ b/solution.py
@@ -82,21 +82,18 @@
     router_hbm,
     d_out,
     w_in,
-    w_out,
     send,
     tok,
     dout,
     disp_out,
     comb_out,
     w_one,
-    w_two,
     router_t,
     block,
     sems,
     other_sems,
 ):
     images = tok.shape[0]
-    slots = router_t.shape[0]
     main = send.shape[2]
     extra = tok.shape[2] - main
     fetch_router = pltpu.make_async_copy(router_hbm, router_t, other_sems.at[0])
@@ -107,10 +104,7 @@
     fetch_dout = [
         pltpu.make_async_copy(d_out.at[b], dout.at[b], sems.at[images + b]) for b in range(images)
     ]
-    fetch_weights = [
-        pltpu.make_async_copy(w_in, w_one, other_sems.at[1]),
-        pltpu.make_async_copy(w_out, w_two, other_sems.at[2]),
-    ]
+    fetch_weight = pltpu.make_async_copy(w_in, w_one, other_sems.at[1])
     for copy in fetch_tok:
         copy.start()
     block[...] = jnp.zeros_like(block)
@@ -121,35 +115,55 @@
         block[:, to, column : column + extra] = values[:, main:]
 
     fetch_router.wait()
-    logits = []
-    for b in range(images):
-        fetch_tok[b].wait()
-        if b == 0:
-            for copy in fetch_dout:
-                copy.start()
-        if b == images - 1:
-            for copy in fetch_weights:
-                copy.start()
-        logits.append(dot(router_t[...], tok[b], NT))
-    disps = []
-    combs = []
-    for b in range(images):
+    logits = {}
+    combs = {}
+    disps = {}
+
+    def softmaxes(b):
         exps = jnp.exp(logits[b] - jnp.max(logits[b], axis=1, keepdims=True))
-        disps.append(exps * (1.0 / jnp.sum(exps, axis=1, keepdims=True)))
+        disp = exps * (1.0 / jnp.sum(exps, axis=1, keepdims=True))
         exps = jnp.exp(logits[b] - jnp.max(logits[b], axis=0, keepdims=True))
-        combs.append(exps * (1.0 / jnp.sum(exps, axis=0, keepdims=True)))
-        disp_out[b] = disps[b]
-        comb_out[b] = combs[b]
-    for b in range(images):
-        put(b, dot(disps[b].astype(BF16), tok[b]))
+        comb = exps * (1.0 / jnp.sum(exps, axis=0, keepdims=True))
+        disp_out[b] = disp
+        comb_out[b] = comb
+        disps[b] = disp.astype(BF16)
+        combs[b] = comb.astype(BF16)
+
+    for step in range(images + 2):
+        if step < images:
+            fetch_tok[step].wait()
+            if step == 0:
+                for copy in fetch_dout:
+                    copy.start()
+            if step == min(1, images - 1):
+                fetch_weight.start()
+            logits[step] = dot(router_t[...], tok[step], NT)
+        if 0 <= step - 1 < images:
+            softmaxes(step - 1)
+        if 0 <= step - 2 < images:
+            put(step - 2, dot(disps[step - 2], tok[step - 2]))
     for b in range(images):
         fetch_dout[b].wait()
-        put(images + b, dot(combs[b].astype(BF16), dout[b]))
-    for slot in range(slots):
+        put(images + b, dot(combs[b], dout[b]))
+    for slot in range(block.shape[0]):
         rows = block[slot].astype(BF16)
         for chip in range(split_chips):
             send[slot * split_chips + chip] = rows
-    for copy in fetch_weights:
+    fetch_weight.wait()
+
+
+def fetch_kernel(source, _, target, sems):
+    parts = sems.shape[0]
+    step = source.shape[0] // parts
+    copies = [
+        pltpu.make_async_copy(
+            source.at[pl.ds(i * step, step)], target.at[pl.ds(i * step, step)], sems.at[i]
+        )
+        for i in range(parts)
+    ]
+    for copy in copies:
+        copy.start()
+    for copy in copies:
         copy.wait()
 
 
@@ -327,7 +341,7 @@
     big = images * count * width
     weight = width * hidden_units
 
-    send, tok, dout, disp, comb, w_one, w_two = call(
+    send, tok, dout, disp, comb, w_one = call(
         functools.partial(rows_kernel, split_chips),
         (
             vmem_out((chips, rows, main), BF16),
@@ -336,22 +350,30 @@
             vmem_out((images, slots, count), F32),
             vmem_out((images, slots, count), F32),
             vmem_out(w_in.shape[1:], BF16),
-            vmem_out(w_out.shape[1:], BF16),
         ),
-        tuple(in_hbm(array) for array in (tokens, router_t, d_out, w_in[0], w_out[0])),
-        (VMEM,) * 7,
-        (HBM,) * 5,
+        tuple(in_hbm(array) for array in (tokens, router_t, d_out, w_in[0])),
+        (VMEM,) * 6,
+        (HBM,) * 4,
         [
             pltpu.VMEM((slots, width), BF16),
             pltpu.VMEM((slots, rows, main), F32),
             pltpu.SemaphoreType.DMA((2 * images,)),
-            pltpu.SemaphoreType.DMA((3,)),
+            pltpu.SemaphoreType.DMA((2,)),
         ],
         (6 * slots * big, 4 * big),
     )
-    w_one, w_two = in_vmem(w_one), in_vmem(w_two)
     near = swap_chips(send)
     far = swap_cores(near)
+    w_two = call(
+        fetch_kernel,
+        vmem_out(w_out.shape[1:], BF16),
+        (in_hbm(w_out[0]), in_vmem(near)),
+        VMEM,
+        (HBM, VMEM),
+        [pltpu.SemaphoreType.DMA((5,))],
+        (0, 4 * weight),
+    )
+    w_one, w_two = in_vmem(w_one), in_vmem(w_two)
     other, x, hid, grad = call(
         functools.partial(experts_kernel, images),
         (

time: 47.8 us -> 47.6 us (level)
  waiting for transfers between devices: 5.12 us -> 3.56 us
  Pallas kernels: 13.6 us -> 14.4 us
    ppermute x2, waiting for transfers between devices: 1.71 us -> 0.15 us  [swap_cores(): lax.ppermute(block, 'expert', [(device, device ^ 1) for device in range(c...]
    pallas_call x8 -> x9, Pallas kernels: 13.6 us -> 14.4 us  [call(): pl.pallas_call(kernel, out_shape=outs, in_specs=in_specs, out_specs=out_s...]
  transfers between devices with their start and end apart: 3 -> 3, of which waited for: 3 -> 2; matrix products, arithmetic and copies ran while one was open for 0% -> 0% of each run, Pallas kernels for 9% -> 13%
where the time goes in v8:
time: 47.6 us; the launch traced here: 47.3 us
  blocking collectives  24.6 us (52%)
  Pallas kernels  14.4 us (30%)
  starting transfers between devices  4.07 us (9%)
  waiting for transfers between devices  3.56 us (7%)
  between operations  0.7 us (1%)
    all_to_all x2, blocking collectives, swap_chips(): lax.all_to_all(blocks, 'expert', split_axis=0, concat_axis=0, axis_index_...  24.6 us
    pallas_call x9, Pallas kernels, call(): pl.pallas_call(kernel, out_shape=outs, in_specs=in_specs, out_specs=out_s...  14.4 us
    all_to_all x1, starting transfers between devices, per_device(): lax.all_to_all(terms, 'expert', split_axis=0, concat_axis=0, tiled=True)  3.5 us
    all_to_all x1, waiting for transfers between devices, per_device(): lax.all_to_all(terms, 'expert', split_axis=0, concat_axis=0, tiled=True)  3.41 us
  transfers between devices with their start and end apart: 3, of which 2 were waited for; matrix products, arithmetic and copies ran while one was open for 0% of the time, Pallas kernels for 13%

profile of v8, /device:TPU:0, one launch (start us, length us, event | category | flops | bytes accessed | tf_op | source)
XLA Modules:
  0.0 47.3 jit_solution(12903919994356838440)
XLA Ops:
  0.6 3.5 %shard_map.84 = (bf16[8,8,1024]{2,1,0:T(8,128)(2,1)S(1)}, bf16[3,256,1280]{2,1,0:T(8,128)(2,1)S(1)}, bf16[3,256,1280]{2,1,0:T(8,128)(2,1)S(1)}, f32[3,2,256]{2,1...) custom-call(bf16[3,256,1280]{2,1,0:T(8,128)(2,1)} %tokens.1, bf16[2,1280]{1,0:T(2,128)(2,1)} %bitcast.6, ...), custom_call_target="tpu_custom_call" | custom-call | flops 11796480 | bytes 3932160 | tf_op jit(solution)/shard_map/pallas_call | solution.py:38
  4.2 14.4 %all_to_all.15._.near = bf16[8,8,1024]{2,1,0:T(8,128)(2,1)S(1)} all-to-all(bf16[8,8,1024]{2,1,0:T(8,128)(2,1)S(1)} %get-tuple-element.19), channel_id=1, replica_groups={{0,2,4,6,8,10,12,14},{1,3,5,7,9,11,13,15},{16,18,20,22,24,26,28,30},{17..., dimensions={0} | all-to-all | bytes 262144 | tf_op jit(solution)/shard_map/all_to_all | solution.py:321
  18.6 0.0 collective-permute-start
  18.6 1.4 %shard_map.85.w_out = bf16[640,1280]{1,0:T(8,128)(2,1)S(1)} custom-call(bf16[640,1280]{1,0:T(8,128)(2,1)} %bitcast.8, bf16[8,8,1024]{2,1,0:T(8,128)(2,1)S(1)} %all_to_all.15._.near), custom_call_target="tpu_custom_call" | custom-call | bytes 3276800 | tf_op jit(solution)/shard_map/pallas_call | solution.py:38
  20.0 0.0 collective-permute-done.far
  20.0 1.9 %shard_map.86 = (bf16[8,8,1024]{2,1,0:T(8,128)(2,1)S(1)}, bf16[128,1280]{1,0:T(8,128)(2,1)S(1)}, bf16[128,640]{1,0:T(8,128)(2,1)S(1)}, bf16[128,640]{1,0:T(8,128)(2,1)S(1)}) custom-call(bf16[8,8,1024]{2,1,0:T(8,128)(2,1)S(1)} %all_to_all.15._.near, bf16[8,8,1024]{2,1,0:T(8,128)(2,1)S(1)} %collective-permute-done.far, ...), custom_call_target="tpu_custom_call" | custom-call | flops 629145600 | bytes 3276800 | tf_op jit(solution)/shard_map/pallas_call | solution.py:38
  22.0 0.6 %collective-permute-start.1 = (bf16[8,8,1024]{2,1,0:T(8,128)(2,1)S(1)}, bf16[8,8,1024]{2,1,0:T(8,128)(2,1)S(1)}, u32[]{:S(2)}, u32[]{:S(2)}) collective-permute-start(bf16[8,8,1024]{2,1,0:T(8,128)(2,1)S(1)} %get-tuple-element.23), channel_id=1, source_target_pairs={{0,1},{1,0},{2,3},{3,2},{4,5},{5,4},{6,7},{7,6},{8,9},{9,8},{10,11... | collective-permute-start | bytes 393224 | tf_op jit(solution)/shard_map/ppermute | solution.py:328
  22.5 0.0 copy-start
  22.6 0.8 %shard_map.87.own = f32[8,8,1024]{2,1,0:T(8,128)S(1)} custom-call(bf16[128,640]{1,0:T(8,128)(2,1)S(1)} %get-tuple-element.21.hid, bf16[128,640]{1,0:T(8,128)(2,1)S(1)} %get-tuple-element.22.grad, bf16[1280,640]{1,0:T(8,128)(2,1)S(1)} %get-tuple-element.20.w_in, bf16[640,1280]{1,0:T(8,128)(2,1)S(1)} %shard_map.85.w_out), custom_call_target="tpu_custom_call" | custom-call | flops 209715200 | bytes 3276800 | tf_op jit(solution)/shard_map/pallas_call | solution.py:38
  23.4 0.1 collective-permute-done.1.received
  23.6 10.2 %all_to_all.16.shares = bf16[8,8,1024]{2,1,0:T(8,128)(2,1)S(1)} all-to-all(bf16[8,8,1024]{2,1,0:T(8,128)(2,1)S(1)} %shard_map.88), channel_id=1, replica_groups={{0,2,4,6,8,10,12,14},{1,3,5,7,9,11,13,15},{16,18,20,22,24,26,28,30},{17..., dimensions={0} | all-to-all | bytes 262144 | tf_op jit(solution)/shard_map/all_to_all | solution.py:321
  33.7 0.0 copy-done
  33.8 2.3 %shard_map.89 = (bf16[16,2,1280]{2,1,0:T(2,128)(2,1)}, f32[3,4,256]{2,1,0:T(4,128)S(1)}, f32[3,4,1280]{2,1,0:T(4,128)S(1)}) custom-call(bf16[8,8,1024]{2,1,0:T(8,128)(2,1)S(1)} %all_to_all.16.shares, bf16[3,256,1280]{2,1,0:T(8,128)(2,1)S(1)} %get-tuple-element.24.tok, bf16[3,256,1280]{2,1,0:T(8,128)(2,1)S(1)} %get-tuple-element.25.dout, ...), custom_call_target="tpu_custom_call" | custom-call | flops 11796480 | bytes 3932160 | tf_op jit(solution)/shard_map/pallas_call | solution.py:38
  36.0 3.5 %all-to-all-start.2 = ((bf16[16,2,1280]{2,1,0:T(2,128)(2,1)}), bf16[16,2,1280]{2,1,0:T(2,128)(2,1)S(1)}, u32[]{:S(2)}, u32[]{:S(2)}) async-start(bf16[16,2,1280]{2,1,0:T(2,128)(2,1)} %get-tuple-element.33), calls=%async_computation.2 | async-start | bytes 163840 | tf_op jit(solution)/shard_map/all_to_all | solution.py:452
  39.5 2.1 %shard_map.91 = (bf16[1280,640]{1,0:T(8,128)(2,1)}, bf16[640,1280]{1,0:T(8,128)(2,1)}) custom-call(bf16[128,1280]{1,0:T(8,128)(2,1)S(1)} %get-tuple-element.30.x, bf16[128,640]{1,0:T(8,128)(2,1)S(1)} %get-tuple-element.21.hid, bf16[128,640]{1,0:T(8,128)(2,1)S(1)} %get-tuple-element.22.grad), custom_call_target="tpu_custom_call" | custom-call | flops 419430400 | bytes 3276800 | tf_op jit(solution)/shard_map/pallas_call | solution.py:38
  41.6 1.6 %shard_map.90 = bf16[3,256,1280]{2,1,0:T(8,128)(2,1)} custom-call(f32[3,4,256]{2,1,0:T(4,128)S(1)} %get-tuple-element.28.left, f32[3,4,1280]{2,1,0:T(4,128)S(1)} %get-tuple-element.29.right), custom_call_target="tpu_custom_call" | custom-call | flops 7864320 | bytes 1966080 | tf_op jit(solution)/shard_map/pallas_call | solution.py:38
  43.2 3.4 %all-to-all-done.2.terms = bf16[16,2,1280]{2,1,0:T(2,128)(2,1)S(1)} async-done(((bf16[16,2,1280]{2,1,0:T(2,128)(2,1)}), bf16[16,2,1280]{2,1,0:T(2,128)(2,1)S(1)}, u32[]{:S(2)}, u32[]{:S(2)}) %all-to-all-start.2) | async-done | bytes 81952 | tf_op jit(solution)/shard_map/all_to_all | solution.py:452
  46.6 0.7 %shard_map.92 = f32[2,1280]{1,0:T(2,128)} custom-call(bf16[16,2,1280]{2,1,0:T(2,128)(2,1)S(1)} %all-to-all-done.2.terms), custom_call_target="tpu_custom_call" | custom-call | flops 40960 | bytes 81920 | tf_op jit(solution)/shard_map/pallas_call | solution.py:38
  (1 shorter events, 0.0 us)
Async XLA Ops:
  18.6 1.4 %collective-permute-start = (bf16[8,8,1024]{2,1,0:T(8,128)(2,1)S(1)}, bf16[8,8,1024]{2,1,0:T(8,128)(2,1)S(1)}, u32[]{:S(2)}, u32[]{:S(2)}) collective-permute-start(bf16[8,8,1024]{2,1,0:T(8,128)(2,1)S(1)} %all_to_all.15._.near), channel_id=1, source_target_pairs={{0,1},{1,0},{2,3},{3,2},{4,5},{5,4},{6,7},{7,6},{8,9},{9,8},{10,11... | collective-permute-start | bytes 393224 | tf_op jit(solution)/shard_map/ppermute | solution.py:328
  22.0 1.6 %collective-permute-start.1 = (bf16[8,8,1024]{2,1,0:T(8,128)(2,1)S(1)}, bf16[8,8,1024]{2,1,0:T(8,128)(2,1)S(1)}, u32[]{:S(2)}, u32[]{:S(2)}) collective-permute-start(bf16[8,8,1024]{2,1,0:T(8,128)(2,1)S(1)} %get-tuple-element.23), channel_id=1, source_target_pairs={{0,1},{1,0},{2,3},{3,2},{4,5},{5,4},{6,7},{7,6},{8,9},{9,8},{10,11... | collective-permute-start | bytes 393224 | tf_op jit(solution)/shard_map/ppermute | solution.py:328
  22.5 11.2 %copy-start = (bf16[1280,2]{0,1:T(2,128)(2,1)S(1)}, bf16[1280,2]{0,1:T(2,128)(2,1)}, u32[]{:S(2)}) copy-start(bf16[1280,2]{0,1:T(2,128)(2,1)} %param.6) | copy-start | bytes 15364
  36.0 10.6 %all-to-all-start.2 = ((bf16[16,2,1280]{2,1,0:T(2,128)(2,1)}), bf16[16,2,1280]{2,1,0:T(2,128)(2,1)S(1)}, u32[]{:S(2)}, u32[]{:S(2)}) async-start(bf16[16,2,1280]{2,1,0:T(2,128)(2,1)} %get-tuple-element.33), calls=%async_computation.2 | async-start | bytes 163840 | tf_op jit(solution)/shard_map/all_to_all | solution.py:452

commit v9 on v8

--- a/solution.py
+++ b/solution.py
@@ -77,24 +77,21 @@
 
 
 def rows_kernel(
-    split_chips,
     tokens,
     router_hbm,
     d_out,
-    w_in,
-    send,
+    rows_out,
     tok,
     dout,
     disp_out,
     comb_out,
-    w_one,
     router_t,
     block,
     sems,
     other_sems,
 ):
     images = tok.shape[0]
-    main = send.shape[2]
+    main = rows_out.shape[2]
     extra = tok.shape[2] - main
     fetch_router = pltpu.make_async_copy(router_hbm, router_t, other_sems.at[0])
     fetch_router.start()
@@ -104,7 +101,6 @@
     fetch_dout = [
         pltpu.make_async_copy(d_out.at[b], dout.at[b], sems.at[images + b]) for b in range(images)
     ]
-    fetch_weight = pltpu.make_async_copy(w_in, w_one, other_sems.at[1])
     for copy in fetch_tok:
         copy.start()
     block[...] = jnp.zeros_like(block)
@@ -135,8 +131,6 @@
             if step == 0:
                 for copy in fetch_dout:
                     copy.start()
-            if step == min(1, images - 1):
-                fetch_weight.start()
             logits[step] = dot(router_t[...], tok[step], NT)
         if 0 <= step - 1 < images:
             softmaxes(step - 1)
@@ -145,40 +139,24 @@
     for b in range(images):
         fetch_dout[b].wait()
         put(images + b, dot(combs[b], dout[b]))
-    for slot in range(block.shape[0]):
-        rows = block[slot].astype(BF16)
+    rows_out[...] = block[...].astype(BF16)
+
+
+def repeat_kernel(split_chips, rows, tok, dout, send):
+    for slot in range(rows.shape[0]):
         for chip in range(split_chips):
-            send[slot * split_chips + chip] = rows
-    fetch_weight.wait()
-
-
-def fetch_kernel(source, _, target, sems):
-    parts = sems.shape[0]
-    step = source.shape[0] // parts
-    copies = [
-        pltpu.make_async_copy(
-            source.at[pl.ds(i * step, step)], target.at[pl.ds(i * step, step)], sems.at[i]
-        )
-        for i in range(parts)
-    ]
-    for copy in copies:
-        copy.start()
-    for copy in copies:
-        copy.wait()
-
-
-def experts_kernel(images, near, far, w_in, w_out, other, x_out, hid_out, grad_out, ends, packed):
-    chips, rows, main = near.shape
+            send[slot * split_chips + chip] = rows[slot]
+
+
+def hidden_rows(images, blocks, w_in, w_out, x_out, hid_out, grad_out, ends):
+    chips, rows, main = blocks.shape
     half = chips * rows
     width = x_out.shape[1]
-    for i, blocks in enumerate((near, far)):
-        unpack(images, ends.at[pl.ds(i * chips, chips)], blocks[...].astype(F32))
+    unpack(images, ends, blocks[...].astype(F32))
     x = jnp.concatenate(
         [
-            jnp.concatenate(
-                [near[...].reshape(half, main), far[...].reshape(half, main)], axis=0
-            ),
-            ends[...].reshape(2 * half, width - main).astype(BF16),
+            blocks[...].reshape(half, main),
+            ends[...].reshape(half, width - main).astype(BF16),
         ],
         axis=1,
     )
@@ -187,7 +165,7 @@
     grad_hidden = dot(x, w_out[...], NT)
     place = lax.broadcasted_iota(jnp.int32, pre.shape, 0) % rows
     slot_row = place < images
-    grad_hidden = pltpu.roll(grad_hidden, 2 * half - images, 0)
+    grad_hidden = pltpu.roll(grad_hidden, half - images, 0)
     scale = 0.7978845608028654
     square = pre * pre
     tanh = jnp.tanh(scale * pre * (1.0 + 0.044715 * square))
@@ -198,15 +176,23 @@
     grad_low = pltpu.roll(grad_pre, images, 0).astype(BF16)
     hid_out[...] = hidden
     grad_out[...] = grad_low
-    shares = dot(hidden[half:], w_out[...]) + dot(grad_low[half:], w_in[...], NT)
-    pack(images, packed, shares.reshape(chips, rows, width))
+    return hidden, grad_low
+
+
+def near_kernel(images, blocks, w_in, w_out, x_out, hid_out, grad_out, ends):
+    hidden_rows(images, blocks, w_in, w_out, x_out, hid_out, grad_out, ends)
+
+
+def far_kernel(images, blocks, w_in, w_out, _, other, x_out, hid_out, grad_out, ends, packed):
+    hidden, grad_low = hidden_rows(images, blocks, w_in, w_out, x_out, hid_out, grad_out, ends)
+    shares = dot(hidden, w_out[...]) + dot(grad_low, w_in[...], NT)
+    pack(images, packed, shares.reshape(blocks.shape[:2] + (shares.shape[1],)))
     other[...] = packed[...].astype(BF16)
 
 
 def own_kernel(images, hid, grad, w_in, w_out, own):
     chips, rows, _ = own.shape
-    half = chips * rows
-    shares = dot(hid[:half], w_out[...]) + dot(grad[:half], w_in[...], NT)
+    shares = dot(hid[...], w_out[...]) + dot(grad[...], w_in[...], NT)
     pack(images, own, shares.reshape(chips, rows, shares.shape[1]))
 
 
@@ -214,16 +200,32 @@
     total[...] = (own[...] + received[...].astype(F32)).astype(BF16)
 
 
-def weights_kernel(images, x, hid, grad, g_in, g_out, buf_in, buf_out, sem_in, sem_out):
+def weights_kernel(
+    images,
+    x_near,
+    hid_near,
+    grad_near,
+    x_far,
+    hid_far,
+    grad_far,
+    g_in,
+    g_out,
+    buf_in,
+    buf_out,
+    sem_in,
+    sem_out,
+):
     parts = buf_in.shape[0]
     step_in = g_in.shape[0] // parts
     step_out = g_out.shape[0] // parts
-    count = x.shape[0]
-    hid_low = pltpu.roll(hid[...].astype(F32), images, 0).astype(BF16)
-    grad_high = pltpu.roll(grad[...].astype(F32), count - images, 0).astype(BF16)
+    x = jnp.concatenate([x_near[...], x_far[...]], axis=0)
+    hid = jnp.concatenate([hid_near[...], hid_far[...]], axis=0)
+    grad = jnp.concatenate([grad_near[...], grad_far[...]], axis=0)
+    hid_low = pltpu.roll(hid.astype(F32), images, 0).astype(BF16)
+    grad_high = pltpu.roll(grad.astype(F32), x.shape[0] - images, 0).astype(BF16)
     copies = []
     for i in range(parts):
-        buf_out[i] = dot(hid_low[:, i * step_out : (i + 1) * step_out], x[...], TN).astype(BF16)
+        buf_out[i] = dot(hid_low[:, i * step_out : (i + 1) * step_out], x, TN).astype(BF16)
         copy = pltpu.make_async_copy(
             buf_out.at[i], g_out.at[pl.ds(i * step_out, step_out)], sem_out.at[i]
         )
@@ -341,19 +343,18 @@
     big = images * count * width
     weight = width * hidden_units
 
-    send, tok, dout, disp, comb, w_one = call(
-        functools.partial(rows_kernel, split_chips),
+    blocks, tok, dout, disp, comb = call(
+        rows_kernel,
         (
-            vmem_out((chips, rows, main), BF16),
+            vmem_out((slots, rows, main), BF16),
             vmem_out((images, count, width), BF16),
             vmem_out((images, count, width), BF16),
             vmem_out((images, slots, count), F32),
             vmem_out((images, slots, count), F32),
-            vmem_out(w_in.shape[1:], BF16),
         ),
-        tuple(in_hbm(array) for array in (tokens, router_t, d_out, w_in[0])),
-        (VMEM,) * 6,
-        (HBM,) * 4,
+        tuple(in_hbm(array) for array in (tokens, router_t, d_out)),
+        (VMEM,) * 5,
+        (HBM,) * 3,
         [
             pltpu.VMEM((slots, width), BF16),
             pltpu.VMEM((slots, rows, main), F32),
@@ -361,41 +362,53 @@
             pltpu.SemaphoreType.DMA((2,)),
         ],
         (6 * slots * big, 4 * big),
+        limit=56 * MIB,
+    )
+    send = call(
+        functools.partial(repeat_kernel, split_chips),
+        vmem_out((chips, rows, main), BF16),
+        (in_vmem(blocks), in_vmem(tok), in_vmem(dout)),
+        VMEM,
+        (VMEM,) * 3,
+        (),
+        (4 * half * weight, 40 * weight),
     )
     near = swap_chips(send)
     far = swap_cores(near)
-    w_two = call(
-        fetch_kernel,
-        vmem_out(w_out.shape[1:], BF16),
-        (in_hbm(w_out[0]), in_vmem(near)),
-        VMEM,
-        (HBM, VMEM),
-        [pltpu.SemaphoreType.DMA((5,))],
-        (0, 4 * weight),
-    )
-    w_one, w_two = in_vmem(w_one), in_vmem(w_two)
-    other, x, hid, grad = call(
-        functools.partial(experts_kernel, images),
-        (
-            vmem_out((chips, rows, main), BF16),
-            vmem_out((2 * half, width), BF16),
-            vmem_out((2 * half, hidden_units), BF16),
-            vmem_out((2 * half, hidden_units), BF16),
-        ),
-        (in_vmem(near), in_vmem(far), w_one, w_two),
+    w_one, w_two = in_vmem(w_in[0]), in_vmem(w_out[0])
+    inner = (
+        vmem_out((half, width), BF16),
+        vmem_out((half, hidden_units), BF16),
+        vmem_out((half, hidden_units), BF16),
+    )
+    hidden_near = call(
+        functools.partial(near_kernel, images),
+        inner,
+        (in_vmem(near), w_one, w_two),
+        (VMEM,) * 3,
+        (VMEM,) * 3,
+        [pltpu.VMEM((chips, rows, extra), F32)],
+        (4 * half * weight, 4 * weight),
+    )
+    hidden_near = [in_vmem(array) for array in hidden_near]
+    other, *hidden_far = call(
+        functools.partial(far_kernel, images),
+        (vmem_out((chips, rows, main), BF16),) + inner,
+        (in_vmem(far), w_one, w_two, hidden_near[1]),
         (VMEM,) * 4,
         (VMEM,) * 4,
         [
-            pltpu.VMEM((2 * chips, rows, extra), F32),
+            pltpu.VMEM((chips, rows, extra), F32),
             pltpu.VMEM((chips, rows, main), F32),
         ],
-        (12 * half * weight, 4 * weight),
-    )
+        (8 * half * weight, 4 * weight),
+    )
+    hidden_far = [in_vmem(array) for array in hidden_far]
     received = swap_cores(other)
     own = call(
         functools.partial(own_kernel, images),
         vmem_out((chips, rows, main), F32),
-        (in_vmem(hid), in_vmem(grad), w_one, w_two),
+        (hidden_near[1], hidden_near[2], w_one, w_two),
         VMEM,
         (VMEM,) * 4,
         (),
@@ -418,9 +431,9 @@
             jax.ShapeDtypeStruct((width, hidden_units), BF16),
             jax.ShapeDtypeStruct((hidden_units, width), BF16),
         ),
-        (in_vmem(x), in_vmem(hid), in_vmem(grad)),
+        (*hidden_near, *hidden_far),
         (HBM,) * 2,
-        (VMEM,) * 3,
+        (VMEM,) * 6,
         [
             pltpu.VMEM((parts, width // parts, hidden_units), BF16),
             pltpu.VMEM((parts, hidden_units // parts, width), BF16),

time: 47.6 us -> 47.3 us (level)
  Pallas kernels: 14.4 us -> 13.7 us
  waiting for transfers between devices: 3.56 us -> 4.2 us
    ppermute x2, waiting for transfers between devices: 0.15 us -> 0.82 us  [swap_cores(): lax.ppermute(block, 'expert', [(device, device ^ 1) for device in range(c...]
    pallas_call x9 -> x10, Pallas kernels: 14.4 us -> 13.7 us  [call(): pl.pallas_call(kernel, out_shape=outs, in_specs=in_specs, out_specs=out_s...]
  transfers between devices with their start and end apart: 3 -> 3, of which waited for: 2 -> 3; matrix products, arithmetic and copies ran while one was open for 0% -> 0% of each run, Pallas kernels for 13% -> 11%
where the time goes in v9:
time: 47.3 us; the launch traced here: 47.1 us
  blocking collectives  24.7 us (52%)
  Pallas kernels  13.7 us (29%)
  waiting for transfers between devices  4.2 us (9%)
  starting transfers between devices  3.72 us (8%)
  between operations  0.72 us (2%)
    all_to_all x2, blocking collectives, swap_chips(): lax.all_to_all(blocks, 'expert', split_axis=0, concat_axis=0, axis_index_...  24.7 us
    pallas_call x10, Pallas kernels, call(): pl.pallas_call(kernel, out_shape=outs, in_specs=in_specs, out_specs=out_s...  13.7 us
    all_to_all x1, starting transfers between devices, per_device(): lax.all_to_all(terms, 'expert', split_axis=0, concat_axis=0, tiled=True)  3.5 us
    all_to_all x1, waiting for transfers between devices, per_device(): lax.all_to_all(terms, 'expert', split_axis=0, concat_axis=0, tiled=True)  3.39 us
  transfers between devices with their start and end apart: 3, of which 3 were waited for; matrix products, arithmetic and copies ran while one was open for 0% of the time, Pallas kernels for 11%

profile of v9, /device:TPU:0, one launch (start us, length us, event | category | flops | bytes accessed | tf_op | source)
XLA Modules:
  0.0 47.1 jit_solution(6402517479567492734)
XLA Ops:
  0.6 3.5 %shard_map.84 = (bf16[2,8,1024]{2,1,0:T(8,128)(2,1)S(1)}, bf16[3,256,1280]{2,1,0:T(8,128)(2,1)S(1)}, bf16[3,256,1280]{2,1,0:T(8,128)(2,1)S(1)}, f32[3,2,256]{2,1,0:T(2,128)S(1)}, f32[3,2,256]{2,1,0:T(2,128)S(1)}) custom-call(bf16[3,256,1280]{2,1,0:T(8,128)(2,1)} %tokens.1, bf16[2,1280]{1,0:T(2,128)(2,1)} %bitcast.12, bf16[3,256,1280]{2,1,0:T(8,128)(2,1)} %d_out.1), custom_call_target="tpu_custom_call" | custom-call | flops 11796480 | bytes 3932160 | tf_op jit(solution)/shard_map/pallas_call | solution.py:38
  4.2 0.0 copy-start
  4.2 0.0 copy-start.1
  4.2 14.7 %all_to_all.15.blocks = bf16[8,8,1024]{2,1,0:T(8,128)(2,1)S(1)} all-to-all(bf16[8,8,1024]{2,1,0:T(8,128)(2,1)S(1)} %shard_map.85), channel_id=1, replica_groups={{0,2,4,6,8,10,12,14},{1,3,5,7,9,11,13,15},{16,18,20,22,24,26,28,30},{17..., dimensions={0} | all-to-all | bytes 262144 | tf_op jit(solution)/shard_map/all_to_all | solution.py:323
  18.9 0.0 collective-permute-start
  18.9 0.0 copy-done
  18.9 0.0 copy-done.1
  18.9 0.9 %shard_map.86 = (bf16[64,1280]{1,0:T(8,128)(2,1)S(1)}, bf16[64,640]{1,0:T(8,128)(2,1)S(1)}, bf16[64,640]{1,0:T(8,128)(2,1)S(1)}) custom-call(bf16[8,8,1024]{2,1,0:T(8,128)(2,1)S(1)} %all_to_all.15.blocks, bf16[1280,640]{1,0:T(8,128)(2,1)S(1)} %bitcast.6, bf16[640,1280]{1,0:T(8,128)(2,1)S(1)} %bitcast.9), custom_call_target="tpu_custom_call" | custom-call | flops 209715200 | bytes 3276800 | tf_op jit(solution)/shard_map/pallas_call | solution.py:38
  19.8 0.5 collective-permute-done.blocks
  20.3 1.8 %shard_map.88 = (bf16[8,8,1024]{2,1,0:T(8,128)(2,1)S(1)}, bf16[64,1280]{1,0:T(8,128)(2,1)S(1)}, bf16[64,640]{1,0:T(8,128)(2,1)S(1)}, bf16[64,640]{1,0:T(8,128)(2,1)S(1)}) custom-call(bf16[8,8,1024]{2,1,0:T(8,128)(2,1)S(1)} %collective-permute-done.blocks, bf16[1280,640]{1,0:T(8,128)(2,1)S(1)} %bitcast.7, bf16[640,1280]{1,0:T(8,128)(2,1)S(1)} %bitcast.10, ...), custom_call_target="tpu_custom_call" | custom-call | flops 419430400 | bytes 3276800 | tf_op jit(solution)/shard_map/pallas_call | solution.py:38
  22.1 0.2 collective-permute-start.1
  22.3 0.0 copy-start.2
  22.3 0.8 %shard_map.87.own = f32[8,8,1024]{2,1,0:T(8,128)S(1)} custom-call(bf16[64,640]{1,0:T(8,128)(2,1)S(1)} %get-tuple-element.24.hid._.hid_near, bf16[64,640]{1,0:T(8,128)(2,1)S(1)} %get-tuple-element.25.grad.grad_near, bf16[1280,640]{1,0:T(8,128)(2,1)S(1)} %bitcast.8, bf16[640,1280]{1,0:T(8,128)(2,1)S(1)} %bitcast.11), custom_call_target="tpu_custom_call" | custom-call | flops 209715200 | bytes 3276800 | tf_op jit(solution)/shard_map/pallas_call | solution.py:38
  23.1 0.4 collective-permute-done.1.received
  23.5 10.0 %all_to_all.16.shares = bf16[8,8,1024]{2,1,0:T(8,128)(2,1)S(1)} all-to-all(bf16[8,8,1024]{2,1,0:T(8,128)(2,1)S(1)} %shard_map.89), channel_id=1, replica_groups={{0,2,4,6,8,10,12,14},{1,3,5,7,9,11,13,15},{16,18,20,22,24,26,28,30},{17..., dimensions={0} | all-to-all | bytes 262144 | tf_op jit(solution)/shard_map/all_to_all | solution.py:323
  33.5 0.0 copy-done.2
  33.5 2.3 %shard_map.90 = (bf16[16,2,1280]{2,1,0:T(2,128)(2,1)}, f32[3,4,256]{2,1,0:T(4,128)S(1)}, f32[3,4,1280]{2,1,0:T(4,128)S(1)}) custom-call(bf16[8,8,1024]{2,1,0:T(8,128)(2,1)S(1)} %all_to_all.16.shares, bf16[3,256,1280]{2,1,0:T(8,128)(2,1)S(1)} %get-tuple-element.22.tok, bf16[3,256,1280]{2,1,0:T(8,128)(2,1)S(1)} %get-tuple-element.23.dout, ...), custom_call_target="tpu_custom_call" | custom-call | flops 11796480 | bytes 3932160 | tf_op jit(solution)/shard_map/pallas_call | solution.py:38
  35.8 3.5 %all-to-all-start.2 = ((bf16[16,2,1280]{2,1,0:T(2,128)(2,1)}), bf16[16,2,1280]{2,1,0:T(2,128)(2,1)S(1)}, u32[]{:S(2)}, u32[]{:S(2)}) async-start(bf16[16,2,1280]{2,1,0:T(2,128)(2,1)} %get-tuple-element.37), calls=%async_computation.2 | async-start | bytes 163840 | tf_op jit(solution)/shard_map/all_to_all | solution.py:465
  39.3 2.1 %shard_map.92 = (bf16[1280,640]{1,0:T(8,128)(2,1)}, bf16[640,1280]{1,0:T(8,128)(2,1)}) custom-call(bf16[64,1280]{1,0:T(8,128)(2,1)S(1)} %get-tuple-element.31.x_near, bf16[64,640]{1,0:T(8,128)(2,1)S(1)} %get-tuple-element.24.hid._.hid_near, bf16[64,640]{1,0:T(8,128)(2,1)S(1)} %get-tuple-element.25.grad.grad_near, ...), custom_call_target="tpu_custom_call" | custom-call | flops 419430400 | bytes 3276800 | tf_op jit(solution)/shard_map/pallas_call | solution.py:38
  41.4 1.6 %shard_map.91 = bf16[3,256,1280]{2,1,0:T(8,128)(2,1)} custom-call(f32[3,4,256]{2,1,0:T(4,128)S(1)} %get-tuple-element.29.left, f32[3,4,1280]{2,1,0:T(4,128)S(1)} %get-tuple-element.30.right), custom_call_target="tpu_custom_call" | custom-call | flops 7864320 | bytes 1966080 | tf_op jit(solution)/shard_map/pallas_call | solution.py:38
  43.0 3.4 %all-to-all-done.2.terms = bf16[16,2,1280]{2,1,0:T(2,128)(2,1)S(1)} async-done(((bf16[16,2,1280]{2,1,0:T(2,128)(2,1)}), bf16[16,2,1280]{2,1,0:T(2,128)(2,1)S(1)}, u32[]{:S(2)}, u32[]{:S(2)}) %all-to-all-start.2) | async-done | bytes 81952 | tf_op jit(solution)/shard_map/all_to_all | solution.py:465
  46.4 0.7 %shard_map.93 = f32[2,1280]{1,0:T(2,128)} custom-call(bf16[16,2,1280]{2,1,0:T(2,128)(2,1)S(1)} %all-to-all-done.2.terms), custom_call_target="tpu_custom_call" | custom-call | flops 40960 | bytes 81920 | tf_op jit(solution)/shard_map/pallas_call | solution.py:38
  (2 shorter events, 0.0 us)
Async XLA Ops:
  4.2 14.7 %copy-start = (bf16[1,1280,640]{2,1,0:T(8,128)(2,1)S(1)}, bf16[1,1280,640]{2,1,0:T(8,128)(2,1)}, u32[]{:S(2)}) copy-start(bf16[1,1280,640]{2,1,0:T(8,128)(2,1)} %param.7) | copy-start | bytes 4915204
  4.2 14.7 %copy-start.1 = (bf16[1,640,1280]{2,1,0:T(8,128)(2,1)S(1)}, bf16[1,640,1280]{2,1,0:T(8,128)(2,1)}, u32[]{:S(2)}) copy-start(bf16[1,640,1280]{2,1,0:T(8,128)(2,1)} %param.8) | copy-start | bytes 4915204
  18.9 1.3 %collective-permute-start = (bf16[8,8,1024]{2,1,0:T(8,128)(2,1)S(1)}, bf16[8,8,1024]{2,1,0:T(8,128)(2,1)S(1)}, u32[]{:S(2)}, u32[]{:S(2)}) collective-permute-start(bf16[8,8,1024]{2,1,0:T(8,128)(2,1)S(1)} %all_to_all.15.blocks), channel_id=1, source_target_pairs={{0,1},{1,0},{2,3},{3,2},{4,5},{5,4},{6,7},{7,6},{8,9},{9,8},{10,11... | collective-permute-start | bytes 393224 | tf_op jit(solution)/shard_map/ppermute | solution.py:330
  22.1 1.4 %collective-permute-start.1 = (bf16[8,8,1024]{2,1,0:T(8,128)(2,1)S(1)}, bf16[8,8,1024]{2,1,0:T(8,128)(2,1)S(1)}, u32[]{:S(2)}, u32[]{:S(2)}) collective-permute-start(bf16[8,8,1024]{2,1,0:T(8,128)(2,1)S(1)} %get-tuple-element.26), channel_id=1, source_target_pairs={{0,1},{1,0},{2,3},{3,2},{4,5},{5,4},{6,7},{7,6},{8,9},{9,8},{10,11... | collective-permute-start | bytes 393224 | tf_op jit(solution)/shard_map/ppermute | solution.py:330
  22.3 11.2 %copy-start.2 = (bf16[1280,2]{0,1:T(2,128)(2,1)S(1)}, bf16[1280,2]{0,1:T(2,128)(2,1)}, u32[]{:S(2)}) copy-start(bf16[1280,2]{0,1:T(2,128)(2,1)} %param.6) | copy-start | bytes 15364
  35.8 10.6 %all-to-all-start.2 = ((bf16[16,2,1280]{2,1,0:T(2,128)(2,1)}), bf16[16,2,1280]{2,1,0:T(2,128)(2,1)S(1)}, u32[]{:S(2)}, u32[]{:S(2)}) async-start(bf16[16,2,1280]{2,1,0:T(2,128)(2,1)} %get-tuple-element.37), calls=%async_computation.2 | async-start | bytes 163840 | tf_op jit(solution)/shard_map/all_to_all | solution.py:465

commit v10 on v9

--- a/solution.py
+++ b/solution.py
@@ -125,20 +125,23 @@
         disps[b] = disp.astype(BF16)
         combs[b] = comb.astype(BF16)
 
-    for step in range(images + 2):
+    for step in range(2 * images):
         if step < images:
             fetch_tok[step].wait()
             if step == 0:
                 for copy in fetch_dout:
                     copy.start()
             logits[step] = dot(router_t[...], tok[step], NT)
+        else:
+            fetch_dout[step - images].wait()
         if 0 <= step - 1 < images:
             softmaxes(step - 1)
+        if step >= images:
+            put(step, dot(combs[step - images], dout[step - images]))
         if 0 <= step - 2 < images:
             put(step - 2, dot(disps[step - 2], tok[step - 2]))
-    for b in range(images):
-        fetch_dout[b].wait()
-        put(images + b, dot(combs[b], dout[b]))
+    for b in range(max(2 * images - 2, 0), images):
+        put(b, dot(disps[b], tok[b]))
     rows_out[...] = block[...].astype(BF16)
 
 
@@ -262,29 +265,37 @@
         axis=1,
     )
     stacked_b = stacked.astype(BF16)
-    tok_all = tok[...].reshape(images * count, width)
-    by_dout = dot(stacked_b, dout[...].reshape(images * count, width), NT)
-    by_tok = dot(stacked_b, tok_all, NT)
-    grads = []
-    for b in range(images):
-        span = slice(b * count, (b + 1) * count)
+    by_dout = {}
+    by_tok = {}
+    grads = {}
+
+    def products(b):
+        by_dout[b] = dot(stacked_b, dout[b], NT)
+        by_tok[b] = dot(stacked_b, tok[b], NT)
+
+    def logits_grad(b):
         grad_comb = jnp.concatenate(
-            [by_dout[s * rows + b : s * rows + b + 1, span] for s in range(slots)], axis=0
+            [by_dout[b][s * rows + b : s * rows + b + 1] for s in range(slots)], axis=0
         )
+        at = images + b
         grad_disp = jnp.concatenate(
-            [
-                by_tok[s * rows + images + b : s * rows + images + b + 1, span]
-                for s in range(slots)
-            ],
-            axis=0,
+            [by_tok[b][s * rows + at : s * rows + at + 1] for s in range(slots)], axis=0
         )
         dispatch = disp[b]
         combine = comb[b]
-        grads.append(
-            dispatch * (grad_disp - jnp.sum(dispatch * grad_disp, axis=1, keepdims=True))
-            + combine * (grad_comb - jnp.sum(combine * grad_comb, axis=0, keepdims=True))
-        )
-    terms = dot(jnp.concatenate(grads, axis=1).astype(BF16), tok_all).astype(BF16)
+        grads[b] = dispatch * (
+            grad_disp - jnp.sum(dispatch * grad_disp, axis=1, keepdims=True)
+        ) + combine * (grad_comb - jnp.sum(combine * grad_comb, axis=0, keepdims=True))
+
+    terms = jnp.zeros((slots, width), F32)
+    for step in range(images + 2):
+        if step < images:
+            products(step)
+        if 0 <= step - 1 < images:
+            logits_grad(step - 1)
+        if 0 <= step - 2 < images:
+            terms = terms + dot(grads[step - 2].astype(BF16), tok[step - 2])
+    terms = terms.astype(BF16)
     terms_out[...] = jnp.broadcast_to(terms[None], terms_out.shape)
     for b in range(images):
         left[b] = jnp.concatenate([disp[b], grads[b]], axis=0)

time: 47.3 us -> 47.1 us (level)
  transfers between devices with their start and end apart: 3 -> 3, of which waited for: 3 -> 3; matrix products, arithmetic and copies ran while one was open for 0% -> 0% of each run, Pallas kernels for 11% -> 12%
where the time goes in v10:
time: 47.1 us; the launch traced here: 46.8 us
  blocking collectives  24.7 us (52%)
  Pallas kernels  13.5 us (29%)
  waiting for transfers between devices  4.2 us (9%)
  starting transfers between devices  3.72 us (8%)
  between operations  0.72 us (2%)
    all_to_all x2, blocking collectives, swap_chips(): lax.all_to_all(blocks, 'expert', split_axis=0, concat_axis=0, axis_index_...  24.7 us
    pallas_call x10, Pallas kernels, call(): pl.pallas_call(kernel, out_shape=outs, in_specs=in_specs, out_specs=out_s...  13.5 us
    all_to_all x1, starting transfers between devices, per_device(): lax.all_to_all(terms, 'expert', split_axis=0, concat_axis=0, tiled=True)  3.5 us
    all_to_all x1, waiting for transfers between devices, per_device(): lax.all_to_all(terms, 'expert', split_axis=0, concat_axis=0, tiled=True)  3.39 us
  transfers between devices with their start and end apart: 3, of which 3 were waited for; matrix products, arithmetic and copies ran while one was open for 0% of the time, Pallas kernels for 12%

profile of v10, /device:TPU:0, one launch (start us, length us, event | category | flops | bytes accessed | tf_op | source)
XLA Modules:
  0.0 46.8 jit_solution(8419513568627826275)
XLA Ops:
  0.6 3.4 %shard_map.84 = (bf16[2,8,1024]{2,1,0:T(8,128)(2,1)S(1)}, bf16[3,256,1280]{2,1,0:T(8,128)(2,1)S(1)}, bf16[3,256,1280]{2,1,0:T(8,128)(2,1)S(1)}, f32[3,2,256]{2,1,0:T(2,128)S(1)}, f32[3,2,256]{2,1,0:T(2,128)S(1)}) custom-call(bf16[3,256,1280]{2,1,0:T(8,128)(2,1)} %tokens.1, bf16[2,1280]{1,0:T(2,128)(2,1)} %bitcast.12, bf16[3,256,1280]{2,1,0:T(8,128)(2,1)} %d_out.1), custom_call_target="tpu_custom_call" | custom-call | flops 11796480 | bytes 3932160 | tf_op jit(solution)/shard_map/pallas_call | solution.py:38
  4.0 0.0 copy-start
  4.0 0.0 copy-start.1
  4.1 14.7 %all_to_all.15.blocks = bf16[8,8,1024]{2,1,0:T(8,128)(2,1)S(1)} all-to-all(bf16[8,8,1024]{2,1,0:T(8,128)(2,1)S(1)} %shard_map.85), channel_id=1, replica_groups={{0,2,4,6,8,10,12,14},{1,3,5,7,9,11,13,15},{16,18,20,22,24,26,28,30},{17..., dimensions={0} | all-to-all | bytes 262144 | tf_op jit(solution)/shard_map/all_to_all | solution.py:334
  18.8 0.0 collective-permute-start
  18.8 0.0 copy-done
  18.8 0.0 copy-done.1
  18.8 0.9 %shard_map.86 = (bf16[64,1280]{1,0:T(8,128)(2,1)S(1)}, bf16[64,640]{1,0:T(8,128)(2,1)S(1)}, bf16[64,640]{1,0:T(8,128)(2,1)S(1)}) custom-call(bf16[8,8,1024]{2,1,0:T(8,128)(2,1)S(1)} %all_to_all.15.blocks, bf16[1280,640]{1,0:T(8,128)(2,1)S(1)} %bitcast.6, bf16[640,1280]{1,0:T(8,128)(2,1)S(1)} %bitcast.9), custom_call_target="tpu_custom_call" | custom-call | flops 209715200 | bytes 3276800 | tf_op jit(solution)/shard_map/pallas_call | solution.py:38
  19.7 0.5 collective-permute-done.blocks
  20.1 1.8 %shard_map.88 = (bf16[8,8,1024]{2,1,0:T(8,128)(2,1)S(1)}, bf16[64,1280]{1,0:T(8,128)(2,1)S(1)}, bf16[64,640]{1,0:T(8,128)(2,1)S(1)}, bf16[64,640]{1,0:T(8,128)(2,1)S(1)}) custom-call(bf16[8,8,1024]{2,1,0:T(8,128)(2,1)S(1)} %collective-permute-done.blocks, bf16[1280,640]{1,0:T(8,128)(2,1)S(1)} %bitcast.7, bf16[640,1280]{1,0:T(8,128)(2,1)S(1)} %bitcast.10, ...), custom_call_target="tpu_custom_call" | custom-call | flops 419430400 | bytes 3276800 | tf_op jit(solution)/shard_map/pallas_call | solution.py:38
  21.9 0.2 collective-permute-start.1
  22.1 0.0 copy-start.2
  22.1 0.8 %shard_map.87.own = f32[8,8,1024]{2,1,0:T(8,128)S(1)} custom-call(bf16[64,640]{1,0:T(8,128)(2,1)S(1)} %get-tuple-element.24.hid._.hid_near, bf16[64,640]{1,0:T(8,128)(2,1)S(1)} %get-tuple-element.25.grad.grad_near, bf16[1280,640]{1,0:T(8,128)(2,1)S(1)} %bitcast.8, bf16[640,1280]{1,0:T(8,128)(2,1)S(1)} %bitcast.11), custom_call_target="tpu_custom_call" | custom-call | flops 209715200 | bytes 3276800 | tf_op jit(solution)/shard_map/pallas_call | solution.py:38
  23.0 0.4 collective-permute-done.1.received
  23.4 10.0 %all_to_all.16.shares = bf16[8,8,1024]{2,1,0:T(8,128)(2,1)S(1)} all-to-all(bf16[8,8,1024]{2,1,0:T(8,128)(2,1)S(1)} %shard_map.89), channel_id=1, replica_groups={{0,2,4,6,8,10,12,14},{1,3,5,7,9,11,13,15},{16,18,20,22,24,26,28,30},{17..., dimensions={0} | all-to-all | bytes 262144 | tf_op jit(solution)/shard_map/all_to_all | solution.py:334
  33.3 0.0 copy-done.2
  33.3 2.1 %shard_map.90 = (bf16[16,2,1280]{2,1,0:T(2,128)(2,1)}, f32[3,4,256]{2,1,0:T(4,128)S(1)}, f32[3,4,1280]{2,1,0:T(4,128)S(1)}) custom-call(bf16[8,8,1024]{2,1,0:T(8,128)(2,1)S(1)} %all_to_all.16.shares, bf16[3,256,1280]{2,1,0:T(8,128)(2,1)S(1)} %get-tuple-element.22.tok, bf16[3,256,1280]{2,1,0:T(8,128)(2,1)S(1)} %get-tuple-element.23.dout, ...), custom_call_target="tpu_custom_call" | custom-call | flops 11796480 | bytes 3932160 | tf_op jit(solution)/shard_map/pallas_call | solution.py:38
  35.5 3.5 %all-to-all-start.2 = ((bf16[16,2,1280]{2,1,0:T(2,128)(2,1)}), bf16[16,2,1280]{2,1,0:T(2,128)(2,1)S(1)}, u32[]{:S(2)}, u32[]{:S(2)}) async-start(bf16[16,2,1280]{2,1,0:T(2,128)(2,1)} %get-tuple-element.37), calls=%async_computation.2 | async-start | bytes 163840 | tf_op jit(solution)/shard_map/all_to_all | solution.py:476
  39.0 2.1 %shard_map.92 = (bf16[1280,640]{1,0:T(8,128)(2,1)}, bf16[640,1280]{1,0:T(8,128)(2,1)}) custom-call(bf16[64,1280]{1,0:T(8,128)(2,1)S(1)} %get-tuple-element.31.x_near, bf16[64,640]{1,0:T(8,128)(2,1)S(1)} %get-tuple-element.24.hid._.hid_near, bf16[64,640]{1,0:T(8,128)(2,1)S(1)} %get-tuple-element.25.grad.grad_near, ...), custom_call_target="tpu_custom_call" | custom-call | flops 419430400 | bytes 3276800 | tf_op jit(solution)/shard_map/pallas_call | solution.py:38
  41.1 1.6 %shard_map.91 = bf16[3,256,1280]{2,1,0:T(8,128)(2,1)} custom-call(f32[3,4,256]{2,1,0:T(4,128)S(1)} %get-tuple-element.29.left, f32[3,4,1280]{2,1,0:T(4,128)S(1)} %get-tuple-element.30.right), custom_call_target="tpu_custom_call" | custom-call | flops 7864320 | bytes 1966080 | tf_op jit(solution)/shard_map/pallas_call | solution.py:38
  42.7 3.4 %all-to-all-done.2.terms = bf16[16,2,1280]{2,1,0:T(2,128)(2,1)S(1)} async-done(((bf16[16,2,1280]{2,1,0:T(2,128)(2,1)}), bf16[16,2,1280]{2,1,0:T(2,128)(2,1)S(1)}, u32[]{:S(2)}, u32[]{:S(2)}) %all-to-all-start.2) | async-done | bytes 81952 | tf_op jit(solution)/shard_map/all_to_all | solution.py:476
  46.1 0.7 %shard_map.93 = f32[2,1280]{1,0:T(2,128)} custom-call(bf16[16,2,1280]{2,1,0:T(2,128)(2,1)S(1)} %all-to-all-done.2.terms), custom_call_target="tpu_custom_call" | custom-call | flops 40960 | bytes 81920 | tf_op jit(solution)/shard_map/pallas_call | solution.py:38
  (2 shorter events, 0.0 us)
Async XLA Ops:
  4.0 14.7 %copy-start = (bf16[1,1280,640]{2,1,0:T(8,128)(2,1)S(1)}, bf16[1,1280,640]{2,1,0:T(8,128)(2,1)}, u32[]{:S(2)}) copy-start(bf16[1,1280,640]{2,1,0:T(8,128)(2,1)} %param.7) | copy-start | bytes 4915204
  4.0 14.7 %copy-start.1 = (bf16[1,640,1280]{2,1,0:T(8,128)(2,1)S(1)}, bf16[1,640,1280]{2,1,0:T(8,128)(2,1)}, u32[]{:S(2)}) copy-start(bf16[1,640,1280]{2,1,0:T(8,128)(2,1)} %param.8) | copy-start | bytes 4915204
  18.8 1.3 %collective-permute-start = (bf16[8,8,1024]{2,1,0:T(8,128)(2,1)S(1)}, bf16[8,8,1024]{2,1,0:T(8,128)(2,1)S(1)}, u32[]{:S(2)}, u32[]{:S(2)}) collective-permute-start(bf16[8,8,1024]{2,1,0:T(8,128)(2,1)S(1)} %all_to_all.15.blocks), channel_id=1, source_target_pairs={{0,1},{1,0},{2,3},{3,2},{4,5},{5,4},{6,7},{7,6},{8,9},{9,8},{10,11... | collective-permute-start | bytes 393224 | tf_op jit(solution)/shard_map/ppermute | solution.py:341
  21.9 1.4 %collective-permute-start.1 = (bf16[8,8,1024]{2,1,0:T(8,128)(2,1)S(1)}, bf16[8,8,1024]{2,1,0:T(8,128)(2,1)S(1)}, u32[]{:S(2)}, u32[]{:S(2)}) collective-permute-start(bf16[8,8,1024]{2,1,0:T(8,128)(2,1)S(1)} %get-tuple-element.26), channel_id=1, source_target_pairs={{0,1},{1,0},{2,3},{3,2},{4,5},{5,4},{6,7},{7,6},{8,9},{9,8},{10,11... | collective-permute-start | bytes 393224 | tf_op jit(solution)/shard_map/ppermute | solution.py:341
  22.1 11.2 %copy-start.2 = (bf16[1280,2]{0,1:T(2,128)(2,1)S(1)}, bf16[1280,2]{0,1:T(2,128)(2,1)}, u32[]{:S(2)}) copy-start(bf16[1280,2]{0,1:T(2,128)(2,1)} %param.6) | copy-start | bytes 15364
  35.5 10.6 %all-to-all-start.2 = ((bf16[16,2,1280]{2,1,0:T(2,128)(2,1)}), bf16[16,2,1280]{2,1,0:T(2,128)(2,1)S(1)}, u32[]{:S(2)}, u32[]{:S(2)}) async-start(bf16[16,2,1280]{2,1,0:T(2,128)(2,1)} %get-tuple-element.37), calls=%async_computation.2 | async-start | bytes 163840 | tf_op jit(solution)/shard_map/all_to_all | solution.py:476

commit v11 on v10

--- a/solution.py
+++ b/solution.py
@@ -80,11 +80,13 @@
     tokens,
     router_hbm,
     d_out,
+    w_in,
     rows_out,
     tok,
     dout,
     disp_out,
     comb_out,
+    w_one,
     router_t,
     block,
     sems,
@@ -101,6 +103,7 @@
     fetch_dout = [
         pltpu.make_async_copy(d_out.at[b], dout.at[b], sems.at[images + b]) for b in range(images)
     ]
+    fetch_weight = pltpu.make_async_copy(w_in, w_one, other_sems.at[1])
     for copy in fetch_tok:
         copy.start()
     block[...] = jnp.zeros_like(block)
@@ -134,6 +137,8 @@
             logits[step] = dot(router_t[...], tok[step], NT)
         else:
             fetch_dout[step - images].wait()
+            if step == images:
+                fetch_weight.start()
         if 0 <= step - 1 < images:
             softmaxes(step - 1)
         if step >= images:
@@ -143,6 +148,7 @@
     for b in range(max(2 * images - 2, 0), images):
         put(b, dot(disps[b], tok[b]))
     rows_out[...] = block[...].astype(BF16)
+    fetch_weight.wait()
 
 
 def repeat_kernel(split_chips, rows, tok, dout, send):
@@ -354,7 +360,7 @@
     big = images * count * width
     weight = width * hidden_units
 
-    blocks, tok, dout, disp, comb = call(
+    blocks, tok, dout, disp, comb, w_one = call(
         rows_kernel,
         (
             vmem_out((slots, rows, main), BF16),
@@ -362,10 +368,11 @@
             vmem_out((images, count, width), BF16),
             vmem_out((images, slots, count), F32),
             vmem_out((images, slots, count), F32),
+            vmem_out(w_in.shape[1:], BF16),
         ),
-        tuple(in_hbm(array) for array in (tokens, router_t, d_out)),
-        (VMEM,) * 5,
-        (HBM,) * 3,
+        tuple(in_hbm(array) for array in (tokens, router_t, d_out, w_in[0])),
+        (VMEM,) * 6,
+        (HBM,) * 4,
         [
             pltpu.VMEM((slots, width), BF16),
             pltpu.VMEM((slots, rows, main), F32),
@@ -373,7 +380,7 @@
             pltpu.SemaphoreType.DMA((2,)),
         ],
         (6 * slots * big, 4 * big),
-        limit=56 * MIB,
+        limit=58 * MIB,
     )
     send = call(
         functools.partial(repeat_kernel, split_chips),
@@ -386,7 +393,7 @@
     )
     near = swap_chips(send)
     far = swap_cores(near)
-    w_one, w_two = in_vmem(w_in[0]), in_vmem(w_out[0])
+    w_one, w_two = in_vmem(w_one), in_vmem(w_out[0])
     inner = (
         vmem_out((half, width), BF16),
         vmem_out((half, hidden_units), BF16),

time: 47.1 us -> 47.6 us (1.011)
  Pallas kernels: 13.5 us -> 14.1 us
    pallas_call x10, Pallas kernels: 13.5 us -> 14.1 us  [call(): pl.pallas_call(kernel, out_shape=outs, in_specs=in_specs, out_specs=out_s...]
  transfers between devices with their start and end apart: 3 -> 3, of which waited for: 3 -> 3; matrix products, arithmetic and copies ran while one was open for 0% -> 0% of each run, Pallas kernels for 12% -> 11%
where the time goes in v11:
time: 47.6 us; the launch traced here: 47.3 us
  blocking collectives  24.5 us (51%)
  Pallas kernels  14.1 us (30%)
  waiting for transfers between devices  4.21 us (9%)
  starting transfers between devices  3.72 us (8%)
  between operations  0.73 us (2%)
    all_to_all x2, blocking collectives, swap_chips(): lax.all_to_all(blocks, 'expert', split_axis=0, concat_axis=0, axis_index_...  24.5 us
    pallas_call x10, Pallas kernels, call(): pl.pallas_call(kernel, out_shape=outs, in_specs=in_specs, out_specs=out_s...  14.1 us
    all_to_all x1, starting transfers between devices, per_device(): lax.all_to_all(terms, 'expert', split_axis=0, concat_axis=0, tiled=True)  3.5 us
    all_to_all x1, waiting for transfers between devices, per_device(): lax.all_to_all(terms, 'expert', split_axis=0, concat_axis=0, tiled=True)  3.39 us
  transfers between devices with their start and end apart: 3, of which 3 were waited for; matrix products, arithmetic and copies ran while one was open for 0% of the time, Pallas kernels for 11%

profile of v11, /device:TPU:0, one launch (start us, length us, event | category | flops | bytes accessed | tf_op | source)
XLA Modules:
  0.0 47.3 jit_solution(16025345345668132809)
XLA Ops:
  0.6 4.0 %shard_map.84 = (bf16[2,8,1024]{2,1,0:T(8,128)(2,1)S(1)}, bf16[3,256,1280]{2,1,0:T(8,128)(2,1)S(1)}, bf16[3,256,1280]{2,1,0:T(8,128)(2,1)S(1)}, f32[3,2,256]{2,1...) custom-call(bf16[3,256,1280]{2,1,0:T(8,128)(2,1)} %tokens.1, bf16[2,1280]{1,0:T(2,128)(2,1)} %bitcast.9, ...), custom_call_target="tpu_custom_call" | custom-call | flops 11796480 | bytes 3932160 | tf_op jit(solution)/shard_map/pallas_call | solution.py:38
  4.7 0.0 copy-start
  4.7 14.6 %all_to_all.15.blocks = bf16[8,8,1024]{2,1,0:T(8,128)(2,1)S(1)} all-to-all(bf16[8,8,1024]{2,1,0:T(8,128)(2,1)S(1)} %shard_map.85), channel_id=1, replica_groups={{0,2,4,6,8,10,12,14},{1,3,5,7,9,11,13,15},{16,18,20,22,24,26,28,30},{17..., dimensions={0} | all-to-all | bytes 262144 | tf_op jit(solution)/shard_map/all_to_all | solution.py:340
  19.2 0.0 collective-permute-start
  19.2 0.0 copy-done
  19.2 0.9 %shard_map.86 = (bf16[64,1280]{1,0:T(8,128)(2,1)S(1)}, bf16[64,640]{1,0:T(8,128)(2,1)S(1)}, bf16[64,640]{1,0:T(8,128)(2,1)S(1)}) custom-call(bf16[8,8,1024]{2,1,0:T(8,128)(2,1)S(1)} %all_to_all.15.blocks, bf16[1280,640]{1,0:T(8,128)(2,1)S(1)} %get-tuple-element.25.w_in, bf16[640,1280]{1,0:T(8,128)(2,1)S(1)} %bitcast.6), custom_call_target="tpu_custom_call" | custom-call | flops 209715200 | bytes 3276800 | tf_op jit(solution)/shard_map/pallas_call | solution.py:38
  20.1 0.5 collective-permute-done.blocks
  20.6 1.8 %shard_map.88 = (bf16[8,8,1024]{2,1,0:T(8,128)(2,1)S(1)}, bf16[64,1280]{1,0:T(8,128)(2,1)S(1)}, bf16[64,640]{1,0:T(8,128)(2,1)S(1)}, bf16[64,640]{1,0:T(8,128)(2,1)S(1)}) custom-call(bf16[8,8,1024]{2,1,0:T(8,128)(2,1)S(1)} %collective-permute-done.blocks, bf16[1280,640]{1,0:T(8,128)(2,1)S(1)} %get-tuple-element.25.w_in, bf16[640,1280]{1,0:T(8,128)(2,1)S(1)} %bitcast.7, ...), custom_call_target="tpu_custom_call" | custom-call | flops 419430400 | bytes 3276800 | tf_op jit(solution)/shard_map/pallas_call | solution.py:38
  22.4 0.0 copy-start.2
  22.4 0.2 collective-permute-start.1
  22.6 0.0 copy-start.1
  22.6 0.8 %shard_map.87.own = f32[8,8,1024]{2,1,0:T(8,128)S(1)} custom-call(bf16[64,640]{1,0:T(8,128)(2,1)S(1)} %get-tuple-element.26.hid._.hid_near, bf16[64,640]{1,0:T(8,128)(2,1)S(1)} %get-tuple-element.27.grad.grad_near, bf16[1280,640]{1,0:T(8,128)(2,1)S(1)} %get-tuple-element.25.w_in, bf16[640,1280]{1,0:T(8,128)(2,1)S(1)} %bitcast.8), custom_call_target="tpu_custom_call" | custom-call | flops 209715200 | bytes 3276800 | tf_op jit(solution)/shard_map/pallas_call | solution.py:38
  23.5 0.4 collective-permute-done.1.received
  23.9 0.0 copy-done.2
  23.9 10.0 %all_to_all.16.shares = bf16[8,8,1024]{2,1,0:T(8,128)(2,1)S(1)} all-to-all(bf16[8,8,1024]{2,1,0:T(8,128)(2,1)S(1)} %shard_map.89), channel_id=1, replica_groups={{0,2,4,6,8,10,12,14},{1,3,5,7,9,11,13,15},{16,18,20,22,24,26,28,30},{17..., dimensions={0} | all-to-all | bytes 262144 | tf_op jit(solution)/shard_map/all_to_all | solution.py:340
  33.8 0.0 copy-done.1
  33.8 0.0 copy-start.3
  33.8 2.1 %shard_map.90 = (bf16[16,2,1280]{2,1,0:T(2,128)(2,1)}, f32[3,4,256]{2,1,0:T(4,128)S(1)}, f32[3,4,1280]{2,1,0:T(4,128)S(1)}) custom-call(bf16[8,8,1024]{2,1,0:T(8,128)(2,1)S(1)} %all_to_all.16.shares, bf16[3,256,1280]{2,1,0:T(8,128)(2,1)S(1)} %get-tuple-element.23.tok, bf16[3,256,1280]{2,1,0:T(8,128)(2,1)S(1)} %get-tuple-element.24.dout, ...), custom_call_target="tpu_custom_call" | custom-call | flops 11796480 | bytes 3932160 | tf_op jit(solution)/shard_map/pallas_call | solution.py:38
  36.0 3.5 %all-to-all-start.2 = ((bf16[16,2,1280]{2,1,0:T(2,128)(2,1)}), bf16[16,2,1280]{2,1,0:T(2,128)(2,1)S(1)}, u32[]{:S(2)}, u32[]{:S(2)}) async-start(bf16[16,2,1280]{2,1,0:T(2,128)(2,1)} %get-tuple-element.39), calls=%async_computation.2 | async-start | bytes 163840 | tf_op jit(solution)/shard_map/all_to_all | solution.py:483
  39.5 0.0 copy-done.3
  39.5 2.1 %shard_map.92 = (bf16[1280,640]{1,0:T(8,128)(2,1)}, bf16[640,1280]{1,0:T(8,128)(2,1)}) custom-call(bf16[64,1280]{1,0:T(8,128)(2,1)S(1)} %get-tuple-element.33.x_near, bf16[64,640]{1,0:T(8,128)(2,1)S(1)} %get-tuple-element.26.hid._.hid_near, bf16[64,640]{1,0:T(8,128)(2,1)S(1)} %get-tuple-element.27.grad.grad_near, ...), custom_call_target="tpu_custom_call" | custom-call | flops 419430400 | bytes 3276800 | tf_op jit(solution)/shard_map/pallas_call | solution.py:38
  41.6 1.6 %shard_map.91 = bf16[3,256,1280]{2,1,0:T(8,128)(2,1)} custom-call(f32[3,4,256]{2,1,0:T(4,128)S(1)} %get-tuple-element.31.left, f32[3,4,1280]{2,1,0:T(4,128)S(1)} %get-tuple-element.32.right), custom_call_target="tpu_custom_call" | custom-call | flops 7864320 | bytes 1966080 | tf_op jit(solution)/shard_map/pallas_call | solution.py:38
  43.2 3.4 %all-to-all-done.2.terms = bf16[16,2,1280]{2,1,0:T(2,128)(2,1)S(1)} async-done(((bf16[16,2,1280]{2,1,0:T(2,128)(2,1)}), bf16[16,2,1280]{2,1,0:T(2,128)(2,1)S(1)}, u32[]{:S(2)}, u32[]{:S(2)}) %all-to-all-start.2) | async-done | bytes 81952 | tf_op jit(solution)/shard_map/all_to_all | solution.py:483
  46.6 0.7 %shard_map.93 = f32[2,1280]{1,0:T(2,128)} custom-call(bf16[16,2,1280]{2,1,0:T(2,128)(2,1)S(1)} %all-to-all-done.2.terms), custom_call_target="tpu_custom_call" | custom-call | flops 40960 | bytes 81920 | tf_op jit(solution)/shard_map/pallas_call | solution.py:38
  (2 shorter events, 0.0 us)
Async XLA Ops:
  4.7 14.6 %copy-start = (bf16[1,640,1280]{2,1,0:T(8,128)(2,1)S(1)}, bf16[1,640,1280]{2,1,0:T(8,128)(2,1)}, u32[]{:S(2)}) copy-start(bf16[1,640,1280]{2,1,0:T(8,128)(2,1)} %param.8) | copy-start | bytes 4915204
  19.2 1.3 %collective-permute-start = (bf16[8,8,1024]{2,1,0:T(8,128)(2,1)S(1)}, bf16[8,8,1024]{2,1,0:T(8,128)(2,1)S(1)}, u32[]{:S(2)}, u32[]{:S(2)}) collective-permute-start(bf16[8,8,1024]{2,1,0:T(8,128)(2,1)S(1)} %all_to_all.15.blocks), channel_id=1, source_target_pairs={{0,1},{1,0},{2,3},{3,2},{4,5},{5,4},{6,7},{7,6},{8,9},{9,8},{10,11... | collective-permute-start | bytes 393224 | tf_op jit(solution)/shard_map/ppermute | solution.py:347
  22.4 1.5 %copy-start.2 = (bf16[64,640]{1,0:T(8,128)(2,1)}, bf16[64,640]{1,0:T(8,128)(2,1)S(1)}, u32[]{:S(2)}) copy-start(bf16[64,640]{1,0:T(8,128)(2,1)S(1)} %get-tuple-element.36.grad_far) | copy-start | bytes 245764
  22.4 1.4 %collective-permute-start.1 = (bf16[8,8,1024]{2,1,0:T(8,128)(2,1)S(1)}, bf16[8,8,1024]{2,1,0:T(8,128)(2,1)S(1)}, u32[]{:S(2)}, u32[]{:S(2)}) collective-permute-start(bf16[8,8,1024]{2,1,0:T(8,128)(2,1)S(1)} %get-tuple-element.28), channel_id=1, source_target_pairs={{0,1},{1,0},{2,3},{3,2},{4,5},{5,4},{6,7},{7,6},{8,9},{9,8},{10,11... | collective-permute-start | bytes 393224 | tf_op jit(solution)/shard_map/ppermute | solution.py:347
  22.6 11.2 %copy-start.1 = (bf16[1280,2]{0,1:T(2,128)(2,1)S(1)}, bf16[1280,2]{0,1:T(2,128)(2,1)}, u32[]{:S(2)}) copy-start(bf16[1280,2]{0,1:T(2,128)(2,1)} %param.6) | copy-start | bytes 15364
  33.8 5.6 %copy-start.3 = (bf16[64,640]{1,0:T(8,128)(2,1)S(1)}, bf16[64,640]{1,0:T(8,128)(2,1)}, u32[]{:S(2)}) copy-start(bf16[64,640]{1,0:T(8,128)(2,1)} %copy-done.2) | copy-start | bytes 245764
  36.0 10.6 %all-to-all-start.2 = ((bf16[16,2,1280]{2,1,0:T(2,128)(2,1)}), bf16[16,2,1280]{2,1,0:T(2,128)(2,1)S(1)}, u32[]{:S(2)}, u32[]{:S(2)}) async-start(bf16[16,2,1280]{2,1,0:T(2,128)(2,1)} %get-tuple-element.39), calls=%async_computation.2 | async-start | bytes 163840 | tf_op jit(solution)/shard_map/all_to_all | solution.py:483

commit v12 on v10

--- a/solution.py
+++ b/solution.py
@@ -101,7 +101,7 @@
     fetch_dout = [
         pltpu.make_async_copy(d_out.at[b], dout.at[b], sems.at[images + b]) for b in range(images)
     ]
-    for copy in fetch_tok:
+    for copy in fetch_tok + fetch_dout:
         copy.start()
     block[...] = jnp.zeros_like(block)
 
@@ -128,18 +128,14 @@
     for step in range(2 * images):
         if step < images:
             fetch_tok[step].wait()
-            if step == 0:
-                for copy in fetch_dout:
-                    copy.start()
             logits[step] = dot(router_t[...], tok[step], NT)
-        else:
-            fetch_dout[step - images].wait()
         if 0 <= step - 1 < images:
             softmaxes(step - 1)
-        if step >= images:
-            put(step, dot(combs[step - images], dout[step - images]))
         if 0 <= step - 2 < images:
             put(step - 2, dot(disps[step - 2], tok[step - 2]))
+        if step >= images:
+            fetch_dout[step - images].wait()
+            put(step, dot(combs[step - images], dout[step - images]))
     for b in range(max(2 * images - 2, 0), images):
         put(b, dot(disps[b], tok[b]))
     rows_out[...] = block[...].astype(BF16)

time: 47.1 us -> 47.7 us (1.013)
  Pallas kernels: 13.5 us -> 14.1 us
    pallas_call x10, Pallas kernels: 13.5 us -> 14.1 us  [call(): pl.pallas_call(kernel, out_shape=outs, in_specs=in_specs, out_specs=out_s...]
  transfers between devices with their start and end apart: 3 -> 3, of which waited for: 3 -> 3; matrix products, arithmetic and copies ran while one was open for 0% -> 0% of each run, Pallas kernels for 12% -> 11%
where the time goes in v12:
time: 47.7 us; the launch traced here: 47.4 us
  blocking collectives  24.7 us (52%)
  Pallas kernels  14.1 us (30%)
  waiting for transfers between devices  4.21 us (9%)
  starting transfers between devices  3.72 us (8%)
  between operations  0.72 us (2%)
    all_to_all x2, blocking collectives, swap_chips(): lax.all_to_all(blocks, 'expert', split_axis=0, concat_axis=0, axis_index_...  24.7 us
    pallas_call x10, Pallas kernels, call(): pl.pallas_call(kernel, out_shape=outs, in_specs=in_specs, out_specs=out_s...  14.1 us
    all_to_all x1, starting transfers between devices, per_device(): lax.all_to_all(terms, 'expert', split_axis=0, concat_axis=0, tiled=True)  3.5 us
    all_to_all x1, waiting for transfers between devices, per_device(): lax.all_to_all(terms, 'expert', split_axis=0, concat_axis=0, tiled=True)  3.39 us
  transfers between devices with their start and end apart: 3, of which 3 were waited for; matrix products, arithmetic and copies ran while one was open for 0% of the time, Pallas kernels for 11%

profile of v12, /device:TPU:0, one launch (start us, length us, event | category | flops | bytes accessed | tf_op | source)
XLA Modules:
  0.0 47.4 jit_solution(11092054608598346784)
XLA Ops:
  0.6 4.0 %shard_map.84 = (bf16[2,8,1024]{2,1,0:T(8,128)(2,1)S(1)}, bf16[3,256,1280]{2,1,0:T(8,128)(2,1)S(1)}, bf16[3,256,1280]{2,1,0:T(8,128)(2,1)S(1)}, f32[3,2,256]{2,1,0:T(2,128)S(1)}, f32[3,2,256]{2,1,0:T(2,128)S(1)}) custom-call(bf16[3,256,1280]{2,1,0:T(8,128)(2,1)} %tokens.1, bf16[2,1280]{1,0:T(2,128)(2,1)} %bitcast.12, bf16[3,256,1280]{2,1,0:T(8,128)(2,1)} %d_out.1), custom_call_target="tpu_custom_call" | custom-call | flops 11796480 | bytes 3932160 | tf_op jit(solution)/shard_map/pallas_call | solution.py:38
  4.7 0.0 copy-start
  4.7 0.0 copy-start.1
  4.7 14.7 %all_to_all.15.blocks = bf16[8,8,1024]{2,1,0:T(8,128)(2,1)S(1)} all-to-all(bf16[8,8,1024]{2,1,0:T(8,128)(2,1)S(1)} %shard_map.85), channel_id=1, replica_groups={{0,2,4,6,8,10,12,14},{1,3,5,7,9,11,13,15},{16,18,20,22,24,26,28,30},{17..., dimensions={0} | all-to-all | bytes 262144 | tf_op jit(solution)/shard_map/all_to_all | solution.py:330
  19.4 0.0 collective-permute-start
  19.4 0.0 copy-done
  19.4 0.0 copy-done.1
  19.4 0.9 %shard_map.86 = (bf16[64,1280]{1,0:T(8,128)(2,1)S(1)}, bf16[64,640]{1,0:T(8,128)(2,1)S(1)}, bf16[64,640]{1,0:T(8,128)(2,1)S(1)}) custom-call(bf16[8,8,1024]{2,1,0:T(8,128)(2,1)S(1)} %all_to_all.15.blocks, bf16[1280,640]{1,0:T(8,128)(2,1)S(1)} %bitcast.6, bf16[640,1280]{1,0:T(8,128)(2,1)S(1)} %bitcast.9), custom_call_target="tpu_custom_call" | custom-call | flops 209715200 | bytes 3276800 | tf_op jit(solution)/shard_map/pallas_call | solution.py:38
  20.3 0.5 collective-permute-done.blocks
  20.7 1.8 %shard_map.88 = (bf16[8,8,1024]{2,1,0:T(8,128)(2,1)S(1)}, bf16[64,1280]{1,0:T(8,128)(2,1)S(1)}, bf16[64,640]{1,0:T(8,128)(2,1)S(1)}, bf16[64,640]{1,0:T(8,128)(2,1)S(1)}) custom-call(bf16[8,8,1024]{2,1,0:T(8,128)(2,1)S(1)} %collective-permute-done.blocks, bf16[1280,640]{1,0:T(8,128)(2,1)S(1)} %bitcast.7, bf16[640,1280]{1,0:T(8,128)(2,1)S(1)} %bitcast.10, ...), custom_call_target="tpu_custom_call" | custom-call | flops 419430400 | bytes 3276800 | tf_op jit(solution)/shard_map/pallas_call | solution.py:38
  22.5 0.2 collective-permute-start.1
  22.8 0.0 copy-start.2
  22.8 0.8 %shard_map.87.own = f32[8,8,1024]{2,1,0:T(8,128)S(1)} custom-call(bf16[64,640]{1,0:T(8,128)(2,1)S(1)} %get-tuple-element.24.hid._.hid_near, bf16[64,640]{1,0:T(8,128)(2,1)S(1)} %get-tuple-element.25.grad.grad_near, bf16[1280,640]{1,0:T(8,128)(2,1)S(1)} %bitcast.8, bf16[640,1280]{1,0:T(8,128)(2,1)S(1)} %bitcast.11), custom_call_target="tpu_custom_call" | custom-call | flops 209715200 | bytes 3276800 | tf_op jit(solution)/shard_map/pallas_call | solution.py:38
  23.6 0.4 collective-permute-done.1.received
  24.0 10.0 %all_to_all.16.shares = bf16[8,8,1024]{2,1,0:T(8,128)(2,1)S(1)} all-to-all(bf16[8,8,1024]{2,1,0:T(8,128)(2,1)S(1)} %shard_map.89), channel_id=1, replica_groups={{0,2,4,6,8,10,12,14},{1,3,5,7,9,11,13,15},{16,18,20,22,24,26,28,30},{17..., dimensions={0} | all-to-all | bytes 262144 | tf_op jit(solution)/shard_map/all_to_all | solution.py:330
  34.0 0.0 copy-done.2
  34.0 2.1 %shard_map.90 = (bf16[16,2,1280]{2,1,0:T(2,128)(2,1)}, f32[3,4,256]{2,1,0:T(4,128)S(1)}, f32[3,4,1280]{2,1,0:T(4,128)S(1)}) custom-call(bf16[8,8,1024]{2,1,0:T(8,128)(2,1)S(1)} %all_to_all.16.shares, bf16[3,256,1280]{2,1,0:T(8,128)(2,1)S(1)} %get-tuple-element.22.tok, bf16[3,256,1280]{2,1,0:T(8,128)(2,1)S(1)} %get-tuple-element.23.dout, ...), custom_call_target="tpu_custom_call" | custom-call | flops 11796480 | bytes 3932160 | tf_op jit(solution)/shard_map/pallas_call | solution.py:38
  36.1 3.5 %all-to-all-start.2 = ((bf16[16,2,1280]{2,1,0:T(2,128)(2,1)}), bf16[16,2,1280]{2,1,0:T(2,128)(2,1)S(1)}, u32[]{:S(2)}, u32[]{:S(2)}) async-start(bf16[16,2,1280]{2,1,0:T(2,128)(2,1)} %get-tuple-element.37), calls=%async_computation.2 | async-start | bytes 163840 | tf_op jit(solution)/shard_map/all_to_all | solution.py:472
  39.6 2.1 %shard_map.92 = (bf16[1280,640]{1,0:T(8,128)(2,1)}, bf16[640,1280]{1,0:T(8,128)(2,1)}) custom-call(bf16[64,1280]{1,0:T(8,128)(2,1)S(1)} %get-tuple-element.31.x_near, bf16[64,640]{1,0:T(8,128)(2,1)S(1)} %get-tuple-element.24.hid._.hid_near, bf16[64,640]{1,0:T(8,128)(2,1)S(1)} %get-tuple-element.25.grad.grad_near, ...), custom_call_target="tpu_custom_call" | custom-call | flops 419430400 | bytes 3276800 | tf_op jit(solution)/shard_map/pallas_call | solution.py:38
  41.7 1.6 %shard_map.91 = bf16[3,256,1280]{2,1,0:T(8,128)(2,1)} custom-call(f32[3,4,256]{2,1,0:T(4,128)S(1)} %get-tuple-element.29.left, f32[3,4,1280]{2,1,0:T(4,128)S(1)} %get-tuple-element.30.right), custom_call_target="tpu_custom_call" | custom-call | flops 7864320 | bytes 1966080 | tf_op jit(solution)/shard_map/pallas_call | solution.py:38
  43.3 3.4 %all-to-all-done.2.terms = bf16[16,2,1280]{2,1,0:T(2,128)(2,1)S(1)} async-done(((bf16[16,2,1280]{2,1,0:T(2,128)(2,1)}), bf16[16,2,1280]{2,1,0:T(2,128)(2,1)S(1)}, u32[]{:S(2)}, u32[]{:S(2)}) %all-to-all-start.2) | async-done | bytes 81952 | tf_op jit(solution)/shard_map/all_to_all | solution.py:472
  46.7 0.7 %shard_map.93 = f32[2,1280]{1,0:T(2,128)} custom-call(bf16[16,2,1280]{2,1,0:T(2,128)(2,1)S(1)} %all-to-all-done.2.terms), custom_call_target="tpu_custom_call" | custom-call | flops 40960 | bytes 81920 | tf_op jit(solution)/shard_map/pallas_call | solution.py:38
  (2 shorter events, 0.0 us)
Async XLA Ops:
  4.7 14.7 %copy-start = (bf16[1,1280,640]{2,1,0:T(8,128)(2,1)S(1)}, bf16[1,1280,640]{2,1,0:T(8,128)(2,1)}, u32[]{:S(2)}) copy-start(bf16[1,1280,640]{2,1,0:T(8,128)(2,1)} %param.7) | copy-start | bytes 4915204
  4.7 14.7 %copy-start.1 = (bf16[1,640,1280]{2,1,0:T(8,128)(2,1)S(1)}, bf16[1,640,1280]{2,1,0:T(8,128)(2,1)}, u32[]{:S(2)}) copy-start(bf16[1,640,1280]{2,1,0:T(8,128)(2,1)} %param.8) | copy-start | bytes 4915204
  19.4 1.3 %collective-permute-start = (bf16[8,8,1024]{2,1,0:T(8,128)(2,1)S(1)}, bf16[8,8,1024]{2,1,0:T(8,128)(2,1)S(1)}, u32[]{:S(2)}, u32[]{:S(2)}) collective-permute-start(bf16[8,8,1024]{2,1,0:T(8,128)(2,1)S(1)} %all_to_all.15.blocks), channel_id=1, source_target_pairs={{0,1},{1,0},{2,3},{3,2},{4,5},{5,4},{6,7},{7,6},{8,9},{9,8},{10,11... | collective-permute-start | bytes 393224 | tf_op jit(solution)/shard_map/ppermute | solution.py:337
  22.5 1.4 %collective-permute-start.1 = (bf16[8,8,1024]{2,1,0:T(8,128)(2,1)S(1)}, bf16[8,8,1024]{2,1,0:T(8,128)(2,1)S(1)}, u32[]{:S(2)}, u32[]{:S(2)}) collective-permute-start(bf16[8,8,1024]{2,1,0:T(8,128)(2,1)S(1)} %get-tuple-element.26), channel_id=1, source_target_pairs={{0,1},{1,0},{2,3},{3,2},{4,5},{5,4},{6,7},{7,6},{8,9},{9,8},{10,11... | collective-permute-start | bytes 393224 | tf_op jit(solution)/shard_map/ppermute | solution.py:337
  22.8 11.2 %copy-start.2 = (bf16[1280,2]{0,1:T(2,128)(2,1)S(1)}, bf16[1280,2]{0,1:T(2,128)(2,1)}, u32[]{:S(2)}) copy-start(bf16[1280,2]{0,1:T(2,128)(2,1)} %param.6) | copy-start | bytes 15364
  36.1 10.6 %all-to-all-start.2 = ((bf16[16,2,1280]{2,1,0:T(2,128)(2,1)}), bf16[16,2,1280]{2,1,0:T(2,128)(2,1)S(1)}, u32[]{:S(2)}, u32[]{:S(2)}) async-start(bf16[16,2,1280]{2,1,0:T(2,128)(2,1)} %get-tuple-element.37), calls=%async_computation.2 | async-start | bytes 163840 | tf_op jit(solution)/shard_map/all_to_all | solution.py:472

commit v13 on v10

--- a/solution.py
+++ b/solution.py
@@ -111,6 +111,8 @@
         block[:, to, column : column + extra] = values[:, main:]
 
     fetch_router.wait()
+    for copy in fetch_dout:
+        copy.start()
     logits = {}
     combs = {}
     disps = {}
@@ -128,9 +130,6 @@
     for step in range(2 * images):
         if step < images:
             fetch_tok[step].wait()
-            if step == 0:
-                for copy in fetch_dout:
-                    copy.start()
             logits[step] = dot(router_t[...], tok[step], NT)
         else:
             fetch_dout[step - images].wait()

time: 47.1 us -> 47.1 us (level)
  no operation moved by 1% of the time
where the time goes in v13:
time: 47.1 us; the launch traced here: 46.8 us
  blocking collectives  24.7 us (52%)
  Pallas kernels  13.4 us (28%)
  waiting for transfers between devices  4.21 us (9%)
  starting transfers between devices  3.72 us (8%)
  between operations  0.72 us (2%)
    all_to_all x2, blocking collectives, swap_chips(): lax.all_to_all(blocks, 'expert', split_axis=0, concat_axis=0, axis_index_...  24.7 us
    pallas_call x10, Pallas kernels, call(): pl.pallas_call(kernel, out_shape=outs, in_specs=in_specs, out_specs=out_s...  13.4 us
    all_to_all x1, starting transfers between devices, per_device(): lax.all_to_all(terms, 'expert', split_axis=0, concat_axis=0, tiled=True)  3.5 us
    all_to_all x1, waiting for transfers between devices, per_device(): lax.all_to_all(terms, 'expert', split_axis=0, concat_axis=0, tiled=True)  3.39 us
  transfers between devices with their start and end apart: 3, of which 3 were waited for; matrix products, arithmetic and copies ran while one was open for 0% of the time, Pallas kernels for 12%

profile of v13, /device:TPU:0, one launch (start us, length us, event | category | flops | bytes accessed | tf_op | source)
XLA Modules:
  0.0 46.8 jit_solution(12865963558095242125)
XLA Ops:
  0.6 3.4 %shard_map.84 = (bf16[2,8,1024]{2,1,0:T(8,128)(2,1)S(1)}, bf16[3,256,1280]{2,1,0:T(8,128)(2,1)S(1)}, bf16[3,256,1280]{2,1,0:T(8,128)(2,1)S(1)}, f32[3,2,256]{2,1,0:T(2,128)S(1)}, f32[3,2,256]{2,1,0:T(2,128)S(1)}) custom-call(bf16[3,256,1280]{2,1,0:T(8,128)(2,1)} %tokens.1, bf16[2,1280]{1,0:T(2,128)(2,1)} %bitcast.12, bf16[3,256,1280]{2,1,0:T(8,128)(2,1)} %d_out.1), custom_call_target="tpu_custom_call" | custom-call | flops 11796480 | bytes 3932160 | tf_op jit(solution)/shard_map/pallas_call | solution.py:38
  4.0 0.0 copy-start
  4.0 0.0 copy-start.1
  4.1 14.7 %all_to_all.15.blocks = bf16[8,8,1024]{2,1,0:T(8,128)(2,1)S(1)} all-to-all(bf16[8,8,1024]{2,1,0:T(8,128)(2,1)S(1)} %shard_map.85), channel_id=1, replica_groups={{0,2,4,6,8,10,12,14},{1,3,5,7,9,11,13,15},{16,18,20,22,24,26,28,30},{17..., dimensions={0} | all-to-all | bytes 262144 | tf_op jit(solution)/shard_map/all_to_all | solution.py:333
  18.8 0.0 collective-permute-start
  18.8 0.0 copy-done
  18.8 0.0 copy-done.1
  18.8 0.9 %shard_map.86 = (bf16[64,1280]{1,0:T(8,128)(2,1)S(1)}, bf16[64,640]{1,0:T(8,128)(2,1)S(1)}, bf16[64,640]{1,0:T(8,128)(2,1)S(1)}) custom-call(bf16[8,8,1024]{2,1,0:T(8,128)(2,1)S(1)} %all_to_all.15.blocks, bf16[1280,640]{1,0:T(8,128)(2,1)S(1)} %bitcast.6, bf16[640,1280]{1,0:T(8,128)(2,1)S(1)} %bitcast.9), custom_call_target="tpu_custom_call" | custom-call | flops 209715200 | bytes 3276800 | tf_op jit(solution)/shard_map/pallas_call | solution.py:38
  19.7 0.5 collective-permute-done.blocks
  20.1 1.8 %shard_map.88 = (bf16[8,8,1024]{2,1,0:T(8,128)(2,1)S(1)}, bf16[64,1280]{1,0:T(8,128)(2,1)S(1)}, bf16[64,640]{1,0:T(8,128)(2,1)S(1)}, bf16[64,640]{1,0:T(8,128)(2,1)S(1)}) custom-call(bf16[8,8,1024]{2,1,0:T(8,128)(2,1)S(1)} %collective-permute-done.blocks, bf16[1280,640]{1,0:T(8,128)(2,1)S(1)} %bitcast.7, bf16[640,1280]{1,0:T(8,128)(2,1)S(1)} %bitcast.10, ...), custom_call_target="tpu_custom_call" | custom-call | flops 419430400 | bytes 3276800 | tf_op jit(solution)/shard_map/pallas_call | solution.py:38
  21.9 0.2 collective-permute-start.1
  22.1 0.0 copy-start.2
  22.1 0.8 %shard_map.87.own = f32[8,8,1024]{2,1,0:T(8,128)S(1)} custom-call(bf16[64,640]{1,0:T(8,128)(2,1)S(1)} %get-tuple-element.24.hid._.hid_near, bf16[64,640]{1,0:T(8,128)(2,1)S(1)} %get-tuple-element.25.grad.grad_near, bf16[1280,640]{1,0:T(8,128)(2,1)S(1)} %bitcast.8, bf16[640,1280]{1,0:T(8,128)(2,1)S(1)} %bitcast.11), custom_call_target="tpu_custom_call" | custom-call | flops 209715200 | bytes 3276800 | tf_op jit(solution)/shard_map/pallas_call | solution.py:38
  23.0 0.4 collective-permute-done.1.received
  23.4 10.0 %all_to_all.16.shares = bf16[8,8,1024]{2,1,0:T(8,128)(2,1)S(1)} all-to-all(bf16[8,8,1024]{2,1,0:T(8,128)(2,1)S(1)} %shard_map.89), channel_id=1, replica_groups={{0,2,4,6,8,10,12,14},{1,3,5,7,9,11,13,15},{16,18,20,22,24,26,28,30},{17..., dimensions={0} | all-to-all | bytes 262144 | tf_op jit(solution)/shard_map/all_to_all | solution.py:333
  33.3 0.0 copy-done.2
  33.3 2.1 %shard_map.90 = (bf16[16,2,1280]{2,1,0:T(2,128)(2,1)}, f32[3,4,256]{2,1,0:T(4,128)S(1)}, f32[3,4,1280]{2,1,0:T(4,128)S(1)}) custom-call(bf16[8,8,1024]{2,1,0:T(8,128)(2,1)S(1)} %all_to_all.16.shares, bf16[3,256,1280]{2,1,0:T(8,128)(2,1)S(1)} %get-tuple-element.22.tok, bf16[3,256,1280]{2,1,0:T(8,128)(2,1)S(1)} %get-tuple-element.23.dout, ...), custom_call_target="tpu_custom_call" | custom-call | flops 11796480 | bytes 3932160 | tf_op jit(solution)/shard_map/pallas_call | solution.py:38
  35.5 3.5 %all-to-all-start.2 = ((bf16[16,2,1280]{2,1,0:T(2,128)(2,1)}), bf16[16,2,1280]{2,1,0:T(2,128)(2,1)S(1)}, u32[]{:S(2)}, u32[]{:S(2)}) async-start(bf16[16,2,1280]{2,1,0:T(2,128)(2,1)} %get-tuple-element.37), calls=%async_computation.2 | async-start | bytes 163840 | tf_op jit(solution)/shard_map/all_to_all | solution.py:475
  39.0 2.1 %shard_map.92 = (bf16[1280,640]{1,0:T(8,128)(2,1)}, bf16[640,1280]{1,0:T(8,128)(2,1)}) custom-call(bf16[64,1280]{1,0:T(8,128)(2,1)S(1)} %get-tuple-element.31.x_near, bf16[64,640]{1,0:T(8,128)(2,1)S(1)} %get-tuple-element.24.hid._.hid_near, bf16[64,640]{1,0:T(8,128)(2,1)S(1)} %get-tuple-element.25.grad.grad_near, ...), custom_call_target="tpu_custom_call" | custom-call | flops 419430400 | bytes 3276800 | tf_op jit(solution)/shard_map/pallas_call | solution.py:38
  41.1 1.6 %shard_map.91 = bf16[3,256,1280]{2,1,0:T(8,128)(2,1)} custom-call(f32[3,4,256]{2,1,0:T(4,128)S(1)} %get-tuple-element.29.left, f32[3,4,1280]{2,1,0:T(4,128)S(1)} %get-tuple-element.30.right), custom_call_target="tpu_custom_call" | custom-call | flops 7864320 | bytes 1966080 | tf_op jit(solution)/shard_map/pallas_call | solution.py:38
  42.7 3.4 %all-to-all-done.2.terms = bf16[16,2,1280]{2,1,0:T(2,128)(2,1)S(1)} async-done(((bf16[16,2,1280]{2,1,0:T(2,128)(2,1)}), bf16[16,2,1280]{2,1,0:T(2,128)(2,1)S(1)}, u32[]{:S(2)}, u32[]{:S(2)}) %all-to-all-start.2) | async-done | bytes 81952 | tf_op jit(solution)/shard_map/all_to_all | solution.py:475
  46.1 0.7 %shard_map.93 = f32[2,1280]{1,0:T(2,128)} custom-call(bf16[16,2,1280]{2,1,0:T(2,128)(2,1)S(1)} %all-to-all-done.2.terms), custom_call_target="tpu_custom_call" | custom-call | flops 40960 | bytes 81920 | tf_op jit(solution)/shard_map/pallas_call | solution.py:38
  (2 shorter events, 0.0 us)
Async XLA Ops:
  4.0 14.7 %copy-start = (bf16[1,1280,640]{2,1,0:T(8,128)(2,1)S(1)}, bf16[1,1280,640]{2,1,0:T(8,128)(2,1)}, u32[]{:S(2)}) copy-start(bf16[1,1280,640]{2,1,0:T(8,128)(2,1)} %param.7) | copy-start | bytes 4915204
  4.0 14.7 %copy-start.1 = (bf16[1,640,1280]{2,1,0:T(8,128)(2,1)S(1)}, bf16[1,640,1280]{2,1,0:T(8,128)(2,1)}, u32[]{:S(2)}) copy-start(bf16[1,640,1280]{2,1,0:T(8,128)(2,1)} %param.8) | copy-start | bytes 4915204
  18.8 1.3 %collective-permute-start = (bf16[8,8,1024]{2,1,0:T(8,128)(2,1)S(1)}, bf16[8,8,1024]{2,1,0:T(8,128)(2,1)S(1)}, u32[]{:S(2)}, u32[]{:S(2)}) collective-permute-start(bf16[8,8,1024]{2,1,0:T(8,128)(2,1)S(1)} %all_to_all.15.blocks), channel_id=1, source_target_pairs={{0,1},{1,0},{2,3},{3,2},{4,5},{5,4},{6,7},{7,6},{8,9},{9,8},{10,11... | collective-permute-start | bytes 393224 | tf_op jit(solution)/shard_map/ppermute | solution.py:340
  21.9 1.4 %collective-permute-start.1 = (bf16[8,8,1024]{2,1,0:T(8,128)(2,1)S(1)}, bf16[8,8,1024]{2,1,0:T(8,128)(2,1)S(1)}, u32[]{:S(2)}, u32[]{:S(2)}) collective-permute-start(bf16[8,8,1024]{2,1,0:T(8,128)(2,1)S(1)} %get-tuple-element.26), channel_id=1, source_target_pairs={{0,1},{1,0},{2,3},{3,2},{4,5},{5,4},{6,7},{7,6},{8,9},{9,8},{10,11... | collective-permute-start | bytes 393224 | tf_op jit(solution)/shard_map/ppermute | solution.py:340
  22.1 11.2 %copy-start.2 = (bf16[1280,2]{0,1:T(2,128)(2,1)S(1)}, bf16[1280,2]{0,1:T(2,128)(2,1)}, u32[]{:S(2)}) copy-start(bf16[1280,2]{0,1:T(2,128)(2,1)} %param.6) | copy-start | bytes 15364
  35.5 10.6 %all-to-all-start.2 = ((bf16[16,2,1280]{2,1,0:T(2,128)(2,1)}), bf16[16,2,1280]{2,1,0:T(2,128)(2,1)S(1)}, u32[]{:S(2)}, u32[]{:S(2)}) async-start(bf16[16,2,1280]{2,1,0:T(2,128)(2,1)} %get-tuple-element.37), calls=%async_computation.2 | async-start | bytes 163840 | tf_op jit(solution)/shard_map/all_to_all | solution.py:475

commit v14 on v11

--- a/solution.py
+++ b/solution.py
@@ -114,6 +114,8 @@
         block[:, to, column : column + extra] = values[:, main:]
 
     fetch_router.wait()
+    for copy in fetch_dout:
+        copy.start()
     logits = {}
     combs = {}
     disps = {}
@@ -132,13 +134,10 @@
         if step < images:
             fetch_tok[step].wait()
             if step == 0:
-                for copy in fetch_dout:
-                    copy.start()
+                fetch_weight.start()
             logits[step] = dot(router_t[...], tok[step], NT)
         else:
             fetch_dout[step - images].wait()
-            if step == images:
-                fetch_weight.start()
         if 0 <= step - 1 < images:
             softmaxes(step - 1)
         if step >= images:

time: 47.6 us -> 46.9 us (0.985)
  Pallas kernels: 14.1 us -> 13.4 us
    pallas_call x10, Pallas kernels: 14.1 us -> 13.4 us  [call(): pl.pallas_call(kernel, out_shape=outs, in_specs=in_specs, out_specs=out_s...]
  transfers between devices with their start and end apart: 3 -> 3, of which waited for: 3 -> 3; matrix products, arithmetic and copies ran while one was open for 0% -> 0% of each run, Pallas kernels for 11% -> 12%
where the time goes in v14:
time: 46.9 us; the launch traced here: 46.7 us
  blocking collectives  24.5 us (52%)
  Pallas kernels  13.4 us (29%)
  waiting for transfers between devices  4.21 us (9%)
  starting transfers between devices  3.72 us (8%)
  between operations  0.73 us (2%)
    all_to_all x2, blocking collectives, swap_chips(): lax.all_to_all(blocks, 'expert', split_axis=0, concat_axis=0, axis_index_...  24.5 us
    pallas_call x10, Pallas kernels, call(): pl.pallas_call(kernel, out_shape=outs, in_specs=in_specs, out_specs=out_s...  13.4 us
    all_to_all x1, starting transfers between devices, per_device(): lax.all_to_all(terms, 'expert', split_axis=0, concat_axis=0, tiled=True)  3.5 us
    all_to_all x1, waiting for transfers between devices, per_device(): lax.all_to_all(terms, 'expert', split_axis=0, concat_axis=0, tiled=True)  3.39 us
  transfers between devices with their start and end apart: 3, of which 3 were waited for; matrix products, arithmetic and copies ran while one was open for 0% of the time, Pallas kernels for 12%

profile of v14, /device:TPU:0, one launch (start us, length us, event | category | flops | bytes accessed | tf_op | source)
XLA Modules:
  0.0 46.7 jit_solution(11225573408524528401)
XLA Ops:
  0.6 3.4 %shard_map.84 = (bf16[2,8,1024]{2,1,0:T(8,128)(2,1)S(1)}, bf16[3,256,1280]{2,1,0:T(8,128)(2,1)S(1)}, bf16[3,256,1280]{2,1,0:T(8,128)(2,1)S(1)}, f32[3,2,256]{2,1...) custom-call(bf16[3,256,1280]{2,1,0:T(8,128)(2,1)} %tokens.1, bf16[2,1280]{1,0:T(2,128)(2,1)} %bitcast.9, ...), custom_call_target="tpu_custom_call" | custom-call | flops 11796480 | bytes 3932160 | tf_op jit(solution)/shard_map/pallas_call | solution.py:38
  4.0 0.0 copy-start
  4.1 14.6 %all_to_all.15.blocks = bf16[8,8,1024]{2,1,0:T(8,128)(2,1)S(1)} all-to-all(bf16[8,8,1024]{2,1,0:T(8,128)(2,1)S(1)} %shard_map.85), channel_id=1, replica_groups={{0,2,4,6,8,10,12,14},{1,3,5,7,9,11,13,15},{16,18,20,22,24,26,28,30},{17..., dimensions={0} | all-to-all | bytes 262144 | tf_op jit(solution)/shard_map/all_to_all | solution.py:339
  18.6 0.0 collective-permute-start
  18.6 0.0 copy-done
  18.6 0.9 %shard_map.86 = (bf16[64,1280]{1,0:T(8,128)(2,1)S(1)}, bf16[64,640]{1,0:T(8,128)(2,1)S(1)}, bf16[64,640]{1,0:T(8,128)(2,1)S(1)}) custom-call(bf16[8,8,1024]{2,1,0:T(8,128)(2,1)S(1)} %all_to_all.15.blocks, bf16[1280,640]{1,0:T(8,128)(2,1)S(1)} %get-tuple-element.25.w_in, bf16[640,1280]{1,0:T(8,128)(2,1)S(1)} %bitcast.6), custom_call_target="tpu_custom_call" | custom-call | flops 209715200 | bytes 3276800 | tf_op jit(solution)/shard_map/pallas_call | solution.py:38
  19.5 0.5 collective-permute-done.blocks
  20.0 1.8 %shard_map.88 = (bf16[8,8,1024]{2,1,0:T(8,128)(2,1)S(1)}, bf16[64,1280]{1,0:T(8,128)(2,1)S(1)}, bf16[64,640]{1,0:T(8,128)(2,1)S(1)}, bf16[64,640]{1,0:T(8,128)(2,1)S(1)}) custom-call(bf16[8,8,1024]{2,1,0:T(8,128)(2,1)S(1)} %collective-permute-done.blocks, bf16[1280,640]{1,0:T(8,128)(2,1)S(1)} %get-tuple-element.25.w_in, bf16[640,1280]{1,0:T(8,128)(2,1)S(1)} %bitcast.7, ...), custom_call_target="tpu_custom_call" | custom-call | flops 419430400 | bytes 3276800 | tf_op jit(solution)/shard_map/pallas_call | solution.py:38
  21.8 0.0 copy-start.2
  21.8 0.2 collective-permute-start.1
  22.0 0.0 copy-start.1
  22.0 0.8 %shard_map.87.own = f32[8,8,1024]{2,1,0:T(8,128)S(1)} custom-call(bf16[64,640]{1,0:T(8,128)(2,1)S(1)} %get-tuple-element.26.hid._.hid_near, bf16[64,640]{1,0:T(8,128)(2,1)S(1)} %get-tuple-element.27.grad.grad_near, bf16[1280,640]{1,0:T(8,128)(2,1)S(1)} %get-tuple-element.25.w_in, bf16[640,1280]{1,0:T(8,128)(2,1)S(1)} %bitcast.8), custom_call_target="tpu_custom_call" | custom-call | flops 209715200 | bytes 3276800 | tf_op jit(solution)/shard_map/pallas_call | solution.py:38
  22.9 0.4 collective-permute-done.1.received
  23.2 0.0 copy-done.2
  23.3 10.0 %all_to_all.16.shares = bf16[8,8,1024]{2,1,0:T(8,128)(2,1)S(1)} all-to-all(bf16[8,8,1024]{2,1,0:T(8,128)(2,1)S(1)} %shard_map.89), channel_id=1, replica_groups={{0,2,4,6,8,10,12,14},{1,3,5,7,9,11,13,15},{16,18,20,22,24,26,28,30},{17..., dimensions={0} | all-to-all | bytes 262144 | tf_op jit(solution)/shard_map/all_to_all | solution.py:339
  33.2 0.0 copy-done.1
  33.2 0.0 copy-start.3
  33.2 2.1 %shard_map.90 = (bf16[16,2,1280]{2,1,0:T(2,128)(2,1)}, f32[3,4,256]{2,1,0:T(4,128)S(1)}, f32[3,4,1280]{2,1,0:T(4,128)S(1)}) custom-call(bf16[8,8,1024]{2,1,0:T(8,128)(2,1)S(1)} %all_to_all.16.shares, bf16[3,256,1280]{2,1,0:T(8,128)(2,1)S(1)} %get-tuple-element.23.tok, bf16[3,256,1280]{2,1,0:T(8,128)(2,1)S(1)} %get-tuple-element.24.dout, ...), custom_call_target="tpu_custom_call" | custom-call | flops 11796480 | bytes 3932160 | tf_op jit(solution)/shard_map/pallas_call | solution.py:38
  35.4 3.5 %all-to-all-start.2 = ((bf16[16,2,1280]{2,1,0:T(2,128)(2,1)}), bf16[16,2,1280]{2,1,0:T(2,128)(2,1)S(1)}, u32[]{:S(2)}, u32[]{:S(2)}) async-start(bf16[16,2,1280]{2,1,0:T(2,128)(2,1)} %get-tuple-element.39), calls=%async_computation.2 | async-start | bytes 163840 | tf_op jit(solution)/shard_map/all_to_all | solution.py:482
  38.9 0.0 copy-done.3
  38.9 2.1 %shard_map.92 = (bf16[1280,640]{1,0:T(8,128)(2,1)}, bf16[640,1280]{1,0:T(8,128)(2,1)}) custom-call(bf16[64,1280]{1,0:T(8,128)(2,1)S(1)} %get-tuple-element.33.x_near, bf16[64,640]{1,0:T(8,128)(2,1)S(1)} %get-tuple-element.26.hid._.hid_near, bf16[64,640]{1,0:T(8,128)(2,1)S(1)} %get-tuple-element.27.grad.grad_near, ...), custom_call_target="tpu_custom_call" | custom-call | flops 419430400 | bytes 3276800 | tf_op jit(solution)/shard_map/pallas_call | solution.py:38
  41.0 1.6 %shard_map.91 = bf16[3,256,1280]{2,1,0:T(8,128)(2,1)} custom-call(f32[3,4,256]{2,1,0:T(4,128)S(1)} %get-tuple-element.31.left, f32[3,4,1280]{2,1,0:T(4,128)S(1)} %get-tuple-element.32.right), custom_call_target="tpu_custom_call" | custom-call | flops 7864320 | bytes 1966080 | tf_op jit(solution)/shard_map/pallas_call | solution.py:38
  42.6 3.4 %all-to-all-done.2.terms = bf16[16,2,1280]{2,1,0:T(2,128)(2,1)S(1)} async-done(((bf16[16,2,1280]{2,1,0:T(2,128)(2,1)}), bf16[16,2,1280]{2,1,0:T(2,128)(2,1)S(1)}, u32[]{:S(2)}, u32[]{:S(2)}) %all-to-all-start.2) | async-done | bytes 81952 | tf_op jit(solution)/shard_map/all_to_all | solution.py:482
  46.0 0.7 %shard_map.93 = f32[2,1280]{1,0:T(2,128)} custom-call(bf16[16,2,1280]{2,1,0:T(2,128)(2,1)S(1)} %all-to-all-done.2.terms), custom_call_target="tpu_custom_call" | custom-call | flops 40960 | bytes 81920 | tf_op jit(solution)/shard_map/pallas_call | solution.py:38
  (2 shorter events, 0.0 us)
Async XLA Ops:
  4.0 14.6 %copy-start = (bf16[1,640,1280]{2,1,0:T(8,128)(2,1)S(1)}, bf16[1,640,1280]{2,1,0:T(8,128)(2,1)}, u32[]{:S(2)}) copy-start(bf16[1,640,1280]{2,1,0:T(8,128)(2,1)} %param.8) | copy-start | bytes 4915204
  18.6 1.3 %collective-permute-start = (bf16[8,8,1024]{2,1,0:T(8,128)(2,1)S(1)}, bf16[8,8,1024]{2,1,0:T(8,128)(2,1)S(1)}, u32[]{:S(2)}, u32[]{:S(2)}) collective-permute-start(bf16[8,8,1024]{2,1,0:T(8,128)(2,1)S(1)} %all_to_all.15.blocks), channel_id=1, source_target_pairs={{0,1},{1,0},{2,3},{3,2},{4,5},{5,4},{6,7},{7,6},{8,9},{9,8},{10,11... | collective-permute-start | bytes 393224 | tf_op jit(solution)/shard_map/ppermute | solution.py:346
  21.8 1.5 %copy-start.2 = (bf16[64,640]{1,0:T(8,128)(2,1)}, bf16[64,640]{1,0:T(8,128)(2,1)S(1)}, u32[]{:S(2)}) copy-start(bf16[64,640]{1,0:T(8,128)(2,1)S(1)} %get-tuple-element.36.grad_far) | copy-start | bytes 245764
  21.8 1.4 %collective-permute-start.1 = (bf16[8,8,1024]{2,1,0:T(8,128)(2,1)S(1)}, bf16[8,8,1024]{2,1,0:T(8,128)(2,1)S(1)}, u32[]{:S(2)}, u32[]{:S(2)}) collective-permute-start(bf16[8,8,1024]{2,1,0:T(8,128)(2,1)S(1)} %get-tuple-element.28), channel_id=1, source_target_pairs={{0,1},{1,0},{2,3},{3,2},{4,5},{5,4},{6,7},{7,6},{8,9},{9,8},{10,11... | collective-permute-start | bytes 393224 | tf_op jit(solution)/shard_map/ppermute | solution.py:346
  22.0 11.2 %copy-start.1 = (bf16[1280,2]{0,1:T(2,128)(2,1)S(1)}, bf16[1280,2]{0,1:T(2,128)(2,1)}, u32[]{:S(2)}) copy-start(bf16[1280,2]{0,1:T(2,128)(2,1)} %param.6) | copy-start | bytes 15364
  33.2 5.6 %copy-start.3 = (bf16[64,640]{1,0:T(8,128)(2,1)S(1)}, bf16[64,640]{1,0:T(8,128)(2,1)}, u32[]{:S(2)}) copy-start(bf16[64,640]{1,0:T(8,128)(2,1)} %copy-done.2) | copy-start | bytes 245764
  35.4 10.6 %all-to-all-start.2 = ((bf16[16,2,1280]{2,1,0:T(2,128)(2,1)}), bf16[16,2,1280]{2,1,0:T(2,128)(2,1)S(1)}, u32[]{:S(2)}, u32[]{:S(2)}) async-start(bf16[16,2,1280]{2,1,0:T(2,128)(2,1)} %get-tuple-element.39), calls=%async_computation.2 | async-start | bytes 163840 | tf_op jit(solution)/shard_map/all_to_all | solution.py:482

commit v15 on v13

--- a/solution.py
+++ b/solution.py
@@ -130,7 +130,7 @@
     for step in range(2 * images):
         if step < images:
             fetch_tok[step].wait()
-            logits[step] = dot(router_t[...], tok[step], NT)
+            logits[step] = dot(tok[step], router_t[...], NT).T
         else:
             fetch_dout[step - images].wait()
         if 0 <= step - 1 < images:
@@ -269,8 +269,8 @@
     grads = {}
 
     def products(b):
-        by_dout[b] = dot(stacked_b, dout[b], NT)
-        by_tok[b] = dot(stacked_b, tok[b], NT)
+        by_dout[b] = dot(dout[b], stacked_b, NT).T
+        by_tok[b] = dot(tok[b], stacked_b, NT).T
 
     def logits_grad(b):
         grad_comb = jnp.concatenate(

time: 47.1 us -> 47.3 us (level)
  transfers between devices with their start and end apart: 3 -> 3, of which waited for: 3 -> 3; matrix products, arithmetic and copies ran while one was open for 0% -> 0% of each run, Pallas kernels for 12% -> 11%
where the time goes in v15:
time: 47.3 us; the launch traced here: 47 us
  blocking collectives  24.7 us (52%)
  Pallas kernels  13.6 us (29%)
  waiting for transfers between devices  4.22 us (9%)
  starting transfers between devices  3.72 us (8%)
  between operations  0.72 us (2%)
    all_to_all x2, blocking collectives, swap_chips(): lax.all_to_all(blocks, 'expert', split_axis=0, concat_axis=0, axis_index_...  24.7 us
    pallas_call x10, Pallas kernels, call(): pl.pallas_call(kernel, out_shape=outs, in_specs=in_specs, out_specs=out_s...  13.6 us
    all_to_all x1, starting transfers between devices, per_device(): lax.all_to_all(terms, 'expert', split_axis=0, concat_axis=0, tiled=True)  3.5 us
    all_to_all x1, waiting for transfers between devices, per_device(): lax.all_to_all(terms, 'expert', split_axis=0, concat_axis=0, tiled=True)  3.4 us
  transfers between devices with their start and end apart: 3, of which 3 were waited for; matrix products, arithmetic and copies ran while one was open for 0% of the time, Pallas kernels for 11%

profile of v15, /device:TPU:0, one launch (start us, length us, event | category | flops | bytes accessed | tf_op | source)
XLA Modules:
  0.0 47.0 jit_solution(12181241792659170170)
XLA Ops:
  0.6 3.5 %shard_map.84 = (bf16[2,8,1024]{2,1,0:T(8,128)(2,1)S(1)}, bf16[3,256,1280]{2,1,0:T(8,128)(2,1)S(1)}, bf16[3,256,1280]{2,1,0:T(8,128)(2,1)S(1)}, f32[3,2,256]{2,1,0:T(2,128)S(1)}, f32[3,2,256]{2,1,0:T(2,128)S(1)}) custom-call(bf16[3,256,1280]{2,1,0:T(8,128)(2,1)} %tokens.1, bf16[2,1280]{1,0:T(2,128)(2,1)} %bitcast.12, bf16[3,256,1280]{2,1,0:T(8,128)(2,1)} %d_out.1), custom_call_target="tpu_custom_call" | custom-call | flops 11796480 | bytes 3932160 | tf_op jit(solution)/shard_map/pallas_call | solution.py:38
  4.2 0.0 copy-start
  4.2 0.0 copy-start.1
  4.2 14.7 %all_to_all.15.blocks = bf16[8,8,1024]{2,1,0:T(8,128)(2,1)S(1)} all-to-all(bf16[8,8,1024]{2,1,0:T(8,128)(2,1)S(1)} %shard_map.85), channel_id=1, replica_groups={{0,2,4,6,8,10,12,14},{1,3,5,7,9,11,13,15},{16,18,20,22,24,26,28,30},{17..., dimensions={0} | all-to-all | bytes 262144 | tf_op jit(solution)/shard_map/all_to_all | solution.py:333
  18.9 0.0 collective-permute-start
  18.9 0.0 copy-done
  18.9 0.0 copy-done.1
  18.9 0.9 %shard_map.86 = (bf16[64,1280]{1,0:T(8,128)(2,1)S(1)}, bf16[64,640]{1,0:T(8,128)(2,1)S(1)}, bf16[64,640]{1,0:T(8,128)(2,1)S(1)}) custom-call(bf16[8,8,1024]{2,1,0:T(8,128)(2,1)S(1)} %all_to_all.15.blocks, bf16[1280,640]{1,0:T(8,128)(2,1)S(1)} %bitcast.6, bf16[640,1280]{1,0:T(8,128)(2,1)S(1)} %bitcast.9), custom_call_target="tpu_custom_call" | custom-call | flops 209715200 | bytes 3276800 | tf_op jit(solution)/shard_map/pallas_call | solution.py:38
  19.8 0.5 collective-permute-done.blocks
  20.2 1.8 %shard_map.88 = (bf16[8,8,1024]{2,1,0:T(8,128)(2,1)S(1)}, bf16[64,1280]{1,0:T(8,128)(2,1)S(1)}, bf16[64,640]{1,0:T(8,128)(2,1)S(1)}, bf16[64,640]{1,0:T(8,128)(2,1)S(1)}) custom-call(bf16[8,8,1024]{2,1,0:T(8,128)(2,1)S(1)} %collective-permute-done.blocks, bf16[1280,640]{1,0:T(8,128)(2,1)S(1)} %bitcast.7, bf16[640,1280]{1,0:T(8,128)(2,1)S(1)} %bitcast.10, ...), custom_call_target="tpu_custom_call" | custom-call | flops 419430400 | bytes 3276800 | tf_op jit(solution)/shard_map/pallas_call | solution.py:38
  22.1 0.2 collective-permute-start.1
  22.3 0.0 copy-start.2
  22.3 0.8 %shard_map.87.own = f32[8,8,1024]{2,1,0:T(8,128)S(1)} custom-call(bf16[64,640]{1,0:T(8,128)(2,1)S(1)} %get-tuple-element.24.hid._.hid_near, bf16[64,640]{1,0:T(8,128)(2,1)S(1)} %get-tuple-element.25.grad.grad_near, bf16[1280,640]{1,0:T(8,128)(2,1)S(1)} %bitcast.8, bf16[640,1280]{1,0:T(8,128)(2,1)S(1)} %bitcast.11), custom_call_target="tpu_custom_call" | custom-call | flops 209715200 | bytes 3276800 | tf_op jit(solution)/shard_map/pallas_call | solution.py:38
  23.1 0.4 collective-permute-done.1.received
  23.5 10.0 %all_to_all.16.shares = bf16[8,8,1024]{2,1,0:T(8,128)(2,1)S(1)} all-to-all(bf16[8,8,1024]{2,1,0:T(8,128)(2,1)S(1)} %shard_map.89), channel_id=1, replica_groups={{0,2,4,6,8,10,12,14},{1,3,5,7,9,11,13,15},{16,18,20,22,24,26,28,30},{17..., dimensions={0} | all-to-all | bytes 262144 | tf_op jit(solution)/shard_map/all_to_all | solution.py:333
  33.5 0.0 copy-done.2
  33.5 2.2 %shard_map.90 = (bf16[16,2,1280]{2,1,0:T(2,128)(2,1)}, f32[3,4,256]{2,1,0:T(4,128)S(1)}, f32[3,4,1280]{2,1,0:T(4,128)S(1)}) custom-call(bf16[8,8,1024]{2,1,0:T(8,128)(2,1)S(1)} %all_to_all.16.shares, bf16[3,256,1280]{2,1,0:T(8,128)(2,1)S(1)} %get-tuple-element.22.tok, bf16[3,256,1280]{2,1,0:T(8,128)(2,1)S(1)} %get-tuple-element.23.dout, ...), custom_call_target="tpu_custom_call" | custom-call | flops 11796480 | bytes 3932160 | tf_op jit(solution)/shard_map/pallas_call | solution.py:38
  35.7 3.5 %all-to-all-start.2 = ((bf16[16,2,1280]{2,1,0:T(2,128)(2,1)}), bf16[16,2,1280]{2,1,0:T(2,128)(2,1)S(1)}, u32[]{:S(2)}, u32[]{:S(2)}) async-start(bf16[16,2,1280]{2,1,0:T(2,128)(2,1)} %get-tuple-element.37), calls=%async_computation.2 | async-start | bytes 163840 | tf_op jit(solution)/shard_map/all_to_all | solution.py:475
  39.2 2.1 %shard_map.92 = (bf16[1280,640]{1,0:T(8,128)(2,1)}, bf16[640,1280]{1,0:T(8,128)(2,1)}) custom-call(bf16[64,1280]{1,0:T(8,128)(2,1)S(1)} %get-tuple-element.31.x_near, bf16[64,640]{1,0:T(8,128)(2,1)S(1)} %get-tuple-element.24.hid._.hid_near, bf16[64,640]{1,0:T(8,128)(2,1)S(1)} %get-tuple-element.25.grad.grad_near, ...), custom_call_target="tpu_custom_call" | custom-call | flops 419430400 | bytes 3276800 | tf_op jit(solution)/shard_map/pallas_call | solution.py:38
  41.3 1.6 %shard_map.91 = bf16[3,256,1280]{2,1,0:T(8,128)(2,1)} custom-call(f32[3,4,256]{2,1,0:T(4,128)S(1)} %get-tuple-element.29.left, f32[3,4,1280]{2,1,0:T(4,128)S(1)} %get-tuple-element.30.right), custom_call_target="tpu_custom_call" | custom-call | flops 7864320 | bytes 1966080 | tf_op jit(solution)/shard_map/pallas_call | solution.py:38
  42.9 3.4 %all-to-all-done.2.terms = bf16[16,2,1280]{2,1,0:T(2,128)(2,1)S(1)} async-done(((bf16[16,2,1280]{2,1,0:T(2,128)(2,1)}), bf16[16,2,1280]{2,1,0:T(2,128)(2,1)S(1)}, u32[]{:S(2)}, u32[]{:S(2)}) %all-to-all-start.2) | async-done | bytes 81952 | tf_op jit(solution)/shard_map/all_to_all | solution.py:475
  46.3 0.7 %shard_map.93 = f32[2,1280]{1,0:T(2,128)} custom-call(bf16[16,2,1280]{2,1,0:T(2,128)(2,1)S(1)} %all-to-all-done.2.terms), custom_call_target="tpu_custom_call" | custom-call | flops 40960 | bytes 81920 | tf_op jit(solution)/shard_map/pallas_call | solution.py:38
  (2 shorter events, 0.0 us)
Async XLA Ops:
  4.2 14.7 %copy-start = (bf16[1,1280,640]{2,1,0:T(8,128)(2,1)S(1)}, bf16[1,1280,640]{2,1,0:T(8,128)(2,1)}, u32[]{:S(2)}) copy-start(bf16[1,1280,640]{2,1,0:T(8,128)(2,1)} %param.7) | copy-start | bytes 4915204
  4.2 14.7 %copy-start.1 = (bf16[1,640,1280]{2,1,0:T(8,128)(2,1)S(1)}, bf16[1,640,1280]{2,1,0:T(8,128)(2,1)}, u32[]{:S(2)}) copy-start(bf16[1,640,1280]{2,1,0:T(8,128)(2,1)} %param.8) | copy-start | bytes 4915204
  18.9 1.3 %collective-permute-start = (bf16[8,8,1024]{2,1,0:T(8,128)(2,1)S(1)}, bf16[8,8,1024]{2,1,0:T(8,128)(2,1)S(1)}, u32[]{:S(2)}, u32[]{:S(2)}) collective-permute-start(bf16[8,8,1024]{2,1,0:T(8,128)(2,1)S(1)} %all_to_all.15.blocks), channel_id=1, source_target_pairs={{0,1},{1,0},{2,3},{3,2},{4,5},{5,4},{6,7},{7,6},{8,9},{9,8},{10,11... | collective-permute-start | bytes 393224 | tf_op jit(solution)/shard_map/ppermute | solution.py:340
  22.1 1.4 %collective-permute-start.1 = (bf16[8,8,1024]{2,1,0:T(8,128)(2,1)S(1)}, bf16[8,8,1024]{2,1,0:T(8,128)(2,1)S(1)}, u32[]{:S(2)}, u32[]{:S(2)}) collective-permute-start(bf16[8,8,1024]{2,1,0:T(8,128)(2,1)S(1)} %get-tuple-element.26), channel_id=1, source_target_pairs={{0,1},{1,0},{2,3},{3,2},{4,5},{5,4},{6,7},{7,6},{8,9},{9,8},{10,11... | collective-permute-start | bytes 393224 | tf_op jit(solution)/shard_map/ppermute | solution.py:340
  22.3 11.2 %copy-start.2 = (bf16[1280,2]{0,1:T(2,128)(2,1)S(1)}, bf16[1280,2]{0,1:T(2,128)(2,1)}, u32[]{:S(2)}) copy-start(bf16[1280,2]{0,1:T(2,128)(2,1)} %param.6) | copy-start | bytes 15364
  35.7 10.6 %all-to-all-start.2 = ((bf16[16,2,1280]{2,1,0:T(2,128)(2,1)}), bf16[16,2,1280]{2,1,0:T(2,128)(2,1)S(1)}, u32[]{:S(2)}, u32[]{:S(2)}) async-start(bf16[16,2,1280]{2,1,0:T(2,128)(2,1)} %get-tuple-element.37), calls=%async_computation.2 | async-start | bytes 163840 | tf_op jit(solution)/shard_map/all_to_all | solution.py:475

commit v16 on v13

--- a/solution.py
+++ b/solution.py
@@ -87,6 +87,7 @@
     comb_out,
     router_t,
     block,
+    tok_sems,
     sems,
     other_sems,
 ):
@@ -95,14 +96,26 @@
     extra = tok.shape[2] - main
     fetch_router = pltpu.make_async_copy(router_hbm, router_t, other_sems.at[0])
     fetch_router.start()
-    fetch_tok = [
-        pltpu.make_async_copy(tokens.at[b], tok.at[b], sems.at[b]) for b in range(images)
+    fetch_tok = []
+    for b in range(images):
+        parts = max(4 >> b, 1)
+        step = tok.shape[1] // parts
+        fetch_tok.append(
+            [
+                pltpu.make_async_copy(
+                    tokens.at[b, pl.ds(i * step, step)],
+                    tok.at[b, pl.ds(i * step, step)],
+                    tok_sems.at[b, i],
+                )
+                for i in range(parts)
+            ]
+        )
+    fetch_dout = [
+        pltpu.make_async_copy(d_out.at[b], dout.at[b], sems.at[b]) for b in range(images)
     ]
-    fetch_dout = [
-        pltpu.make_async_copy(d_out.at[b], dout.at[b], sems.at[images + b]) for b in range(images)
-    ]
-    for copy in fetch_tok:
-        copy.start()
+    for copies in fetch_tok:
+        for copy in copies:
+            copy.start()
     block[...] = jnp.zeros_like(block)
 
     def put(row, values):
@@ -129,7 +142,8 @@
 
     for step in range(2 * images):
         if step < images:
-            fetch_tok[step].wait()
+            for copy in fetch_tok[step]:
+                copy.wait()
             logits[step] = dot(router_t[...], tok[step], NT)
         else:
             fetch_dout[step - images].wait()
@@ -368,7 +382,8 @@
         [
             pltpu.VMEM((slots, width), BF16),
             pltpu.VMEM((slots, rows, main), F32),
-            pltpu.SemaphoreType.DMA((2 * images,)),
+            pltpu.SemaphoreType.DMA((images, 4)),
+            pltpu.SemaphoreType.DMA((images,)),
             pltpu.SemaphoreType.DMA((2,)),
         ],
         (6 * slots * big, 4 * big),

time: 47.1 us -> 47.3 us (level)
  no operation moved by 1% of the time
where the time goes in v16:
time: 47.3 us; the launch traced here: 47 us
  blocking collectives  24.7 us (52%)
  Pallas kernels  13.7 us (29%)
  waiting for transfers between devices  4.21 us (9%)
  starting transfers between devices  3.72 us (8%)
  between operations  0.72 us (2%)
    all_to_all x2, blocking collectives, swap_chips(): lax.all_to_all(blocks, 'expert', split_axis=0, concat_axis=0, axis_index_...  24.7 us
    pallas_call x10, Pallas kernels, call(): pl.pallas_call(kernel, out_shape=outs, in_specs=in_specs, out_specs=out_s...  13.7 us
    all_to_all x1, starting transfers between devices, per_device(): lax.all_to_all(terms, 'expert', split_axis=0, concat_axis=0, tiled=True)  3.5 us
    all_to_all x1, waiting for transfers between devices, per_device(): lax.all_to_all(terms, 'expert', split_axis=0, concat_axis=0, tiled=True)  3.39 us
  transfers between devices with their start and end apart: 3, of which 3 were waited for; matrix products, arithmetic and copies ran while one was open for 0% of the time, Pallas kernels for 12%

profile of v16, /device:TPU:0, one launch (start us, length us, event | category | flops | bytes accessed | tf_op | source)
XLA Modules:
  0.0 47.0 jit_solution(2555513200329214338)
XLA Ops:
  0.6 3.6 %shard_map.84 = (bf16[2,8,1024]{2,1,0:T(8,128)(2,1)S(1)}, bf16[3,256,1280]{2,1,0:T(8,128)(2,1)S(1)}, bf16[3,256,1280]{2,1,0:T(8,128)(2,1)S(1)}, f32[3,2,256]{2,1,0:T(2,128)S(1)}, f32[3,2,256]{2,1,0:T(2,128)S(1)}) custom-call(bf16[3,256,1280]{2,1,0:T(8,128)(2,1)} %tokens.1, bf16[2,1280]{1,0:T(2,128)(2,1)} %bitcast.12, bf16[3,256,1280]{2,1,0:T(8,128)(2,1)} %d_out.1), custom_call_target="tpu_custom_call" | custom-call | flops 11796480 | bytes 3932160 | tf_op jit(solution)/shard_map/pallas_call | solution.py:38
  4.2 0.0 copy-start
  4.2 0.0 copy-start.1
  4.3 14.7 %all_to_all.15.blocks = bf16[8,8,1024]{2,1,0:T(8,128)(2,1)S(1)} all-to-all(bf16[8,8,1024]{2,1,0:T(8,128)(2,1)S(1)} %shard_map.85), channel_id=1, replica_groups={{0,2,4,6,8,10,12,14},{1,3,5,7,9,11,13,15},{16,18,20,22,24,26,28,30},{17..., dimensions={0} | all-to-all | bytes 262144 | tf_op jit(solution)/shard_map/all_to_all | solution.py:347
  19.0 0.0 collective-permute-start
  19.0 0.0 copy-done
  19.0 0.0 copy-done.1
  19.0 0.9 %shard_map.86 = (bf16[64,1280]{1,0:T(8,128)(2,1)S(1)}, bf16[64,640]{1,0:T(8,128)(2,1)S(1)}, bf16[64,640]{1,0:T(8,128)(2,1)S(1)}) custom-call(bf16[8,8,1024]{2,1,0:T(8,128)(2,1)S(1)} %all_to_all.15.blocks, bf16[1280,640]{1,0:T(8,128)(2,1)S(1)} %bitcast.6, bf16[640,1280]{1,0:T(8,128)(2,1)S(1)} %bitcast.9), custom_call_target="tpu_custom_call" | custom-call | flops 209715200 | bytes 3276800 | tf_op jit(solution)/shard_map/pallas_call | solution.py:38
  19.9 0.5 collective-permute-done.blocks
  20.3 1.8 %shard_map.88 = (bf16[8,8,1024]{2,1,0:T(8,128)(2,1)S(1)}, bf16[64,1280]{1,0:T(8,128)(2,1)S(1)}, bf16[64,640]{1,0:T(8,128)(2,1)S(1)}, bf16[64,640]{1,0:T(8,128)(2,1)S(1)}) custom-call(bf16[8,8,1024]{2,1,0:T(8,128)(2,1)S(1)} %collective-permute-done.blocks, bf16[1280,640]{1,0:T(8,128)(2,1)S(1)} %bitcast.7, bf16[640,1280]{1,0:T(8,128)(2,1)S(1)} %bitcast.10, ...), custom_call_target="tpu_custom_call" | custom-call | flops 419430400 | bytes 3276800 | tf_op jit(solution)/shard_map/pallas_call | solution.py:38
  22.1 0.2 collective-permute-start.1
  22.3 0.0 copy-start.2
  22.3 0.8 %shard_map.87.own = f32[8,8,1024]{2,1,0:T(8,128)S(1)} custom-call(bf16[64,640]{1,0:T(8,128)(2,1)S(1)} %get-tuple-element.24.hid._.hid_near, bf16[64,640]{1,0:T(8,128)(2,1)S(1)} %get-tuple-element.25.grad.grad_near, bf16[1280,640]{1,0:T(8,128)(2,1)S(1)} %bitcast.8, bf16[640,1280]{1,0:T(8,128)(2,1)S(1)} %bitcast.11), custom_call_target="tpu_custom_call" | custom-call | flops 209715200 | bytes 3276800 | tf_op jit(solution)/shard_map/pallas_call | solution.py:38
  23.2 0.4 collective-permute-done.1.received
  23.6 10.0 %all_to_all.16.shares = bf16[8,8,1024]{2,1,0:T(8,128)(2,1)S(1)} all-to-all(bf16[8,8,1024]{2,1,0:T(8,128)(2,1)S(1)} %shard_map.89), channel_id=1, replica_groups={{0,2,4,6,8,10,12,14},{1,3,5,7,9,11,13,15},{16,18,20,22,24,26,28,30},{17..., dimensions={0} | all-to-all | bytes 262144 | tf_op jit(solution)/shard_map/all_to_all | solution.py:347
  33.5 0.0 copy-done.2
  33.5 2.1 %shard_map.90 = (bf16[16,2,1280]{2,1,0:T(2,128)(2,1)}, f32[3,4,256]{2,1,0:T(4,128)S(1)}, f32[3,4,1280]{2,1,0:T(4,128)S(1)}) custom-call(bf16[8,8,1024]{2,1,0:T(8,128)(2,1)S(1)} %all_to_all.16.shares, bf16[3,256,1280]{2,1,0:T(8,128)(2,1)S(1)} %get-tuple-element.22.tok, bf16[3,256,1280]{2,1,0:T(8,128)(2,1)S(1)} %get-tuple-element.23.dout, ...), custom_call_target="tpu_custom_call" | custom-call | flops 11796480 | bytes 3932160 | tf_op jit(solution)/shard_map/pallas_call | solution.py:38
  35.7 3.5 %all-to-all-start.2 = ((bf16[16,2,1280]{2,1,0:T(2,128)(2,1)}), bf16[16,2,1280]{2,1,0:T(2,128)(2,1)S(1)}, u32[]{:S(2)}, u32[]{:S(2)}) async-start(bf16[16,2,1280]{2,1,0:T(2,128)(2,1)} %get-tuple-element.37), calls=%async_computation.2 | async-start | bytes 163840 | tf_op jit(solution)/shard_map/all_to_all | solution.py:490
  39.2 2.1 %shard_map.92 = (bf16[1280,640]{1,0:T(8,128)(2,1)}, bf16[640,1280]{1,0:T(8,128)(2,1)}) custom-call(bf16[64,1280]{1,0:T(8,128)(2,1)S(1)} %get-tuple-element.31.x_near, bf16[64,640]{1,0:T(8,128)(2,1)S(1)} %get-tuple-element.24.hid._.hid_near, bf16[64,640]{1,0:T(8,128)(2,1)S(1)} %get-tuple-element.25.grad.grad_near, ...), custom_call_target="tpu_custom_call" | custom-call | flops 419430400 | bytes 3276800 | tf_op jit(solution)/shard_map/pallas_call | solution.py:38
  41.3 1.6 %shard_map.91 = bf16[3,256,1280]{2,1,0:T(8,128)(2,1)} custom-call(f32[3,4,256]{2,1,0:T(4,128)S(1)} %get-tuple-element.29.left, f32[3,4,1280]{2,1,0:T(4,128)S(1)} %get-tuple-element.30.right), custom_call_target="tpu_custom_call" | custom-call | flops 7864320 | bytes 1966080 | tf_op jit(solution)/shard_map/pallas_call | solution.py:38
  42.9 3.4 %all-to-all-done.2.terms = bf16[16,2,1280]{2,1,0:T(2,128)(2,1)S(1)} async-done(((bf16[16,2,1280]{2,1,0:T(2,128)(2,1)}), bf16[16,2,1280]{2,1,0:T(2,128)(2,1)S(1)}, u32[]{:S(2)}, u32[]{:S(2)}) %all-to-all-start.2) | async-done | bytes 81952 | tf_op jit(solution)/shard_map/all_to_all | solution.py:490
  46.3 0.7 %shard_map.93 = f32[2,1280]{1,0:T(2,128)} custom-call(bf16[16,2,1280]{2,1,0:T(2,128)(2,1)S(1)} %all-to-all-done.2.terms), custom_call_target="tpu_custom_call" | custom-call | flops 40960 | bytes 81920 | tf_op jit(solution)/shard_map/pallas_call | solution.py:38
  (2 shorter events, 0.0 us)
Async XLA Ops:
  4.2 14.7 %copy-start = (bf16[1,1280,640]{2,1,0:T(8,128)(2,1)S(1)}, bf16[1,1280,640]{2,1,0:T(8,128)(2,1)}, u32[]{:S(2)}) copy-start(bf16[1,1280,640]{2,1,0:T(8,128)(2,1)} %param.7) | copy-start | bytes 4915204
  4.2 14.7 %copy-start.1 = (bf16[1,640,1280]{2,1,0:T(8,128)(2,1)S(1)}, bf16[1,640,1280]{2,1,0:T(8,128)(2,1)}, u32[]{:S(2)}) copy-start(bf16[1,640,1280]{2,1,0:T(8,128)(2,1)} %param.8) | copy-start | bytes 4915204
  19.0 1.3 %collective-permute-start = (bf16[8,8,1024]{2,1,0:T(8,128)(2,1)S(1)}, bf16[8,8,1024]{2,1,0:T(8,128)(2,1)S(1)}, u32[]{:S(2)}, u32[]{:S(2)}) collective-permute-start(bf16[8,8,1024]{2,1,0:T(8,128)(2,1)S(1)} %all_to_all.15.blocks), channel_id=1, source_target_pairs={{0,1},{1,0},{2,3},{3,2},{4,5},{5,4},{6,7},{7,6},{8,9},{9,8},{10,11... | collective-permute-start | bytes 393224 | tf_op jit(solution)/shard_map/ppermute | solution.py:354
  22.1 1.4 %collective-permute-start.1 = (bf16[8,8,1024]{2,1,0:T(8,128)(2,1)S(1)}, bf16[8,8,1024]{2,1,0:T(8,128)(2,1)S(1)}, u32[]{:S(2)}, u32[]{:S(2)}) collective-permute-start(bf16[8,8,1024]{2,1,0:T(8,128)(2,1)S(1)} %get-tuple-element.26), channel_id=1, source_target_pairs={{0,1},{1,0},{2,3},{3,2},{4,5},{5,4},{6,7},{7,6},{8,9},{9,8},{10,11... | collective-permute-start | bytes 393224 | tf_op jit(solution)/shard_map/ppermute | solution.py:354
  22.3 11.2 %copy-start.2 = (bf16[1280,2]{0,1:T(2,128)(2,1)S(1)}, bf16[1280,2]{0,1:T(2,128)(2,1)}, u32[]{:S(2)}) copy-start(bf16[1280,2]{0,1:T(2,128)(2,1)} %param.6) | copy-start | bytes 15364
  35.7 10.6 %all-to-all-start.2 = ((bf16[16,2,1280]{2,1,0:T(2,128)(2,1)}), bf16[16,2,1280]{2,1,0:T(2,128)(2,1)S(1)}, u32[]{:S(2)}, u32[]{:S(2)}) async-start(bf16[16,2,1280]{2,1,0:T(2,128)(2,1)} %get-tuple-element.37), calls=%async_computation.2 | async-start | bytes 163840 | tf_op jit(solution)/shard_map/all_to_all | solution.py:490
